TPU v7x, 256 devices: a whole 4x4x8 slice. The times are simulated.
256 devices in a mesh: fsdp: 32 (over y, x, core), ctx: 8 (over z).
Axes of the slice: x: 4, y: 4, z: 8, core: 2. Of those that a mesh axis runs over, the one named last changes fastest.
Arguments:
- tokens: bfloat16 [16384, 8192], P('fsdp'), may hold values from -12 to 12
- wq: bfloat16 [8192, 4096], P('fsdp', 'ctx'), may hold values from -0.0625 to 0.0625
- wo: bfloat16 [4096, 8192], P('ctx', 'fsdp'), may hold values from -1.5 to 1.5
- key_cache: bfloat16 [65536, 1024], P(('fsdp', 'ctx')), may hold values from -500 to 500, as said below
- value_cache: bfloat16 [65536, 1024], P(('fsdp', 'ctx')), may hold values from -6 to 6
- key_blocks: int32 [32, 4, 8], P('fsdp'), may hold values from 0 to 15, as said below
Outputs:
- mixed: bfloat16 [16384, 8192], P('fsdp', 'ctx')
Inputs may be any that keep to these rules, and one draw needn't show every extreme that they name: `key_cache`: keys of order one; a sequence's first block may hold much larger ones. `key_blocks`: for query block b of sequence s, entries 0 to 2 name key blocks 16 - 4 + b - 2, 12 + b - 1 and 12 + b; entries 3 and 4 name blocks 0 and 1; the last 3 entries are random blocks. Counting the random entries of a sequence over its query blocks in order as t = 0, 1, ..., the t-th lies in blocks k * 2 to (k+1) * 2 - 1 with k = 1 + t mod (6); entries may repeat.
All inputs are finite; a program needn't handle non-finite values.
Results may differ from a plain program's by a relative error of at most 0.018.
Values may be sent and summed in bfloat16 or wider, within the bound.
No kernel may reach another device: no remote copies, remote signals or barrier semaphores. Data moves between devices by JAX's collectives and lax.ppermute only.
A program may use at most 128 MiB of HBM per device.

v0:
```python
import jax
import jax.numpy as jnp
from jax import lax
from jax.sharding import PartitionSpec as P

HEAD = 128
BLOCK = 128


rope_base = 1000000.0


def rotate(vectors, positions):
    half_width = vectors.shape[-1] // 2
    frequency = rope_base ** (
        -(jnp.arange(half_width, dtype=jnp.float32) * 2.0) / vectors.shape[-1]
    )
    angles = positions.astype(jnp.float32)[:, None] * frequency[None, :]
    cosine_table = jnp.cos(angles)[:, None, :]
    sine_table = jnp.sin(angles)[:, None, :]
    front_half = vectors[..., :half_width]
    back_half = vectors[..., half_width:]
    return jnp.concatenate(
        [
            front_half * cosine_table - back_half * sine_table,
            back_half * cosine_table + front_half * sine_table,
        ],
        axis=-1,
    )


def body(tokens, wq, wo, key_cache, value_cache, key_blocks):
    ctx_count = lax.axis_size("ctx")
    row_count = tokens.shape[0]
    query_cols = wq.shape[1]
    projected = jnp.dot(
        tokens, lax.all_gather(wq, "fsdp", axis=0, tiled=True), preferred_element_type=jnp.float32
    )
    cache_count = key_cache.shape[0]
    key_total = cache_count * ctx_count
    positions = key_total - row_count + jnp.arange(row_count, dtype=jnp.int32)
    query = (
        rotate(projected.reshape(row_count, query_cols // HEAD, HEAD), positions) * HEAD ** (-0.5)
    ).astype(jnp.bfloat16)
    kv_cols = key_cache.shape[1] // ctx_count
    keys_whole, values_whole = (
        lax.all_gather(key_cache, "ctx", axis=0, tiled=True),
        lax.all_gather(value_cache, "ctx", axis=0, tiled=True),
    )
    first_col = lax.axis_index("ctx") * kv_cols
    keys_all = lax.dynamic_slice_in_dim(keys_whole, first_col, kv_cols, 1)
    values_all = lax.dynamic_slice_in_dim(values_whole, first_col, kv_cols, 1)
    kv_local = kv_cols // HEAD
    group_size = query_cols // kv_cols
    block_count = key_total // BLOCK
    query_blocks = row_count // BLOCK
    lists = key_blocks[0]
    picked_keys = jnp.take(keys_all.reshape(block_count, BLOCK, kv_local, HEAD), lists, axis=0)
    picked_values = jnp.take(values_all.reshape(block_count, BLOCK, kv_local, HEAD), lists, axis=0)
    shaped = query.reshape(query_blocks, BLOCK, kv_local, group_size, HEAD)
    scores = jnp.einsum(
        "bqkgd,bnskd->bkgqns", shaped, picked_keys, preferred_element_type=jnp.float32
    )
    own_block = block_count - query_blocks + jnp.arange(query_blocks, dtype=jnp.int32)
    own = lists == own_block[:, None]
    causal = jnp.arange(BLOCK)[None, :] <= jnp.arange(BLOCK)[:, None]
    allowed = jnp.logical_or(
        jnp.logical_not(own)[:, None, None, None, :, None], causal[None, None, None, :, None, :]
    )
    scores = jnp.where(allowed, scores, -jnp.inf)
    top_score = jnp.max(scores, axis=(4, 5), keepdims=True)
    raised = jnp.exp(scores - top_score)
    weights = (raised / jnp.sum(raised, axis=(4, 5), keepdims=True)).astype(jnp.bfloat16)
    context = jnp.einsum(
        "bkgqns,bnskd->bqkgd", weights, picked_values, preferred_element_type=jnp.float32
    )
    context = context.astype(jnp.bfloat16).reshape(row_count, query_cols)
    share_terms = jnp.dot(
        context, lax.all_gather(wo, "fsdp", axis=1, tiled=True), preferred_element_type=jnp.float32
    )
    return lax.psum_scatter(
        share_terms.astype(jnp.bfloat16), "ctx", scatter_dimension=1, tiled=True
    )


def solution(mesh):
    in_specs = (
        P("fsdp", None),
        P("fsdp", "ctx"),
        P("ctx", "fsdp"),
        P(("fsdp", "ctx"), None),
        P(("fsdp", "ctx"), None),
        P("fsdp", None, None),
    )
    out_specs = P("fsdp", "ctx")
    return jax.shard_map(body, mesh=mesh, in_specs=in_specs, out_specs=out_specs, check_vma=False)
```

profile of v0, /device:TPU:6, one launch (start us, length us, event | category | flops | bytes accessed | tf_op | source)
XLA Modules:
  0.0 359.2 jit_solution(5195303256417563035)
XLA Ops:
  6.5 0.0 all-gather.5.cloned.1.call-start
  6.5 0.7 all-gather.5.cloned.1.call-update
  7.3 0.0 all-gather.7.cloned.1.call-start
  7.3 0.7 all-gather.7.cloned.1.call-update
  8.0 0.0 all-gather.9.cloned.1.call-start
  8.1 0.7 all-gather.9.cloned.1.call-update
  8.7 0.0 all-gather.11.cloned.1.call-start
  8.8 0.5 all-gather.11.cloned.1.call-update
  9.3 0.0 reduce-scatter.2.cloned.1.call-start
  9.4 0.7 compare_select_fusion
  10.1 0.1 reshape.192
  10.2 0.8 fusion.28
  11.0 0.5 multiply_cosine_fusion
  11.5 0.3 broadcast_or_fusion
  11.8 55.1 %all-gather.5.cloned.1.call-done = bf16[2048,1024]{1,0:T(8,128)(2,1)} async-done(((bf16[256,1024]{1,0:T(8,128)(2,1)}), bf16[2048,1024]{1,0:T(8,128)(2,1)}) %all-gather.5.cloned.1.call-update) | async-done | bytes 4194320 | tf_op jit(solution)/shard_map/all_gather | solution.py:48
  66.9 55.2 %all-gather.7.cloned.1.call-done = bf16[2048,1024]{1,0:T(8,128)(2,1)} async-done(((bf16[256,1024]{1,0:T(8,128)(2,1)}), bf16[2048,1024]{1,0:T(8,128)(2,1)}) %all-gather.7.cloned.1.call-update) | async-done | bytes 4194320 | tf_op jit(solution)/shard_map/all_gather | solution.py:47
  122.1 1.3 constant_dynamic-slice_fusion
  123.4 0.7 gather_fusion.1
  124.2 0.7 gather_fusion
  124.9 1.3 copy.8
  126.3 55.0 %all-gather.9.cloned.1.call-done = bf16[8192,512]{1,0:T(8,128)(2,1)} async-done(((bf16[256,512]{1,0:T(8,128)(2,1)}), bf16[8192,512]{1,0:T(8,128)(2,1)}) %all-gather.9.cloned.1.call-update) | async-done | bytes 8388624 | tf_op jit(solution)/shard_map/all_gather | solution.py:37
  181.2 9.4 %fusion.34 = f32[512,512]{0,1:T(8,128)S(1)} fusion(bf16[512,8192]{1,0:T(8,128)(2,1)} %param.8, bf16[8192,512]{1,0:T(8,128)(2,1)} %all-gather.9.cloned.1.call-done), kind=kOutput, calls=%fused_computation.49 | convolution fusion | flops 4294967296 | bytes 17825792 | tf_op jit(solution)/shard_map/dot_general | solution.py:36
  190.7 1.0 multiply_subtract_fusion
  191.6 0.2 concatenate.10
  191.8 0.3 copy.10
  192.2 1.2 concatenate.9
  193.4 1.3 copy.9
  194.7 2.6 fusion
  197.4 0.0 copy-start
  197.4 1.7 fusion.1
  199.1 0.0 copy-done
  199.1 2.2 fusion.10
  201.4 0.3 copy.12
  201.7 45.5 %all-gather.11.cloned.1.call-done = bf16[512,8192]{1,0:T(8,128)(2,1)} async-done(((bf16[512,256]{1,0:T(8,128)(2,1)}), bf16[512,8192]{1,0:T(8,128)(2,1)}) %all-gather.11.cloned.1.call-update) | async-done | bytes 8388624 | tf_op jit(solution)/shard_map/all_gather | solution.py:79
  247.1 10.0 %convolution_convert_fusion = bf16[512,8192]{1,0:T(8,128)(2,1)} fusion(bf16[512,8192]{1,0:T(8,128)(2,1)} %all-gather.11.cloned.1.call-done, bf16[64,8,4,128]{3,2,1,0:T(4,128)(2,1)S(1)} %bitcast.100), kind=kOutput, calls=%fused_computation.2 | convolution fusion | flops 4299161600 | bytes 17301504 | tf_op jit(solution)/shard_map/dot_general | solution.py:78
  257.2 0.0 reduce-scatter.2.cloned.1.call-update
  257.2 95.5 %reduce-scatter.2.cloned.1.call-done = bf16[512,1024]{1,0:T(8,128)(2,1)} async-done(((bf16[512,8192]{1,0:T(8,128)(2,1)}), bf16[512,1024]{1,0:T(8,128)(2,1)}) %reduce-scatter.2.cloned.1.call-update) | async-done | bytes 1048592 | tf_op jit(solution)/shard_map/reduce_scatter | solution.py:81
  (5 shorter events, 0.0 us)
Async XLA Ops:
  6.5 60.4 %all-gather.5.cloned.1.call-start = ((), (), s32[]{:S(2)}) async-start(), calls=%async_computation.1 | async-start | bytes 4718592 | tf_op jit(solution)/shard_map/all_gather | solution.py:48
  7.3 114.9 %all-gather.7.cloned.1.call-start = ((), (), s32[]{:S(2)}) async-start(), calls=%async_computation.2 | async-start | bytes 4718592 | tf_op jit(solution)/shard_map/all_gather | solution.py:47
  8.0 173.2 %all-gather.9.cloned.1.call-start = ((), (), s32[]{:S(2)}) async-start(), calls=%async_computation.3 | async-start | bytes 8650752 | tf_op jit(solution)/shard_map/all_gather | solution.py:37
  8.7 238.4 %all-gather.11.cloned.1.call-start = ((), (), s32[]{:S(2)}) async-start(), calls=%async_computation.4 | async-start | bytes 8650752 | tf_op jit(solution)/shard_map/all_gather | solution.py:79
  9.3 343.4 %reduce-scatter.2.cloned.1.call-start = ((), (), s32[]{:S(2)}) async-start(), calls=%async_computation.5 | async-start | bytes 9437184 | tf_op jit(solution)/shard_map/reduce_scatter | solution.py:81
  197.4 1.8 copy-start
Sparse Core Ops, SparseCore 0:
  9.1 57.7 all-gather.4
  68.7 53.4 all-gather.6
  124.7 56.4 all-gather.8
  183.6 63.5 all-gather.10
  257.3 95.3 reduce-scatter.1
where the time goes:
time: 360 us; the launch traced here: 359 us
  waiting for transfers between devices  309 us (86%)
  matrix products  24.3 us (7%)
  between operations  13.3 us (4%)
  local copies, waits for them, and re-layouts  7.56 us (2%)
  other arithmetic  5.01 us (1%)
    reduce_scatter x1, waiting for transfers between devices, body(): lax.psum_scatter(share_terms.astype(jnp.bfloat16), 'ctx', scatter_dimensi...  95.5 us
    all_gather x1, waiting for transfers between devices, body(): lax.all_gather(key_cache, 'ctx', axis=0, tiled=True)  55.2 us
    all_gather x1, waiting for transfers between devices, body(): lax.all_gather(value_cache, 'ctx', axis=0, tiled=True)  55.1 us
    all_gather x1, waiting for transfers between devices, body(): lax.all_gather(wq, 'fsdp', axis=0, tiled=True)  55 us
    all_gather x1, waiting for transfers between devices, body(): lax.all_gather(wo, 'fsdp', axis=1, tiled=True)  45.5 us
    dot_general x1, matrix products, body(): jnp.dot(context, lax.all_gather(wo, 'fsdp', axis=1, tiled=True), preferre...  10 us
    dot_general x1, matrix products, body(): jnp.dot(tokens, lax.all_gather(wq, 'fsdp', axis=0, tiled=True), preferred...  9.44 us
  transfers between devices with their start and end apart: 5, of which 5 were waited for; matrix products, arithmetic and copies ran while one was open for 7% of the time, Pallas kernels for 0%

commit v1 on v0

v1 whole, which is shorter than its diff:
```python
import functools

import jax
import jax.numpy as jnp
from jax import lax
from jax.experimental import pallas as pl
from jax.experimental.pallas import tpu as pltpu
from jax.sharding import PartitionSpec as P

HEAD = 128
BLOCK = 128
SIDE = 4
ROPE_BASE = 1000000.0
F32 = jnp.float32
BF16 = jnp.bfloat16
VMEM_LIMIT = 48 * 2**20


def fsdp_index(y, x, core):
    return ((y % SIDE) * SIDE + x % SIDE) * 2 + core


def ring_pairs(phase, step):
    pairs = []
    for y in range(SIDE):
        for x in range(SIDE):
            for core in range(2):
                along_x = (core == 0) == (phase == 0)
                target = (y, x + step) if along_x else (y + step, x)
                pairs.append((fsdp_index(y, x, core), fsdp_index(*target, core)))
    return pairs


CORE_PAIRS = [(f, f ^ 1) for f in range(2 * SIDE * SIDE)]


def swap_cores(block):
    return lax.ppermute(block, "fsdp", CORE_PAIRS)


FIRST = (0, -1, 1, 2)


def block_index(core, first, second):
    me = lax.axis_index("fsdp") // 2
    y, x = me // SIDE, me % SIDE
    dx = jnp.where(core == 0, first, second)
    dy = jnp.where(core == 0, second, first)
    return (((y + dy) % SIDE) * SIDE + (x + dx) % SIDE) * 2 + core


def project_kernel(terms, has_sum, index_ref, *refs):
    tokens, weights = refs[:terms], refs[terms : 2 * terms]
    rest = refs[2 * terms :]
    before = rest[0] if has_sum else None
    out, total = rest[-2], rest[-1]
    step = pl.program_id(0)

    @pl.when(step == 0)
    def _():
        if has_sum:
            total[...] = before[...]
        else:
            total[...] = jnp.zeros_like(total)

    added = jnp.dot(tokens[0][...], weights[0][...], preferred_element_type=F32)
    for t, w in zip(tokens[1:], weights[1:]):
        added += jnp.dot(t[...], w[...], preferred_element_type=F32)
    total[...] += added

    @pl.when(step == pl.num_programs(0) - 1)
    def _():
        out[...] = total[...]


def project(tokens, pieces, index, before=None):
    rows = tokens.shape[0]
    terms = len(pieces)
    depth, cols = tokens.shape[1] // (2 * SIDE * SIDE), pieces[0].shape[1]
    steps = pieces[0].shape[0] // depth

    def token_spec(t):
        return pl.BlockSpec((rows, depth), lambda i, index_ref: (0, index_ref[t, i]))

    whole = pl.BlockSpec((rows, cols), lambda i, index_ref: (0, 0))
    piece_spec = pl.BlockSpec((depth, cols), lambda i, index_ref: (i, 0))
    sums = [] if before is None else [before]
    return pl.pallas_call(
        functools.partial(project_kernel, terms, before is not None),
        grid_spec=pltpu.PrefetchScalarGridSpec(
            num_scalar_prefetch=1,
            grid=(steps,),
            in_specs=[token_spec(t) for t in range(terms)] + [piece_spec] * terms + [whole] * len(sums),
            out_specs=whole,
            scratch_shapes=[pltpu.VMEM((rows, cols), F32)],
        ),
        out_shape=jax.ShapeDtypeStruct((rows, cols), F32),
        compiler_params=pltpu.CompilerParams(vmem_limit_bytes=VMEM_LIMIT),
        cost_estimate=pl.CostEstimate(
            flops=2 * rows * cols * depth * steps * terms,
            bytes_accessed=2 * (rows + cols) * depth * steps * terms + 8 * rows * cols,
            transcendentals=0,
        ),
        name="project",
    )(index, *([tokens] * terms), *pieces, *sums)


def attend_kernel(heads, entries, own_first, blocks_ref, q_ref, cos_ref, sin_ref, kv_ref, out_ref, keys, values):
    b = pl.program_id(0)
    own = own_first + b
    for n in range(entries):
        block = blocks_ref[b, n]
        row = pl.multiple_of((block % 2) * BLOCK, BLOCK)
        keys[pl.ds(n * BLOCK, BLOCK), :] = kv_ref[block // 2, 0, pl.ds(row, BLOCK), :]
        values[pl.ds(n * BLOCK, BLOCK), :] = kv_ref[block // 2, 1, pl.ds(row, BLOCK), :]
    query_row = lax.broadcasted_iota(jnp.int32, (BLOCK, BLOCK), 0)
    key_row = lax.broadcasted_iota(jnp.int32, (BLOCK, BLOCK), 1)
    late = key_row > query_row
    cos, sin = cos_ref[...], sin_ref[...]
    for h in range(heads):
        x = q_ref[:, h * HEAD : (h + 1) * HEAD]
        query = (x * cos + pltpu.roll(x, HEAD // 2, 1) * sin).astype(BF16)
        scores = lax.dot_general(query, keys[...], (((1,), (1,)), ((), ())), preferred_element_type=F32)
        kept = []
        for n in range(entries):
            left_out = jnp.logical_and(late, blocks_ref[b, n] == own)
            kept.append(jnp.where(left_out, -jnp.inf, scores[:, n * BLOCK : (n + 1) * BLOCK]))
        scores = jnp.concatenate(kept, axis=1)
        top = jnp.max(scores, axis=1, keepdims=True)
        raised = jnp.exp(scores - top)
        total = jnp.sum(raised, axis=1, keepdims=True)
        mixed = jnp.dot(raised.astype(BF16), values[...], preferred_element_type=F32)
        out_ref[:, h * HEAD : (h + 1) * HEAD] = (mixed / total).astype(BF16)


def attend(projected, cos, sin, kv, lists):
    rows, cols = projected.shape
    query_blocks, entries = lists.shape
    owners, _, held, _ = kv.shape
    heads = cols // HEAD
    own_first = owners * held // BLOCK - query_blocks
    strip = pl.BlockSpec((BLOCK, cols), lambda b, lists_ref: (b, 0))
    table = pl.BlockSpec((BLOCK, HEAD), lambda b, lists_ref: (b, 0))
    return pl.pallas_call(
        functools.partial(attend_kernel, heads, entries, own_first),
        grid_spec=pltpu.PrefetchScalarGridSpec(
            num_scalar_prefetch=1,
            grid=(query_blocks,),
            in_specs=[strip, table, table, pl.BlockSpec(kv.shape, lambda b, lists_ref: (0, 0, 0, 0))],
            out_specs=strip,
            scratch_shapes=[
                pltpu.VMEM((entries * BLOCK, HEAD), BF16),
                pltpu.VMEM((entries * BLOCK, HEAD), BF16),
            ],
        ),
        out_shape=jax.ShapeDtypeStruct((rows, cols), BF16),
        compiler_params=pltpu.CompilerParams(vmem_limit_bytes=VMEM_LIMIT),
        cost_estimate=pl.CostEstimate(
            flops=4 * rows * entries * BLOCK * cols,
            bytes_accessed=6 * rows * cols + 2 * kv.size,
            transcendentals=rows * heads * entries * BLOCK,
        ),
        name="attend",
    )(lists, projected, cos, sin, kv)


def output_kernel(terms, has_sum, index_ref, *refs):
    contexts, weights = refs[:terms], refs[terms : 2 * terms]
    out = refs[-1]
    total = jnp.dot(contexts[0][...], weights[0][0], preferred_element_type=F32)
    for c, w in zip(contexts[1:], weights[1:]):
        total += jnp.dot(c[...], w[0], preferred_element_type=F32)
    if has_sum:
        total += refs[2 * terms][...]
    out[...] = total.astype(out.dtype)


def output(contexts, weights, index, before=None, dtype=F32):
    rows, depth = contexts[0].shape
    terms = len(contexts)
    blocks, _, width = weights.shape
    owners = 8
    parts = blocks // owners

    def weight_spec(t):
        return pl.BlockSpec((1, depth, width), lambda j, index_ref: (j * owners + index_ref[t], 0, 0))

    strip = pl.BlockSpec((rows, width), lambda j, index_ref: (0, j))
    sums = [] if before is None else [before]
    return pl.pallas_call(
        functools.partial(output_kernel, terms, before is not None),
        grid_spec=pltpu.PrefetchScalarGridSpec(
            num_scalar_prefetch=1,
            grid=(parts,),
            in_specs=[pl.BlockSpec((rows, depth), lambda j, index_ref: (0, 0))] * terms
            + [weight_spec(t) for t in range(terms)]
            + [strip] * len(sums),
            out_specs=strip,
        ),
        out_shape=jax.ShapeDtypeStruct((rows, parts * width), dtype),
        compiler_params=pltpu.CompilerParams(vmem_limit_bytes=VMEM_LIMIT),
        cost_estimate=pl.CostEstimate(
            flops=2 * rows * depth * width * parts * terms,
            bytes_accessed=2 * depth * (rows + width * parts) * terms + 8 * rows * width * parts,
            transcendentals=0,
        ),
        name="output",
    )(index, *contexts, *([weights] * terms), *sums)


def tables(rows, first):
    frequency = ROPE_BASE ** (-(jnp.arange(HEAD // 2, dtype=F32) * 2.0) / HEAD)
    positions = (first + jnp.arange(rows, dtype=jnp.int32)).astype(F32)
    angles = positions[:, None] * frequency[None, :]
    scale = HEAD ** (-0.5)
    cos, sin = jnp.cos(angles) * scale, jnp.sin(angles) * scale
    return jnp.concatenate([cos, cos], axis=1), jnp.concatenate([-sin, sin], axis=1)


def gather_wq(wq):
    minus = lax.ppermute(wq, "fsdp", ring_pairs(0, 1))
    plus = lax.ppermute(wq, "fsdp", ring_pairs(0, -1))
    far = lax.ppermute(wq, "fsdp", ring_pairs(0, 2))
    line = jnp.concatenate([wq, minus, plus, far], axis=0)
    half = line.shape[0] // 2
    line_minus = lax.ppermute(line, "fsdp", ring_pairs(1, 1))
    line_plus = lax.ppermute(line, "fsdp", ring_pairs(1, -1))
    far_top = lax.ppermute(line_minus[:half], "fsdp", ring_pairs(1, 1))
    far_low = lax.ppermute(line_plus[half:], "fsdp", ring_pairs(1, -1))
    groups = [[line], [line_minus, line_plus], [far_top, far_low]]
    return [group + [swap_cores(piece) for piece in group] for group in groups]


def wq_indices():
    core = lax.axis_index("fsdp") % 2
    cores = (core, 1 - core)

    def rows(which, second, firsts):
        return jnp.stack([block_index(which, o, second) for o in firsts])

    return [
        jnp.stack([rows(k, 0, FIRST) for k in cores]),
        jnp.stack([rows(k, s, FIRST) for k in cores for s in (-1, 1)]),
        jnp.stack([rows(k, 2, part) for k in cores for part in (FIRST[:2], FIRST[2:])]),
    ]


def body(tokens, wq, wo, key_cache, value_cache, key_blocks):
    ctx_count = lax.axis_size("ctx")
    fsdp_count = lax.axis_size("fsdp")
    z = lax.axis_index("ctx")
    rows = tokens.shape[0]
    held = key_cache.shape[0]

    groups = gather_wq(wq)

    by_head = jnp.stack(
        [
            key_cache.reshape(held, ctx_count, HEAD).transpose(1, 0, 2),
            value_cache.reshape(held, ctx_count, HEAD).transpose(1, 0, 2),
        ],
        axis=1,
    )
    kv = lax.all_to_all(by_head, "ctx", 0, 0, tiled=True)

    parts = fsdp_count // ctx_count
    moves = []
    for f in range(fsdp_count):
        for c in range(ctx_count):
            plane, part = f // parts, f % parts
            moves.append((f * ctx_count + c, (part * ctx_count + (c + plane) % ctx_count) * ctx_count + plane))
    wo_here = lax.ppermute(wo, ("fsdp", "ctx"), moves)
    weights = lax.all_gather(wo_here, "fsdp", axis=0, tiled=False)

    cos, sin = tables(rows, held * ctx_count - rows)
    projected = None
    for pieces, index in zip(groups, wq_indices()):
        projected = project(tokens, pieces, index, projected)
    context = attend(projected, cos, sin, kv, key_blocks[0])

    def owner(*offsets):
        return jnp.stack([(2 * z + o) % ctx_count for o in offsets])

    right = [(i, (i + 1) % ctx_count) for i in range(ctx_count)]
    left = [(i, (i - 1) % ctx_count) for i in range(ctx_count)]
    half = rows // 2
    down, up = [context], [context]
    for _ in range(3):
        down.append(lax.ppermute(down[-1], "ctx", right))
        up.append(lax.ppermute(up[-1], "ctx", left))
    far_top = lax.ppermute(down[-1][:half], "ctx", right)
    far_low = lax.ppermute(up[-1][half:], "ctx", left)

    total = output([context], weights, owner(0))
    for s in (1, 2, 3):
        total = output([down[s], up[s]], weights, owner(-s, s), total)
    far = jnp.concatenate([far_top, far_low], axis=0)
    return output([far], weights, owner(4), total, BF16)


def solution(mesh):
    in_specs = (
        P("fsdp", None),
        P("fsdp", "ctx"),
        P("ctx", "fsdp"),
        P(("fsdp", "ctx"), None),
        P(("fsdp", "ctx"), None),
        P("fsdp", None, None),
    )
    return jax.shard_map(body, mesh=mesh, in_specs=in_specs, out_specs=P("fsdp", "ctx"), check_vma=False)
```

time: 360 us -> 218 us (0.61)
  waiting for transfers between devices: 309 us -> 98.1 us
  starting transfers between devices: 0.15 us -> 42.1 us
  Pallas kernels: 0 us -> 41.7 us
  matrix products: 24.3 us -> 0 us
  local copies, waits for them, and re-layouts: 7.56 us -> 11.8 us
    all_gather x4 -> x1, waiting for transfers between devices: 211 us -> 0.02 us  [body(): weights = lax.all_gather(wo_here, 'fsdp', axis=0, tiled=False)]
    ppermute x0 -> x21, waiting for transfers between devices: none -> 98.1 us  [the longest x3 33.5 us: body(): down.append(lax.ppermute(down[-1], 'ctx', right))]
    reduce_scatter x1 -> x0, waiting for transfers between devices: 95.5 us -> none  [body(): lax.psum_scatter(share_terms.astype(jnp.bfloat16), 'ctx', scatter_dimensi...]
    pallas_call x0 -> x9, Pallas kernels: none -> 41.7 us  [the longest x5 19.6 us: output(): pl.pallas_call(functools.partial(output_kernel, terms, before is not None...]
    ppermute x0 -> x21, starting transfers between devices: none -> 31.8 us  [the longest x3 7.28 us: body(): up.append(lax.ppermute(up[-1], 'ctx', left))]
    dot_general x4 -> x0, matrix products: 24.3 us -> none  [the longest x1 10 us: body(): jnp.dot(context, lax.all_gather(wo, 'fsdp', axis=1, tiled=True), preferre...]
    all_to_all x0 -> x1, starting transfers between devices: none -> 10.3 us  [body(): kv = lax.all_to_all(by_head, 'ctx', 0, 0, tiled=True)]
    unnamed x2 -> x17, local copies, waits for them, and re-layouts: 0.01 us -> 6.84 us
  transfers between devices with their start and end apart: 5 -> 23, of which waited for: 5 -> 9; matrix products, arithmetic and copies ran while one was open for 7% -> 7% of each run, Pallas kernels for 0% -> 10%
where the time goes in v1:
time: 218 us; the launch traced here: 214 us
  waiting for transfers between devices  98.1 us (45%)
  starting transfers between devices  42.1 us (19%)
  Pallas kernels  41.7 us (19%)
  between operations  14.8 us (7%)
  local copies, waits for them, and re-layouts  11.8 us (5%)
  other arithmetic  5.93 us (3%)
    ppermute x3, waiting for transfers between devices, body(): down.append(lax.ppermute(down[-1], 'ctx', right))  33.5 us
    ppermute x1, waiting for transfers between devices, body(): wo_here = lax.ppermute(wo, ('fsdp', 'ctx'), moves)  32.9 us
    pallas_call x5, Pallas kernels, output(): pl.pallas_call(functools.partial(output_kernel, terms, before is not None...  19.6 us
    ppermute x1, waiting for transfers between devices, gather_wq(): far_top = lax.ppermute(line_minus[:half], 'fsdp', ring_pairs(1, 1))  17.2 us
    pallas_call x3, Pallas kernels, project(): pl.pallas_call(functools.partial(project_kernel, terms, before is not Non...  13.8 us
    all_to_all x1, starting transfers between devices, body(): kv = lax.all_to_all(by_head, 'ctx', 0, 0, tiled=True)  10.3 us
    pallas_call x1, Pallas kernels, attend(): pl.pallas_call(functools.partial(attend_kernel, heads, entries, own_first...  8.29 us
    ppermute x3, starting transfers between devices, body(): up.append(lax.ppermute(up[-1], 'ctx', left))  7.28 us
  transfers between devices with their start and end apart: 23, of which 9 were waited for; matrix products, arithmetic and copies ran while one was open for 7% of the time, Pallas kernels for 10%

profile of v1, /device:TPU:6, one launch (start us, length us, event | category | flops | bytes accessed | tf_op | source)
XLA Modules:
  0.0 214.4 jit_solution(11087261791447964427)
XLA Ops:
  6.5 5.8 %collective-permute-start.20 = (bf16[512,256]{1,0:T(8,128)(2,1)}, bf16[512,256]{1,0:T(8,128)(2,1)S(1)}, u32[]{:S(2)}, u32[]{:S(2)}) collective-permute-start(bf16[512,256]{1,0:T(8,128)(2,1)} %param.8), channel_id=1, source_target_pairs={{0,0},{1,8},{2,16},{3,24},{4,32},{5,40},{6,48},{7,56},{8,64},{9,72... | collective-permute-start | bytes 786440 | tf_op jit(solution)/shard_map/ppermute | solution.py:272
  12.3 32.9 %collective-permute-done.20 = bf16[512,256]{1,0:T(8,128)(2,1)S(1)} collective-permute-done((bf16[512,256]{1,0:T(8,128)(2,1)}, bf16[512,256]{1,0:T(8,128)(2,1)S(1)}, u32[]{:S(2)}, u32[]{:S(2)}) %collective-permute-start.20) | collective-permute-done | bytes 262176 | tf_op jit(solution)/shard_map/ppermute | solution.py:272
  45.3 0.7 copy-done.5
  46.0 0.1 collective-permute-start
  46.1 2.0 collective-permute-start.1
  48.1 1.0 constant_dynamic-update-slice_fusion.3
  49.1 3.5 %collective-permute-done = bf16[256,512]{1,0:T(8,128)(2,1)S(1)} collective-permute-done((bf16[256,512]{1,0:T(8,128)(2,1)}, bf16[256,512]{1,0:T(8,128)(2,1)S(1)}, u32[]{:S(2)}, u32[]{:S(2)}) %collective-permute-start) | collective-permute-done | bytes 262176 | tf_op jit(solution)/shard_map/ppermute | solution.py:221
  52.7 7.0 %collective-permute-done.1 = bf16[256,512]{1,0:T(8,128)(2,1)S(1)} collective-permute-done((bf16[256,512]{1,0:T(8,128)(2,1)}, bf16[256,512]{1,0:T(8,128)(2,1)S(1)}, u32[]{:S(2)}, u32[]{:S(2)}) %collective-permute-start.1) | collective-permute-done | bytes 262176 | tf_op jit(solution)/shard_map/ppermute | solution.py:222
  59.7 6.1 %collective-permute-start.5 = (bf16[1024,512]{1,0:T(8,128)(2,1)S(1)}, bf16[1024,512]{1,0:T(8,128)(2,1)S(1)}, u32[]{:S(2)}, u32[]{:S(2)}) collective-permute-start(bf16[1024,512]{1,0:T(8,128)(2,1)S(1)} %constant_dynamic-update-slice_fusion.refs_2_), channel_id=1, source_target_pairs={{0,192},{8,56},{16,208},{24,8},{32,224},{40,24},{48,240},{56,40},{... | collective-permute-start | bytes 3145736 | tf_op jit(solution)/shard_map/ppermute | solution.py:227
  65.8 2.0 copy.7
  67.8 2.1 copy.8
  69.9 2.1 copy.9
  72.0 2.0 copy.10
  74.0 2.3 %pad_maximum_fusion = bf16[8,2,256,128]{3,2,1,0:T(8,128)(2,1)} fusion(bf16[8,1,256,128]{3,2,1,0:T(8,128)(2,1)} %bitcast.82, bf16[8,1,256,128]{3,2,1,0:T(8,128)(2,1)} %bitcast.81), kind=kLoop, calls=%fused_computation | loop fusion | flops 524288 | bytes 2097152 | tf_op jit(solution)/shard_map/stack | solution.py:257
  76.3 10.3 %all-to-all-start = ((bf16[8,2,256,128]{3,2,1,0:T(8,128)(2,1)}), bf16[8,2,256,128]{3,2,1,0:T(8,128)(2,1)}, u32[]{:S(2)}, u32[]{:S(2)}) async-start(bf16[8,2,256,128]{3,2,1,0:T(8,128)(2,1)} %pad_maximum_fusion), calls=%async_computation | async-start | bytes 2097152 | tf_op jit(solution)/shard_map/all_to_all | solution.py:264
  87.6 0.1 add_bitcast_fusion.2
  88.1 0.3 collective-permute-start.10
  88.4 0.3 collective-permute-start.9
  88.8 0.1 collective-permute-start.4
  88.9 3.3 %collective-permute-start.6 = (bf16[512,512]{1,0:T(8,128)(2,1)S(1)}, bf16[512,512]{1,0:T(8,128)(2,1)S(1)}, u32[]{:S(2)}, u32[]{:S(2)}) collective-permute-start(bf16[512,512]{1,0:T(8,128)(2,1)S(1)} %slice.17), channel_id=1, source_target_pairs={{0,192},{8,56},{16,208},{24,8},{32,224},{40,24},{48,240},{56,40},{... | collective-permute-start | bytes 1572872 | tf_op jit(solution)/shard_map/ppermute | solution.py:229
  92.3 1.0 fusion.2
  93.3 17.2 %collective-permute-done.4.refs_4_ = bf16[512,512]{1,0:T(8,128)(2,1)S(1)} collective-permute-done((bf16[512,512]{1,0:T(8,128)(2,1)S(1)}, bf16[512,512]{1,0:T(8,128)(2,1)S(1)}, u32[]{:S(2)}, u32[]{:S(2)}) %collective-permute-start.4) | collective-permute-done | bytes 524320 | tf_op jit(solution)/shard_map/ppermute | solution.py:228
  110.5 0.5 collective-permute-start.8
  111.0 0.9 pad_maximum_fusion.2
  111.9 4.4 %project.3.refs_8_ = f32[512,512]{1,0:T(8,128)S(1)} custom-call(s32[2,4]{1,0:T(2,128)S(1)} %pad_add_fusion.2.index_ref, bf16[512,8192]{1,0:T(8,128)(2,1)} %refs_3_.3, bf16[512,8192]{1,0:T(8,128)(2,1)} %refs_3_.3, bf16[1024,512]{1,0:T(8,128)(2,1)S(1)} %constant_dynamic-update-slice_fusion.refs_2_, bf16[1024,512]{1,0:T(8,128)(2,1)} %collective-permute-done.11.refs_3_), custom_call_target="tpu_custom_call" | custom-call | flops 1073741824 | bytes 6291456 | tf_op jit(solution)/shard_map/project/pallas_call | solution.py:88
  116.3 1.0 copy-done
  117.3 5.9 %project.4.refs_8_ = f32[512,512]{1,0:T(8,128)S(1)} custom-call(s32[4,4]{1,0:T(4,128)S(1)} %pad_add_fusion.1.index_ref, bf16[512,8192]{1,0:T(8,128)(2,1)} %refs_3_.3, bf16[512,8192]{1,0:T(8,128)(2,1)} %refs_3_.3, bf16[512,8192]{1,0:T(8,128)(2,1)} %refs_3_.3, bf16[512,8192]{1,0:T(8,128)(2,1)} %refs_3_.3, ...), custom_call_target="tpu_custom_call" | custom-call | flops 2147483648 | bytes 10485760 | tf_op jit(solution)/shard_map/project/pallas_call | solution.py:88
  123.3 3.5 %project.5.q_ref = f32[512,512]{1,0:T(8,128)S(1)} custom-call(s32[4,2]{1,0:T(4,128)S(1)} %pad_add_fusion.index_ref, bf16[512,8192]{1,0:T(8,128)(2,1)} %refs_3_.3, bf16[512,8192]{1,0:T(8,128)(2,1)} %refs_3_.3, bf16[512,8192]{1,0:T(8,128)(2,1)} %refs_3_.3, bf16[512,8192]{1,0:T(8,128)(2,1)} %refs_3_.3, bf16[512,512]{1,0:T(8,128)(2,1)S(1)} %collective-permute-done.4.refs_4_, ...), custom_call_target="tpu_custom_call" | custom-call | flops 1073741824 | bytes 6291456 | tf_op jit(solution)/shard_map/project/pallas_call | solution.py:88
  126.8 8.3 %attend.1.refs_0_ = bf16[512,512]{1,0:T(8,128)(2,1)S(1)} custom-call(s32[4,8]{1,0:T(4,128)S(1)} %bitcast.70, f32[512,512]{1,0:T(8,128)S(1)} %project.5.q_ref, f32[512,128]{1,0:T(8,128)S(1)} %get-tuple-element.18.cos_ref, f32[512,128]{1,0:T(8,128)S(1)} %copy-done.3, bf16[8,2,256,128]{3,2,1,0:T(8,128)(2,1)} %all-to-all-done.kv_ref), custom_call_target="tpu_custom_call" | custom-call | flops 1073741824 | bytes 2621440 | tf_op jit(solution)/shard_map/attend/pallas_call | solution.py:144
  135.1 2.1 collective-permute-start.12
  137.2 1.3 collective-permute-start.16
  138.5 12.0 %collective-permute-done.12.refs_0_ = bf16[512,512]{1,0:T(8,128)(2,1)S(1)} collective-permute-done((bf16[512,512]{1,0:T(8,128)(2,1)S(1)}, bf16[512,512]{1,0:T(8,128)(2,1)S(1)}, u32[]{:S(2)}, u32[]{:S(2)}) %collective-permute-start.12) | collective-permute-done | bytes 524320 | tf_op jit(solution)/shard_map/ppermute | solution.py:289
  150.5 0.5 collective-permute-start.13
  151.0 2.7 %collective-permute-start.17 = (bf16[512,512]{1,0:T(8,128)(2,1)S(1)}, bf16[512,512]{1,0:T(8,128)(2,1)}, u32[]{:S(2)}, u32[]{:S(2)}) collective-permute-start(bf16[512,512]{1,0:T(8,128)(2,1)S(1)} %collective-permute-done.16.refs_1_), channel_id=1, source_target_pairs={{0,7},{1,0},{2,1},{3,2},{4,3},{5,4},{6,5},{7,6},{8,15},{9,8},{10,9... | collective-permute-start | bytes 1572872 | tf_op jit(solution)/shard_map/ppermute | solution.py:290
  153.7 11.2 %collective-permute-done.13.refs_0_ = bf16[512,512]{1,0:T(8,128)(2,1)S(1)} collective-permute-done((bf16[512,512]{1,0:T(8,128)(2,1)S(1)}, bf16[512,512]{1,0:T(8,128)(2,1)S(1)}, u32[]{:S(2)}, u32[]{:S(2)}) %collective-permute-start.13) | collective-permute-done | bytes 524320 | tf_op jit(solution)/shard_map/ppermute | solution.py:289
  165.0 3.2 %collective-permute-start.18 = (bf16[512,512]{1,0:T(8,128)(2,1)}, bf16[512,512]{1,0:T(8,128)(2,1)S(1)}, u32[]{:S(2)}, u32[]{:S(2)}) collective-permute-start(bf16[512,512]{1,0:T(8,128)(2,1)} %collective-permute-done.17.refs_1_), channel_id=1, source_target_pairs={{0,7},{1,0},{2,1},{3,2},{4,3},{5,4},{6,5},{7,6},{8,15},{9,8},{10,9... | collective-permute-start | bytes 1572872 | tf_op jit(solution)/shard_map/ppermute | solution.py:290
  168.2 10.3 %collective-permute-done.14.refs_0_ = bf16[512,512]{1,0:T(8,128)(2,1)S(1)} collective-permute-done((bf16[512,512]{1,0:T(8,128)(2,1)S(1)}, bf16[512,512]{1,0:T(8,128)(2,1)S(1)}, u32[]{:S(2)}, u32[]{:S(2)}) %collective-permute-start.14) | collective-permute-done | bytes 524320 | tf_op jit(solution)/shard_map/ppermute | solution.py:289
  178.5 0.1 collective-permute-start.15
  178.6 0.7 slice.19
  179.3 3.2 %collective-permute-start.19 = (bf16[256,512]{1,0:T(8,128)(2,1)}, bf16[256,512]{1,0:T(8,128)(2,1)}, u32[]{:S(2)}, u32[]{:S(2)}) collective-permute-start(bf16[256,512]{1,0:T(8,128)(2,1)} %slice.19), channel_id=1, source_target_pairs={{0,7},{1,0},{2,1},{3,2},{4,3},{5,4},{6,5},{7,6},{8,15},{9,8},{10,9... | collective-permute-start | bytes 786440 | tf_op jit(solution)/shard_map/ppermute | solution.py:292
  182.8 3.5 %collective-permute-done.15 = bf16[256,512]{1,0:T(8,128)(2,1)} collective-permute-done((bf16[256,512]{1,0:T(8,128)(2,1)S(1)}, bf16[256,512]{1,0:T(8,128)(2,1)}, u32[]{:S(2)}, u32[]{:S(2)}) %collective-permute-start.15) | collective-permute-done | bytes 262176 | tf_op jit(solution)/shard_map/ppermute | solution.py:291
  186.3 0.5 collective-permute-done.19
  186.7 1.1 pad_maximum_fusion.1.refs_0_
  187.8 2.9 %output.5.refs_4_ = f32[512,1024]{1,0:T(8,128)S(1)} custom-call(s32[1]{0:T(128)} %bitcast.57.index_ref, bf16[512,512]{1,0:T(8,128)(2,1)S(1)} %attend.1.refs_0_, bf16[32,512,256]{2,1,0:T(8,128)(2,1)} %bitcast.71), custom_call_target="tpu_custom_call" | custom-call | flops 536870912 | bytes 5767168 | tf_op jit(solution)/shard_map/output/pallas_call | solution.py:190
  190.8 4.2 %output.6.refs_4_ = f32[512,1024]{1,0:T(8,128)S(1)} custom-call(s32[2]{0:T(128)S(1)} %pad_add_fusion.5.index_ref, bf16[512,512]{1,0:T(8,128)(2,1)S(1)} %collective-permute-done.12.refs_0_, bf16[512,512]{1,0:T(8,128)(2,1)S(1)} %collective-permute-done.16.refs_1_, bf16[32,512,256]{2,1,0:T(8,128)(2,1)} %bitcast.72, bf16[32,512,256]{2,1,0:T(8,128)(2,1)} %bitcast.73, ...), custom_call_target="tpu_custom_call" | custom-call | flops 1073741824 | bytes 7340032 | tf_op jit(solution)/shard_map/output/pallas_call | solution.py:190
  195.0 4.4 %output.7.refs_4_ = f32[512,1024]{1,0:T(8,128)S(1)} custom-call(s32[2]{0:T(128)S(1)} %pad_add_fusion.4.index_ref, bf16[512,512]{1,0:T(8,128)(2,1)S(1)} %copy-done.2, bf16[512,512]{1,0:T(8,128)(2,1)} %collective-permute-done.17.refs_1_, bf16[32,512,256]{2,1,0:T(8,128)(2,1)} %bitcast.74, bf16[32,512,256]{2,1,0:T(8,128)(2,1)} %bitcast.75, ...), custom_call_target="tpu_custom_call" | custom-call | flops 1073741824 | bytes 7340032 | tf_op jit(solution)/shard_map/output/pallas_call | solution.py:190
  199.4 4.2 %output.8.refs_2_ = f32[512,1024]{1,0:T(8,128)S(1)} custom-call(s32[2]{0:T(128)S(1)} %pad_add_fusion.3.index_ref, bf16[512,512]{1,0:T(8,128)(2,1)S(1)} %collective-permute-done.14.refs_0_, bf16[512,512]{1,0:T(8,128)(2,1)S(1)} %collective-permute-done.18.refs_1_, bf16[32,512,256]{2,1,0:T(8,128)(2,1)} %bitcast.76, bf16[32,512,256]{2,1,0:T(8,128)(2,1)} %bitcast.77, ...), custom_call_target="tpu_custom_call" | custom-call | flops 1073741824 | bytes 7340032 | tf_op jit(solution)/shard_map/output/pallas_call | solution.py:190
  203.6 3.9 %output.9 = bf16[512,1024]{1,0:T(8,128)(2,1)} custom-call(s32[1]{0:T(128)} %bitcast.index_ref, bf16[512,512]{1,0:T(8,128)(2,1)S(1)} %pad_maximum_fusion.1.refs_0_, bf16[32,512,256]{2,1,0:T(8,128)(2,1)} %bitcast.78, f32[512,1024]{1,0:T(8,128)S(1)} %output.8.refs_2_), custom_call_target="tpu_custom_call" | custom-call | flops 536870912 | bytes 5767168 | tf_op jit(solution)/shard_map/output/pallas_call | solution.py:190
  (49 shorter events, 0.9 us)
Async XLA Ops:
  6.5 181.3 %all-gather.3.cloned.1.call-start = ((), (), s32[]{:S(2)}) async-start(), calls=%async_computation.1 | async-start | bytes 8650752 | tf_op jit(solution)/shard_map/all_gather | solution.py:273
  6.5 38.7 %collective-permute-start.20 = (bf16[512,256]{1,0:T(8,128)(2,1)}, bf16[512,256]{1,0:T(8,128)(2,1)S(1)}, u32[]{:S(2)}, u32[]{:S(2)}) collective-permute-start(bf16[512,256]{1,0:T(8,128)(2,1)} %param.8), channel_id=1, source_target_pairs={{0,0},{1,8},{2,16},{3,24},{4,32},{5,40},{6,48},{7,56},{8,64},{9,72... | collective-permute-start | bytes 786440 | tf_op jit(solution)/shard_map/ppermute | solution.py:272
  45.3 0.7 copy-start.5
  46.0 6.7 %collective-permute-start = (bf16[256,512]{1,0:T(8,128)(2,1)}, bf16[256,512]{1,0:T(8,128)(2,1)S(1)}, u32[]{:S(2)}, u32[]{:S(2)}) collective-permute-start(bf16[256,512]{1,0:T(8,128)(2,1)} %param.7), channel_id=1, source_target_pairs={{0,16},{8,72},{16,32},{24,88},{32,48},{40,104},{48,0},{56,120},{64... | collective-permute-start | bytes 786440 | tf_op jit(solution)/shard_map/ppermute | solution.py:221
  46.1 13.6 %collective-permute-start.1 = (bf16[256,512]{1,0:T(8,128)(2,1)}, bf16[256,512]{1,0:T(8,128)(2,1)S(1)}, u32[]{:S(2)}, u32[]{:S(2)}) collective-permute-start(bf16[256,512]{1,0:T(8,128)(2,1)} %param.7), channel_id=1, source_target_pairs={{0,48},{8,200},{16,0},{24,216},{32,16},{40,232},{48,32},{56,248},{... | collective-permute-start | bytes 786440 | tf_op jit(solution)/shard_map/ppermute | solution.py:222
  48.1 11.6 %collective-permute-start.2 = (bf16[256,512]{1,0:T(8,128)(2,1)}, bf16[256,512]{1,0:T(8,128)(2,1)S(1)}, u32[]{:S(2)}, u32[]{:S(2)}) collective-permute-start(bf16[256,512]{1,0:T(8,128)(2,1)} %param.7), channel_id=1, source_target_pairs={{0,32},{8,136},{16,48},{24,152},{32,0},{40,168},{48,16},{56,184},{... | collective-permute-start | bytes 786440 | tf_op jit(solution)/shard_map/ppermute | solution.py:223
  59.7 28.4 %collective-permute-start.5 = (bf16[1024,512]{1,0:T(8,128)(2,1)S(1)}, bf16[1024,512]{1,0:T(8,128)(2,1)S(1)}, u32[]{:S(2)}, u32[]{:S(2)}) collective-permute-start(bf16[1024,512]{1,0:T(8,128)(2,1)S(1)} %constant_dynamic-update-slice_fusion.refs_2_), channel_id=1, source_target_pairs={{0,192},{8,56},{16,208},{24,8},{32,224},{40,24},{48,240},{56,40},{... | collective-permute-start | bytes 3145736 | tf_op jit(solution)/shard_map/ppermute | solution.py:227
  65.8 22.6 %collective-permute-start.3 = (bf16[1024,512]{1,0:T(8,128)(2,1)S(1)}, bf16[1024,512]{1,0:T(8,128)(2,1)S(1)}, u32[]{:S(2)}, u32[]{:S(2)}) collective-permute-start(bf16[1024,512]{1,0:T(8,128)(2,1)S(1)} %constant_dynamic-update-slice_fusion.refs_2_), channel_id=1, source_target_pairs={{0,64},{8,24},{16,80},{24,40},{32,96},{40,56},{48,112},{56,8},{64,... | collective-permute-start | bytes 3145736 | tf_op jit(solution)/shard_map/ppermute | solution.py:226
  76.3 50.4 %all-to-all-start = ((bf16[8,2,256,128]{3,2,1,0:T(8,128)(2,1)}), bf16[8,2,256,128]{3,2,1,0:T(8,128)(2,1)}, u32[]{:S(2)}, u32[]{:S(2)}) async-start(bf16[8,2,256,128]{3,2,1,0:T(8,128)(2,1)} %pad_maximum_fusion), calls=%async_computation | async-start | bytes 2097152 | tf_op jit(solution)/shard_map/all_to_all | solution.py:264
  87.8 24.1 %collective-permute-start.11 = (bf16[1024,512]{1,0:T(8,128)(2,1)S(1)}, bf16[1024,512]{1,0:T(8,128)(2,1)}, u32[]{:S(2)}, u32[]{:S(2)}) collective-permute-start(bf16[1024,512]{1,0:T(8,128)(2,1)S(1)} %constant_dynamic-update-slice_fusion.refs_2_), channel_id=1, source_target_pairs={{0,8},{8,0},{16,24},{24,16},{32,40},{40,32},{48,56},{56,48},{64,72... | collective-permute-start | bytes 3145736 | tf_op jit(solution)/shard_map/ppermute | solution.py:38
  88.1 29.2 %collective-permute-start.10 = (bf16[1024,512]{1,0:T(8,128)(2,1)S(1)}, bf16[1024,512]{1,0:T(8,128)(2,1)S(1)}, u32[]{:S(2)}, u32[]{:S(2)}) collective-permute-start(bf16[1024,512]{1,0:T(8,128)(2,1)S(1)} %collective-permute-done.5.refs_5_), channel_id=1, source_target_pairs={{0,8},{8,0},{16,24},{24,16},{32,40},{40,32},{48,56},{56,48},{64,72... | collective-permute-start | bytes 3145736 | tf_op jit(solution)/shard_map/ppermute | solution.py:38
  88.4 28.9 %collective-permute-start.9 = (bf16[1024,512]{1,0:T(8,128)(2,1)S(1)}, bf16[1024,512]{1,0:T(8,128)(2,1)S(1)}, u32[]{:S(2)}, u32[]{:S(2)}) collective-permute-start(bf16[1024,512]{1,0:T(8,128)(2,1)S(1)} %collective-permute-done.3.refs_4_), channel_id=1, source_target_pairs={{0,8},{8,0},{16,24},{24,16},{32,40},{40,32},{48,56},{56,48},{64,72... | collective-permute-start | bytes 3145736 | tf_op jit(solution)/shard_map/ppermute | solution.py:38
  88.8 21.7 %collective-permute-start.4 = (bf16[512,512]{1,0:T(8,128)(2,1)S(1)}, bf16[512,512]{1,0:T(8,128)(2,1)S(1)}, u32[]{:S(2)}, u32[]{:S(2)}) collective-permute-start(bf16[512,512]{1,0:T(8,128)(2,1)S(1)} %slice.16), channel_id=1, source_target_pairs={{0,64},{8,24},{16,80},{24,40},{32,96},{40,56},{48,112},{56,8},{64,... | collective-permute-start | bytes 1572872 | tf_op jit(solution)/shard_map/ppermute | solution.py:228
  88.9 21.5 %collective-permute-start.6 = (bf16[512,512]{1,0:T(8,128)(2,1)S(1)}, bf16[512,512]{1,0:T(8,128)(2,1)S(1)}, u32[]{:S(2)}, u32[]{:S(2)}) collective-permute-start(bf16[512,512]{1,0:T(8,128)(2,1)S(1)} %slice.17), channel_id=1, source_target_pairs={{0,192},{8,56},{16,208},{24,8},{32,224},{40,24},{48,240},{56,40},{... | collective-permute-start | bytes 1572872 | tf_op jit(solution)/shard_map/ppermute | solution.py:229
  110.5 12.8 %collective-permute-start.7 = (bf16[512,512]{1,0:T(8,128)(2,1)S(1)}, bf16[512,512]{1,0:T(8,128)(2,1)S(1)}, u32[]{:S(2)}, u32[]{:S(2)}) collective-permute-start(bf16[512,512]{1,0:T(8,128)(2,1)S(1)} %collective-permute-done.4.refs_4_), channel_id=1, source_target_pairs={{0,8},{8,0},{16,24},{24,16},{32,40},{40,32},{48,56},{56,48},{64,72... | collective-permute-start | bytes 1572872 | tf_op jit(solution)/shard_map/ppermute | solution.py:38
  110.5 12.8 %collective-permute-start.8 = (bf16[512,512]{1,0:T(8,128)(2,1)S(1)}, bf16[512,512]{1,0:T(8,128)(2,1)S(1)}, u32[]{:S(2)}, u32[]{:S(2)}) collective-permute-start(bf16[512,512]{1,0:T(8,128)(2,1)S(1)} %collective-permute-done.6.refs_5_), channel_id=1, source_target_pairs={{0,8},{8,0},{16,24},{24,16},{32,40},{40,32},{48,56},{56,48},{64,72... | collective-permute-start | bytes 1572872 | tf_op jit(solution)/shard_map/ppermute | solution.py:38
  116.3 1.0 copy-start
  123.2 3.5 %copy-start.3 = (f32[512,128]{1,0:T(8,128)S(1)}, f32[512,128]{1,0:T(8,128)}, u32[]{:S(2)}) copy-start(f32[512,128]{1,0:T(8,128)} %get-tuple-element.19.sin_ref) | copy-start | bytes 786436
  123.2 3.5 %copy-start.4 = (s32[1,4,8]{2,1,0:T(4,128)S(1)}, s32[1,4,8]{2,1,0:T(4,128)}, u32[]{:S(2)}) copy-start(s32[1,4,8]{2,1,0:T(4,128)} %param.11) | copy-start | bytes 388
  135.1 15.4 %collective-permute-start.12 = (bf16[512,512]{1,0:T(8,128)(2,1)S(1)}, bf16[512,512]{1,0:T(8,128)(2,1)S(1)}, u32[]{:S(2)}, u32[]{:S(2)}) collective-permute-start(bf16[512,512]{1,0:T(8,128)(2,1)S(1)} %attend.1.refs_0_), channel_id=1, source_target_pairs={{0,1},{1,2},{2,3},{3,4},{4,5},{5,6},{6,7},{7,0},{8,9},{9,10},{10,1... | collective-permute-start | bytes 1572872 | tf_op jit(solution)/shard_map/ppermute | solution.py:289
  137.2 13.8 %collective-permute-start.16 = (bf16[512,512]{1,0:T(8,128)(2,1)S(1)}, bf16[512,512]{1,0:T(8,128)(2,1)S(1)}, u32[]{:S(2)}, u32[]{:S(2)}) collective-permute-start(bf16[512,512]{1,0:T(8,128)(2,1)S(1)} %attend.1.refs_0_), channel_id=1, source_target_pairs={{0,7},{1,0},{2,1},{3,2},{4,3},{5,4},{6,5},{7,6},{8,15},{9,8},{10,9... | collective-permute-start | bytes 1572872 | tf_op jit(solution)/shard_map/ppermute | solution.py:290
  150.5 14.5 %collective-permute-start.13 = (bf16[512,512]{1,0:T(8,128)(2,1)S(1)}, bf16[512,512]{1,0:T(8,128)(2,1)S(1)}, u32[]{:S(2)}, u32[]{:S(2)}) collective-permute-start(bf16[512,512]{1,0:T(8,128)(2,1)S(1)} %collective-permute-done.12.refs_0_), channel_id=1, source_target_pairs={{0,1},{1,2},{2,3},{3,4},{4,5},{5,6},{6,7},{7,0},{8,9},{9,10},{10,1... | collective-permute-start | bytes 1572872 | tf_op jit(solution)/shard_map/ppermute | solution.py:289
  151.0 13.9 %collective-permute-start.17 = (bf16[512,512]{1,0:T(8,128)(2,1)S(1)}, bf16[512,512]{1,0:T(8,128)(2,1)}, u32[]{:S(2)}, u32[]{:S(2)}) collective-permute-start(bf16[512,512]{1,0:T(8,128)(2,1)S(1)} %collective-permute-done.16.refs_1_), channel_id=1, source_target_pairs={{0,7},{1,0},{2,1},{3,2},{4,3},{5,4},{6,5},{7,6},{8,15},{9,8},{10,9... | collective-permute-start | bytes 1572872 | tf_op jit(solution)/shard_map/ppermute | solution.py:290
  164.9 21.3 %copy-start.1 = (bf16[512,512]{1,0:T(8,128)(2,1)}, bf16[512,512]{1,0:T(8,128)(2,1)S(1)}, u32[]{:S(2)}) copy-start(bf16[512,512]{1,0:T(8,128)(2,1)S(1)} %collective-permute-done.13.refs_0_) | copy-start | bytes 1572868
  164.9 13.5 %collective-permute-start.14 = (bf16[512,512]{1,0:T(8,128)(2,1)S(1)}, bf16[512,512]{1,0:T(8,128)(2,1)S(1)}, u32[]{:S(2)}, u32[]{:S(2)}) collective-permute-start(bf16[512,512]{1,0:T(8,128)(2,1)S(1)} %collective-permute-done.13.refs_0_), channel_id=1, source_target_pairs={{0,1},{1,2},{2,3},{3,4},{4,5},{5,6},{6,7},{7,0},{8,9},{9,10},{10,1... | collective-permute-start | bytes 1572872 | tf_op jit(solution)/shard_map/ppermute | solution.py:289
  165.0 13.7 %collective-permute-start.18 = (bf16[512,512]{1,0:T(8,128)(2,1)}, bf16[512,512]{1,0:T(8,128)(2,1)S(1)}, u32[]{:S(2)}, u32[]{:S(2)}) collective-permute-start(bf16[512,512]{1,0:T(8,128)(2,1)} %collective-permute-done.17.refs_1_), channel_id=1, source_target_pairs={{0,7},{1,0},{2,1},{3,2},{4,3},{5,4},{6,5},{7,6},{8,15},{9,8},{10,9... | collective-permute-start | bytes 1572872 | tf_op jit(solution)/shard_map/ppermute | solution.py:290
  178.5 7.8 %collective-permute-start.15 = (bf16[256,512]{1,0:T(8,128)(2,1)S(1)}, bf16[256,512]{1,0:T(8,128)(2,1)}, u32[]{:S(2)}, u32[]{:S(2)}) collective-permute-start(bf16[256,512]{1,0:T(8,128)(2,1)S(1)} %slice.18), channel_id=1, source_target_pairs={{0,1},{1,2},{2,3},{3,4},{4,5},{5,6},{6,7},{7,0},{8,9},{9,10},{10,1... | collective-permute-start | bytes 786440 | tf_op jit(solution)/shard_map/ppermute | solution.py:291
  179.3 7.4 %collective-permute-start.19 = (bf16[256,512]{1,0:T(8,128)(2,1)}, bf16[256,512]{1,0:T(8,128)(2,1)}, u32[]{:S(2)}, u32[]{:S(2)}) collective-permute-start(bf16[256,512]{1,0:T(8,128)(2,1)} %slice.19), channel_id=1, source_target_pairs={{0,7},{1,0},{2,1},{3,2},{4,3},{5,4},{6,5},{7,6},{8,15},{9,8},{10,9... | collective-permute-start | bytes 786440 | tf_op jit(solution)/shard_map/ppermute | solution.py:292
  190.8 4.2 %copy-start.2 = (bf16[512,512]{1,0:T(8,128)(2,1)S(1)}, bf16[512,512]{1,0:T(8,128)(2,1)}, u32[]{:S(2)}) copy-start(bf16[512,512]{1,0:T(8,128)(2,1)} %copy-done.1) | copy-start | bytes 1572868
Sparse Core Ops, SparseCore 0:
  46.1 67.6 all-gather.2

commit v2 on v1

--- a/solution.py
+++ b/solution.py
@@ -105,8 +105,8 @@
     )(index, *([tokens] * terms), *pieces, *sums)
 
 
-def attend_kernel(heads, entries, own_first, blocks_ref, q_ref, cos_ref, sin_ref, kv_ref, out_ref, keys, values):
-    b = pl.program_id(0)
+def attend_kernel(heads, entries, first, own_first, blocks_ref, q_ref, cos_ref, sin_ref, kv_ref, out_ref, keys, values, queries):
+    b = first + pl.program_id(0)
     own = own_first + b
     for n in range(entries):
         block = blocks_ref[b, n]
@@ -119,38 +119,43 @@
     cos, sin = cos_ref[...], sin_ref[...]
     for h in range(heads):
         x = q_ref[:, h * HEAD : (h + 1) * HEAD]
-        query = (x * cos + pltpu.roll(x, HEAD // 2, 1) * sin).astype(BF16)
-        scores = lax.dot_general(query, keys[...], (((1,), (1,)), ((), ())), preferred_element_type=F32)
-        kept = []
-        for n in range(entries):
-            left_out = jnp.logical_and(late, blocks_ref[b, n] == own)
-            kept.append(jnp.where(left_out, -jnp.inf, scores[:, n * BLOCK : (n + 1) * BLOCK]))
-        scores = jnp.concatenate(kept, axis=1)
-        top = jnp.max(scores, axis=1, keepdims=True)
-        raised = jnp.exp(scores - top)
+        queries[h * BLOCK : (h + 1) * BLOCK, :] = (x * cos + pltpu.roll(x, HEAD // 2, 1) * sin).astype(BF16)
+    scores = lax.dot_general(queries[...], keys[...], (((1,), (1,)), ((), ())), preferred_element_type=F32)
+    hidden = [jnp.logical_and(late, blocks_ref[b, n] == own) for n in range(entries)]
+    for h in range(heads):
+        strip = scores[h * BLOCK : (h + 1) * BLOCK, :]
+        kept = [jnp.where(hidden[n], -jnp.inf, strip[:, n * BLOCK : (n + 1) * BLOCK]) for n in range(entries)]
+        strip = jnp.concatenate(kept, axis=1)
+        raised = jnp.exp(strip - jnp.max(strip, axis=1, keepdims=True))
         total = jnp.sum(raised, axis=1, keepdims=True)
         mixed = jnp.dot(raised.astype(BF16), values[...], preferred_element_type=F32)
         out_ref[:, h * HEAD : (h + 1) * HEAD] = (mixed / total).astype(BF16)
 
 
-def attend(projected, cos, sin, kv, lists):
-    rows, cols = projected.shape
+def attend(projected, cos, sin, kv, lists, first, count):
+    cols = projected.shape[1]
     query_blocks, entries = lists.shape
     owners, _, held, _ = kv.shape
     heads = cols // HEAD
+    rows = count * BLOCK
     own_first = owners * held // BLOCK - query_blocks
-    strip = pl.BlockSpec((BLOCK, cols), lambda b, lists_ref: (b, 0))
-    table = pl.BlockSpec((BLOCK, HEAD), lambda b, lists_ref: (b, 0))
-    return pl.pallas_call(
-        functools.partial(attend_kernel, heads, entries, own_first),
+    table = pl.BlockSpec((BLOCK, HEAD), lambda b, lists_ref: (first + b, 0))
+    return pl.pallas_call(
+        functools.partial(attend_kernel, heads, entries, first, own_first),
         grid_spec=pltpu.PrefetchScalarGridSpec(
             num_scalar_prefetch=1,
-            grid=(query_blocks,),
-            in_specs=[strip, table, table, pl.BlockSpec(kv.shape, lambda b, lists_ref: (0, 0, 0, 0))],
-            out_specs=strip,
+            grid=(count,),
+            in_specs=[
+                pl.BlockSpec((BLOCK, cols), lambda b, lists_ref: (first + b, 0)),
+                table,
+                table,
+                pl.BlockSpec(kv.shape, lambda b, lists_ref: (0, 0, 0, 0)),
+            ],
+            out_specs=pl.BlockSpec((BLOCK, cols), lambda b, lists_ref: (b, 0)),
             scratch_shapes=[
                 pltpu.VMEM((entries * BLOCK, HEAD), BF16),
                 pltpu.VMEM((entries * BLOCK, HEAD), BF16),
+                pltpu.VMEM((heads * BLOCK, HEAD), BF16),
             ],
         ),
         out_shape=jax.ShapeDtypeStruct((rows, cols), BF16),
@@ -165,47 +170,49 @@
 
 
 def output_kernel(terms, has_sum, index_ref, *refs):
-    contexts, weights = refs[:terms], refs[terms : 2 * terms]
+    contexts, weights = refs[: 2 * terms], refs[2 * terms : 3 * terms]
     out = refs[-1]
-    total = jnp.dot(contexts[0][...], weights[0][0], preferred_element_type=F32)
-    for c, w in zip(contexts[1:], weights[1:]):
-        total += jnp.dot(c[...], w[0], preferred_element_type=F32)
-    if has_sum:
-        total += refs[2 * terms][...]
-    out[...] = total.astype(out.dtype)
+    rows = contexts[0].shape[0]
+    for half in range(2):
+        here = pl.ds(half * rows, rows)
+        total = jnp.dot(contexts[half][...], weights[0][0], preferred_element_type=F32)
+        for t in range(1, terms):
+            total += jnp.dot(contexts[2 * t + half][...], weights[t][0], preferred_element_type=F32)
+        if has_sum:
+            total += refs[3 * terms][here, :]
+        out[here, :] = total.astype(out.dtype)
 
 
 def output(contexts, weights, index, before=None, dtype=F32):
-    rows, depth = contexts[0].shape
+    rows, depth = contexts[0][0].shape
     terms = len(contexts)
-    blocks, _, width = weights.shape
-    owners = 8
-    parts = blocks // owners
+    width = weights.shape[2]
+    parts = index.shape[1]
 
     def weight_spec(t):
-        return pl.BlockSpec((1, depth, width), lambda j, index_ref: (j * owners + index_ref[t], 0, 0))
-
-    strip = pl.BlockSpec((rows, width), lambda j, index_ref: (0, j))
+        return pl.BlockSpec((1, depth, width), lambda j, index_ref: (index_ref[t, j], 0, 0))
+
+    strip = pl.BlockSpec((2 * rows, width), lambda j, index_ref: (0, j))
     sums = [] if before is None else [before]
     return pl.pallas_call(
         functools.partial(output_kernel, terms, before is not None),
         grid_spec=pltpu.PrefetchScalarGridSpec(
             num_scalar_prefetch=1,
             grid=(parts,),
-            in_specs=[pl.BlockSpec((rows, depth), lambda j, index_ref: (0, 0))] * terms
+            in_specs=[pl.BlockSpec((rows, depth), lambda j, index_ref: (0, 0))] * (2 * terms)
             + [weight_spec(t) for t in range(terms)]
             + [strip] * len(sums),
             out_specs=strip,
         ),
-        out_shape=jax.ShapeDtypeStruct((rows, parts * width), dtype),
+        out_shape=jax.ShapeDtypeStruct((2 * rows, parts * width), dtype),
         compiler_params=pltpu.CompilerParams(vmem_limit_bytes=VMEM_LIMIT),
         cost_estimate=pl.CostEstimate(
-            flops=2 * rows * depth * width * parts * terms,
-            bytes_accessed=2 * depth * (rows + width * parts) * terms + 8 * rows * width * parts,
+            flops=4 * rows * depth * width * parts * terms,
+            bytes_accessed=2 * depth * (2 * rows + width * parts) * terms + 16 * rows * width * parts,
             transcendentals=0,
         ),
         name="output",
-    )(index, *contexts, *([weights] * terms), *sums)
+    )(index, *[c for pair in contexts for c in pair], *([weights] * terms), *sums)
 
 
 def tables(rows, first):
@@ -217,18 +224,98 @@
     return jnp.concatenate([cos, cos], axis=1), jnp.concatenate([-sin, sin], axis=1)
 
 
-def gather_wq(wq):
+def side_by_side_kernel(count, *refs):
+    pieces, out, done = refs[:count], refs[count], refs[count + 1]
+    copies = []
+    start = 0
+    for n, piece in enumerate(pieces):
+        size = piece.shape[0]
+        copies.append(pltpu.make_async_copy(piece, out.at[pl.ds(start, size)], done.at[n]))
+        start += size
+    for copy in copies:
+        copy.start()
+    for copy in copies:
+        copy.wait()
+
+
+def side_by_side(pieces):
+    total = sum(p.shape[0] for p in pieces)
+    anywhere = pl.BlockSpec(memory_space=pl.ANY)
+    out = jax.ShapeDtypeStruct((total,) + pieces[0].shape[1:], pieces[0].dtype)
+    return pl.pallas_call(
+        functools.partial(side_by_side_kernel, len(pieces)),
+        in_specs=[anywhere] * len(pieces),
+        out_specs=anywhere,
+        out_shape=out,
+        scratch_shapes=[pltpu.SemaphoreType.DMA((len(pieces),))],
+        compiler_params=pltpu.CompilerParams(vmem_limit_bytes=VMEM_LIMIT),
+        cost_estimate=pl.CostEstimate(flops=0, bytes_accessed=4 * out.size, transcendentals=0),
+        name="side_by_side",
+    )(*pieces)
+
+
+def split_heads_kernel(keys, values, out):
+    out[0, 0] = keys[...]
+    out[0, 1] = values[...]
+
+
+def split_heads(keys, values):
+    held, cols = keys.shape
+    heads = cols // HEAD
+    column = pl.BlockSpec((held, HEAD), lambda h: (0, h))
+    return pl.pallas_call(
+        split_heads_kernel,
+        grid=(heads,),
+        in_specs=[column, column],
+        out_specs=pl.BlockSpec((1, 2, held, HEAD), lambda h: (h, 0, 0, 0)),
+        out_shape=jax.ShapeDtypeStruct((heads, 2, held, HEAD), keys.dtype),
+        compiler_params=pltpu.CompilerParams(vmem_limit_bytes=VMEM_LIMIT),
+        cost_estimate=pl.CostEstimate(flops=0, bytes_accessed=8 * keys.size, transcendentals=0),
+        name="split_heads",
+    )(keys, values)
+
+
+def after(value, *earlier):
+    return lax.optimization_barrier((value,) + earlier)[0]
+
+
+def wo_target(f, c):
+    core, x, y = f % 2, f // 2 % SIDE, f // 2 // SIDE
+    x_to = jnp.where(c % 2 == 0, x, x + jnp.where(x % 2 == 0, -1, 1))
+    return fsdp_index(y + c // 2, x_to, core)
+
+
+def wo_moves(fsdp_count, ctx_count):
+    parts = fsdp_count // ctx_count
+    moves = []
+    for f in range(fsdp_count):
+        for c in range(ctx_count):
+            core, x, y = f % 2, f // 2 % SIDE, f // 2 // SIDE
+            x_to = x if c % 2 == 0 else x + (-1 if x % 2 == 0 else 1)
+            moves.append((f * ctx_count + c, fsdp_index(y + c // 2, x_to, core) * ctx_count + f // parts))
+    return moves
+
+
+def project_all(tokens, wq, by_head):
+    own_line, near, far_away = wq_indices()
     minus = lax.ppermute(wq, "fsdp", ring_pairs(0, 1))
     plus = lax.ppermute(wq, "fsdp", ring_pairs(0, -1))
     far = lax.ppermute(wq, "fsdp", ring_pairs(0, 2))
-    line = jnp.concatenate([wq, minus, plus, far], axis=0)
+    line = side_by_side([wq, minus, plus, after(far, by_head)])
+    kv = lax.all_to_all(after(by_head, line), "ctx", 0, 0, tiled=True)
     half = line.shape[0] // 2
     line_minus = lax.ppermute(line, "fsdp", ring_pairs(1, 1))
     line_plus = lax.ppermute(line, "fsdp", ring_pairs(1, -1))
-    far_top = lax.ppermute(line_minus[:half], "fsdp", ring_pairs(1, 1))
-    far_low = lax.ppermute(line_plus[half:], "fsdp", ring_pairs(1, -1))
-    groups = [[line], [line_minus, line_plus], [far_top, far_low]]
-    return [group + [swap_cores(piece) for piece in group] for group in groups]
+    first = project(tokens, [line, swap_cores(line)], own_line)
+    top, low, waited = lax.optimization_barrier((line_minus[:half], line_plus[half:], first))
+    far_top = lax.ppermute(top, "fsdp", ring_pairs(1, 1))
+    far_low = lax.ppermute(low, "fsdp", ring_pairs(1, -1))
+    second = project(
+        tokens, [line_minus, line_plus, swap_cores(line_minus), swap_cores(line_plus)], near, waited
+    )
+    far_top, far_low, second, kv = lax.optimization_barrier((far_top, far_low, second, kv))
+    third = project(tokens, [far_top, far_low, swap_cores(far_top), swap_cores(far_low)], far_away, second)
+    return third, kv, second
 
 
 def wq_indices():
@@ -252,50 +339,33 @@
     rows = tokens.shape[0]
     held = key_cache.shape[0]
 
-    groups = gather_wq(wq)
-
-    by_head = jnp.stack(
-        [
-            key_cache.reshape(held, ctx_count, HEAD).transpose(1, 0, 2),
-            value_cache.reshape(held, ctx_count, HEAD).transpose(1, 0, 2),
-        ],
-        axis=1,
-    )
-    kv = lax.all_to_all(by_head, "ctx", 0, 0, tiled=True)
-
     parts = fsdp_count // ctx_count
-    moves = []
-    for f in range(fsdp_count):
-        for c in range(ctx_count):
-            plane, part = f // parts, f % parts
-            moves.append((f * ctx_count + c, (part * ctx_count + (c + plane) % ctx_count) * ctx_count + plane))
-    wo_here = lax.ppermute(wo, ("fsdp", "ctx"), moves)
-    weights = lax.all_gather(wo_here, "fsdp", axis=0, tiled=False)
+    wo_here = lax.ppermute(wo, ("fsdp", "ctx"), wo_moves(fsdp_count, ctx_count))
+    by_head = split_heads(key_cache, value_cache)
+    projected, kv, begun = project_all(tokens, wq, by_head)
+    weights = lax.all_gather(after(wo_here, begun), "fsdp", axis=0, tiled=False)
 
     cos, sin = tables(rows, held * ctx_count - rows)
-    projected = None
-    for pieces, index in zip(groups, wq_indices()):
-        projected = project(tokens, pieces, index, projected)
-    context = attend(projected, cos, sin, kv, key_blocks[0])
+    blocks = rows // BLOCK // 2
+    contexts = [attend(projected, cos, sin, kv, key_blocks[0], n * blocks, blocks) for n in range(2)]
 
     def owner(*offsets):
-        return jnp.stack([(2 * z + o) % ctx_count for o in offsets])
+        def at(offset):
+            return jnp.stack([wo_target(z * parts + j, (z + offset) % ctx_count) for j in range(parts)])
+
+        return jnp.stack([at(o) for o in offsets])
 
     right = [(i, (i + 1) % ctx_count) for i in range(ctx_count)]
     left = [(i, (i - 1) % ctx_count) for i in range(ctx_count)]
-    half = rows // 2
-    down, up = [context], [context]
+    down, up = [contexts], [contexts]
     for _ in range(3):
-        down.append(lax.ppermute(down[-1], "ctx", right))
-        up.append(lax.ppermute(up[-1], "ctx", left))
-    far_top = lax.ppermute(down[-1][:half], "ctx", right)
-    far_low = lax.ppermute(up[-1][half:], "ctx", left)
-
-    total = output([context], weights, owner(0))
-    for s in (1, 2, 3):
-        total = output([down[s], up[s]], weights, owner(-s, s), total)
-    far = jnp.concatenate([far_top, far_low], axis=0)
-    return output([far], weights, owner(4), total, BF16)
+        down.append([lax.ppermute(c, "ctx", right) for c in down[-1]])
+        up.append([lax.ppermute(c, "ctx", left) for c in up[-1]])
+    weights, last_down, last_up = lax.optimization_barrier((weights, down[3][0], up[3][1]))
+    far = [lax.ppermute(last_down, "ctx", right), lax.ppermute(last_up, "ctx", left)]
+
+    total = output([contexts, down[1], up[1], down[2], up[2]], weights, owner(0, -1, 1, -2, 2))
+    return output([down[3], up[3], far], weights, owner(-3, 3, 4), total, BF16)
 
 
 def solution(mesh):

time: 218 us -> 161 us (0.74); the launches traced: 214 us -> 160 us
  waiting for transfers between devices: 98.1 us -> 54.3 us
  Pallas kernels: 41.7 us -> 35.6 us
  local copies, waits for them, and re-layouts: 11.8 us -> 5.84 us
  starting transfers between devices: 42.1 us -> 46.3 us
  other arithmetic: 5.93 us -> 2.05 us
    ppermute x16 -> x22, waiting for transfers between devices: 98.1 us -> 38.6 us  [the longest x6 18.9 us: body(): down.append([lax.ppermute(c, 'ctx', right) for c in down[-1]])]
    all_gather x1, waiting for transfers between devices: 0.02 us -> 14.7 us  [body(): weights = lax.all_gather(after(wo_here, begun), 'fsdp', axis=0, tiled=False)]
    pallas_call x5 -> x2, Pallas kernels: 19.6 us -> 11.8 us  [output(): pl.pallas_call(functools.partial(output_kernel, terms, before is not None...]
    ppermute x16 -> x22, starting transfers between devices: 30.6 us -> 37 us  [the longest x6 15.2 us: body(): up.append([lax.ppermute(c, 'ctx', left) for c in up[-1]])]
    reshape x2 -> x0, local copies, waits for them, and re-layouts: 4.11 us -> none  [the longest x1 2.08 us: body(): key_cache.reshape(held, ctx_count, HEAD).transpose(1, 0, 2)]
    unnamed x17 -> x12, local copies, waits for them, and re-layouts: 6.84 us -> 4.71 us
    pallas_call x1 -> x4, Pallas kernels: 8.29 us -> 9.03 us  [the longest x2 6.05 us: attend(): pl.pallas_call(functools.partial(attend_kernel, heads, entries, first, ow...]
  transfers between devices with their start and end apart: 23 -> 29, of which waited for: 9 -> 15; matrix products, arithmetic and copies ran while one was open for 7% -> 2% of each run, Pallas kernels for 10% -> 19%
where the time goes in v2:
time: 161 us; the launch traced here: 160 us
  waiting for transfers between devices  54.3 us (34%)
  starting transfers between devices  46.3 us (29%)
  Pallas kernels  35.6 us (22%)
  between operations  15.7 us (10%)
  local copies, waits for them, and re-layouts  5.84 us (4%)
  other arithmetic  2.05 us (1%)
    ppermute x6, waiting for transfers between devices, body(): down.append([lax.ppermute(c, 'ctx', right) for c in down[-1]])  18.9 us
    ppermute x6, starting transfers between devices, body(): up.append([lax.ppermute(c, 'ctx', left) for c in up[-1]])  15.2 us
    pallas_call x3, Pallas kernels, project(): pl.pallas_call(functools.partial(project_kernel, terms, before is not Non...  14.8 us
    all_gather x1, waiting for transfers between devices, body(): weights = lax.all_gather(after(wo_here, begun), 'fsdp', axis=0, tiled=False)  14.7 us
    pallas_call x2, Pallas kernels, output(): pl.pallas_call(functools.partial(output_kernel, terms, before is not None...  11.8 us
    ppermute x1, waiting for transfers between devices, body(): wo_here = lax.ppermute(wo, ('fsdp', 'ctx'), wo_moves(fsdp_count, ctx_count))  9.58 us
    all_to_all x1, starting transfers between devices, project_all(): kv = lax.all_to_all(after(by_head, line), 'ctx', 0, 0, tiled=True)  8.47 us
    pallas_call x2, Pallas kernels, attend(): pl.pallas_call(functools.partial(attend_kernel, heads, entries, first, ow...  6.05 us
  transfers between devices with their start and end apart: 29, of which 15 were waited for; matrix products, arithmetic and copies ran while one was open for 2% of the time, Pallas kernels for 19%

profile of v2, /device:TPU:6, one launch (start us, length us, event | category | flops | bytes accessed | tf_op | source)
XLA Modules:
  0.0 159.8 jit_solution(16380721798180016279)
XLA Ops:
  6.5 1.4 collective-permute-start.2
  7.9 2.1 %collective-permute-start = (bf16[256,512]{1,0:T(8,128)(2,1)}, bf16[256,512]{1,0:T(8,128)(2,1)S(1)}, u32[]{:S(2)}, u32[]{:S(2)}) collective-permute-start(bf16[256,512]{1,0:T(8,128)(2,1)} %refs_0_.4), channel_id=1, source_target_pairs={{0,16},{8,72},{16,32},{24,88},{32,48},{40,104},{48,0},{56,120},{64... | collective-permute-start | bytes 786440 | tf_op jit(solution)/shard_map/ppermute | solution.py:301
  10.0 1.0 copy-done.1
  11.1 1.0 copy-done.2
  12.1 2.9 %split_heads.1 = bf16[8,2,256,128]{3,2,1,0:T(8,128)(2,1)} custom-call(bf16[256,1024]{1,0:T(8,128)(2,1)S(1)} %copy-done.1, bf16[256,1024]{1,0:T(8,128)(2,1)S(1)} %copy-done.2), custom_call_target="tpu_custom_call" | custom-call | bytes 2097152 | tf_op jit(solution)/shard_map/split_heads/pallas_call | solution.py:266
  15.0 2.0 %collective-permute-done.refs_1_ = bf16[256,512]{1,0:T(8,128)(2,1)S(1)} collective-permute-done((bf16[256,512]{1,0:T(8,128)(2,1)}, bf16[256,512]{1,0:T(8,128)(2,1)S(1)}, u32[]{:S(2)}, u32[]{:S(2)}) %collective-permute-start) | collective-permute-done | bytes 262176 | tf_op jit(solution)/shard_map/ppermute | solution.py:301
  17.0 0.8 collective-permute-done.1.refs_2_
  17.8 0.9 copy-done.3
  18.9 1.7 %collective-permute-start.3 = (bf16[1024,512]{1,0:T(8,128)(2,1)S(1)}, bf16[1024,512]{1,0:T(8,128)(2,1)S(1)}, u32[]{:S(2)}, u32[]{:S(2)}) collective-permute-start(bf16[1024,512]{1,0:T(8,128)(2,1)S(1)} %side_by_side.1.refs_2_), channel_id=1, source_target_pairs={{0,64},{8,24},{16,80},{24,40},{32,96},{40,56},{48,112},{56,8},{64,... | collective-permute-start | bytes 3145736 | tf_op jit(solution)/shard_map/ppermute | solution.py:307
  20.6 1.7 %collective-permute-start.4 = (bf16[1024,512]{1,0:T(8,128)(2,1)S(1)}, bf16[1024,512]{1,0:T(8,128)(2,1)}, u32[]{:S(2)}, u32[]{:S(2)}) collective-permute-start(bf16[1024,512]{1,0:T(8,128)(2,1)S(1)} %side_by_side.1.refs_2_), channel_id=1, source_target_pairs={{0,192},{8,56},{16,208},{24,8},{32,224},{40,24},{48,240},{56,40},{... | collective-permute-start | bytes 3145736 | tf_op jit(solution)/shard_map/ppermute | solution.py:308
  22.2 8.5 %all-to-all-start = ((bf16[8,2,256,128]{3,2,1,0:T(8,128)(2,1)}), bf16[8,2,256,128]{3,2,1,0:T(8,128)(2,1)S(1)}, u32[]{:S(2)}, u32[]{:S(2)}) async-start(bf16[8,2,256,128]{3,2,1,0:T(8,128)(2,1)} %split_heads.1), calls=%async_computation | async-start | bytes 2097152 | tf_op jit(solution)/shard_map/all_to_all | solution.py:305
  30.8 4.2 %collective-permute-done.3.refs_4_ = bf16[1024,512]{1,0:T(8,128)(2,1)S(1)} collective-permute-done((bf16[1024,512]{1,0:T(8,128)(2,1)S(1)}, bf16[1024,512]{1,0:T(8,128)(2,1)S(1)}, u32[]{:S(2)}, u32[]{:S(2)}) %collective-permute-start.3) | collective-permute-done | bytes 1048608 | tf_op jit(solution)/shard_map/ppermute | solution.py:307
  35.0 0.5 collective-permute-done.4.refs_5_
  35.5 3.8 %collective-permute-start.24 = (bf16[512,256]{1,0:T(8,128)(2,1)}, bf16[512,256]{1,0:T(8,128)(2,1)S(1)}, u32[]{:S(2)}, u32[]{:S(2)}) collective-permute-start(bf16[512,256]{1,0:T(8,128)(2,1)} %param.8), channel_id=1, source_target_pairs={{0,0},{1,48},{2,64},{3,112},{4,128},{5,176},{6,192},{7,240},{8,8},... | collective-permute-start | bytes 786440 | tf_op jit(solution)/shard_map/ppermute | solution.py:343
  40.5 1.1 slice.9
  41.6 4.4 %project.3.refs_8_ = f32[512,512]{1,0:T(8,128)S(1)} custom-call(s32[2,4]{1,0:T(2,128)S(1)} %pad_add_fusion.3.index_ref, bf16[512,8192]{1,0:T(8,128)(2,1)} %refs_3_.3, bf16[512,8192]{1,0:T(8,128)(2,1)} %refs_3_.3, bf16[1024,512]{1,0:T(8,128)(2,1)S(1)} %side_by_side.1.refs_2_, bf16[1024,512]{1,0:T(8,128)(2,1)} %collective-permute-done.5.refs_3_), custom_call_target="tpu_custom_call" | custom-call | flops 1073741824 | bytes 6291456 | tf_op jit(solution)/shard_map/project/pallas_call | solution.py:88
  46.0 1.0 copy-done
  47.0 4.2 %collective-permute-start.6 = (bf16[512,512]{1,0:T(8,128)(2,1)S(1)}, bf16[512,512]{1,0:T(8,128)(2,1)}, u32[]{:S(2)}, u32[]{:S(2)}) collective-permute-start(bf16[512,512]{1,0:T(8,128)(2,1)S(1)} %slice.8), channel_id=1, source_target_pairs={{0,64},{8,24},{16,80},{24,40},{32,96},{40,56},{48,112},{56,8},{64,... | collective-permute-start | bytes 1572872 | tf_op jit(solution)/shard_map/ppermute | solution.py:311
  51.2 2.5 %collective-permute-start.7 = (bf16[512,512]{1,0:T(8,128)(2,1)S(1)}, bf16[512,512]{1,0:T(8,128)(2,1)}, u32[]{:S(2)}, u32[]{:S(2)}) collective-permute-start(bf16[512,512]{1,0:T(8,128)(2,1)S(1)} %slice.9), channel_id=1, source_target_pairs={{0,192},{8,56},{16,208},{24,8},{32,224},{40,24},{48,240},{56,40},{... | collective-permute-start | bytes 1572872 | tf_op jit(solution)/shard_map/ppermute | solution.py:312
  53.9 6.7 %project.4.refs_8_ = f32[512,512]{1,0:T(8,128)S(1)} custom-call(s32[4,4]{1,0:T(4,128)S(1)} %pad_add_fusion.2.index_ref, bf16[512,8192]{1,0:T(8,128)(2,1)} %refs_3_.3, bf16[512,8192]{1,0:T(8,128)(2,1)} %refs_3_.3, bf16[512,8192]{1,0:T(8,128)(2,1)} %refs_3_.3, bf16[512,8192]{1,0:T(8,128)(2,1)} %refs_3_.3, ...), custom_call_target="tpu_custom_call" | custom-call | flops 2147483648 | bytes 10485760 | tf_op jit(solution)/shard_map/project/pallas_call | solution.py:88
  60.6 2.0 %collective-permute-done.6.refs_4_ = bf16[512,512]{1,0:T(8,128)(2,1)} collective-permute-done((bf16[512,512]{1,0:T(8,128)(2,1)S(1)}, bf16[512,512]{1,0:T(8,128)(2,1)}, u32[]{:S(2)}, u32[]{:S(2)}) %collective-permute-start.6) | collective-permute-done | bytes 524320 | tf_op jit(solution)/shard_map/ppermute | solution.py:311
  62.6 9.6 %collective-permute-done.24 = bf16[512,256]{1,0:T(8,128)(2,1)S(1)} collective-permute-done((bf16[512,256]{1,0:T(8,128)(2,1)}, bf16[512,256]{1,0:T(8,128)(2,1)S(1)}, u32[]{:S(2)}, u32[]{:S(2)}) %collective-permute-start.24) | collective-permute-done | bytes 262176 | tf_op jit(solution)/shard_map/ppermute | solution.py:343
  72.2 0.7 copy-done.5
  73.4 0.4 collective-permute-start.10
  73.8 0.3 collective-permute-start.11
  74.1 1.0 fusion.2
  75.3 0.2 collective-permute-done.10.refs_6_
  75.5 0.7 collective-permute-done.11.refs_7_
  76.3 3.7 %project.5.q_ref = f32[512,512]{1,0:T(8,128)S(1)} custom-call(s32[4,2]{1,0:T(4,128)S(1)} %pad_add_fusion.1.index_ref, bf16[512,8192]{1,0:T(8,128)(2,1)} %refs_3_.3, bf16[512,8192]{1,0:T(8,128)(2,1)} %refs_3_.3, bf16[512,8192]{1,0:T(8,128)(2,1)} %refs_3_.3, bf16[512,8192]{1,0:T(8,128)(2,1)} %refs_3_.3, bf16[512,512]{1,0:T(8,128)(2,1)} %collective-permute-done.6.refs_4_, ...), custom_call_target="tpu_custom_call" | custom-call | flops 1073741824 | bytes 6291456 | tf_op jit(solution)/shard_map/project/pallas_call | solution.py:88
  80.0 3.0 %attend.3.refs_1_ = bf16[256,512]{1,0:T(8,128)(2,1)S(1)} custom-call(s32[4,8]{1,0:T(4,128)S(1)} %bitcast.102, f32[512,512]{1,0:T(8,128)S(1)} %project.5.q_ref, f32[512,128]{1,0:T(8,128)S(1)} %get-tuple-element.46.cos_ref, f32[512,128]{1,0:T(8,128)S(1)} %get-tuple-element.47.sin_ref, bf16[8,2,256,128]{3,2,1,0:T(8,128)(2,1)S(1)} %all-to-all-done.kv_ref), custom_call_target="tpu_custom_call" | custom-call | flops 536870912 | bytes 1835008 | tf_op jit(solution)/shard_map/attend/pallas_call | solution.py:143
  83.0 3.3 %collective-permute-start.21 = (bf16[256,512]{1,0:T(8,128)(2,1)S(1)}, bf16[256,512]{1,0:T(8,128)(2,1)S(1)}, u32[]{:S(2)}, u32[]{:S(2)}) collective-permute-start(bf16[256,512]{1,0:T(8,128)(2,1)S(1)} %attend.3.refs_1_), channel_id=1, source_target_pairs={{0,7},{1,0},{2,1},{3,2},{4,3},{5,4},{6,5},{7,6},{8,15},{9,8},{10,9... | collective-permute-start | bytes 786440 | tf_op jit(solution)/shard_map/ppermute | solution.py:363
  86.3 3.0 %attend.2.refs_0_ = bf16[256,512]{1,0:T(8,128)(2,1)S(1)} custom-call(s32[4,8]{1,0:T(4,128)S(1)} %bitcast.103, f32[512,512]{1,0:T(8,128)S(1)} %project.5.q_ref, f32[512,128]{1,0:T(8,128)S(1)} %get-tuple-element.46.cos_ref, f32[512,128]{1,0:T(8,128)S(1)} %get-tuple-element.47.sin_ref, bf16[8,2,256,128]{3,2,1,0:T(8,128)(2,1)S(1)} %all-to-all-done.kv_ref), custom_call_target="tpu_custom_call" | custom-call | flops 536870912 | bytes 1835008 | tf_op jit(solution)/shard_map/attend/pallas_call | solution.py:143
  89.6 1.0 collective-permute-start.15
  90.6 2.3 %collective-permute-start.18 = (bf16[256,512]{1,0:T(8,128)(2,1)S(1)}, bf16[256,512]{1,0:T(8,128)(2,1)S(1)}, u32[]{:S(2)}, u32[]{:S(2)}) collective-permute-start(bf16[256,512]{1,0:T(8,128)(2,1)S(1)} %attend.2.refs_0_), channel_id=1, source_target_pairs={{0,7},{1,0},{2,1},{3,2},{4,3},{5,4},{6,5},{7,6},{8,15},{9,8},{10,9... | collective-permute-start | bytes 786440 | tf_op jit(solution)/shard_map/ppermute | solution.py:363
  92.9 2.9 %collective-permute-start.22 = (bf16[256,512]{1,0:T(8,128)(2,1)S(1)}, bf16[256,512]{1,0:T(8,128)(2,1)S(1)}, u32[]{:S(2)}, u32[]{:S(2)}) collective-permute-start(bf16[256,512]{1,0:T(8,128)(2,1)S(1)} %collective-permute-done.21.refs_5_), channel_id=1, source_target_pairs={{0,7},{1,0},{2,1},{3,2},{4,3},{5,4},{6,5},{7,6},{8,15},{9,8},{10,9... | collective-permute-start | bytes 786440 | tf_op jit(solution)/shard_map/ppermute | solution.py:363
  95.9 3.9 %collective-permute-done.12.refs_2_ = bf16[256,512]{1,0:T(8,128)(2,1)S(1)} collective-permute-done((bf16[256,512]{1,0:T(8,128)(2,1)S(1)}, bf16[256,512]{1,0:T(8,128)(2,1)S(1)}, u32[]{:S(2)}, u32[]{:S(2)}) %collective-permute-start.12) | collective-permute-done | bytes 262176 | tf_op jit(solution)/shard_map/ppermute | solution.py:362
  100.0 5.5 %collective-permute-done.15.refs_3_ = bf16[256,512]{1,0:T(8,128)(2,1)S(1)} collective-permute-done((bf16[256,512]{1,0:T(8,128)(2,1)S(1)}, bf16[256,512]{1,0:T(8,128)(2,1)S(1)}, u32[]{:S(2)}, u32[]{:S(2)}) %collective-permute-start.15) | collective-permute-done | bytes 262176 | tf_op jit(solution)/shard_map/ppermute | solution.py:362
  105.5 3.2 %collective-permute-start.19 = (bf16[256,512]{1,0:T(8,128)(2,1)S(1)}, bf16[256,512]{1,0:T(8,128)(2,1)S(1)}, u32[]{:S(2)}, u32[]{:S(2)}) collective-permute-start(bf16[256,512]{1,0:T(8,128)(2,1)S(1)} %collective-permute-done.18.refs_4_), channel_id=1, source_target_pairs={{0,7},{1,0},{2,1},{3,2},{4,3},{5,4},{6,5},{7,6},{8,15},{9,8},{10,9... | collective-permute-start | bytes 786440 | tf_op jit(solution)/shard_map/ppermute | solution.py:363
  108.8 2.3 %collective-permute-done.13.refs_6_ = bf16[256,512]{1,0:T(8,128)(2,1)S(1)} collective-permute-done((bf16[256,512]{1,0:T(8,128)(2,1)S(1)}, bf16[256,512]{1,0:T(8,128)(2,1)S(1)}, u32[]{:S(2)}, u32[]{:S(2)}) %collective-permute-start.13) | collective-permute-done | bytes 262176 | tf_op jit(solution)/shard_map/ppermute | solution.py:362
  111.9 4.8 %collective-permute-done.16.refs_7_ = bf16[256,512]{1,0:T(8,128)(2,1)S(1)} collective-permute-done((bf16[256,512]{1,0:T(8,128)(2,1)S(1)}, bf16[256,512]{1,0:T(8,128)(2,1)S(1)}, u32[]{:S(2)}, u32[]{:S(2)}) %collective-permute-start.16) | collective-permute-done | bytes 262176 | tf_op jit(solution)/shard_map/ppermute | solution.py:362
  116.7 3.2 %collective-permute-start.20 = (bf16[256,512]{1,0:T(8,128)(2,1)S(1)}, bf16[256,512]{1,0:T(8,128)(2,1)}, u32[]{:S(2)}, u32[]{:S(2)}) collective-permute-start(bf16[256,512]{1,0:T(8,128)(2,1)S(1)} %collective-permute-done.19.refs_8_), channel_id=1, source_target_pairs={{0,7},{1,0},{2,1},{3,2},{4,3},{5,4},{6,5},{7,6},{8,15},{9,8},{10,9... | collective-permute-start | bytes 786440 | tf_op jit(solution)/shard_map/ppermute | solution.py:363
  119.9 2.4 %collective-permute-done.14.refs_0_ = bf16[256,512]{1,0:T(8,128)(2,1)S(1)} collective-permute-done((bf16[256,512]{1,0:T(8,128)(2,1)S(1)}, bf16[256,512]{1,0:T(8,128)(2,1)S(1)}, u32[]{:S(2)}, u32[]{:S(2)}) %collective-permute-start.14) | collective-permute-done | bytes 262176 | tf_op jit(solution)/shard_map/ppermute | solution.py:362
  122.3 14.7 %all-gather.3.cloned.1.call-done = bf16[16384,256]{1,0:T(8,128)(2,1)} async-done(((bf16[512,256]{1,0:T(8,128)(2,1)}), bf16[16384,256]{1,0:T(8,128)(2,1)}) %all-gather.3.cloned.1.call-update) | async-done | bytes 8388624 | tf_op jit(solution)/shard_map/all_gather | solution.py:346
  137.0 1.6 collective-permute-start.25
  138.5 1.8 %collective-permute-start.26 = (bf16[256,512]{1,0:T(8,128)(2,1)S(1)}, bf16[256,512]{1,0:T(8,128)(2,1)}, u32[]{:S(2)}, u32[]{:S(2)}) collective-permute-start(bf16[256,512]{1,0:T(8,128)(2,1)S(1)} %collective-permute-done.23.refs_3_), channel_id=1, source_target_pairs={{0,7},{1,0},{2,1},{3,2},{4,3},{5,4},{6,5},{7,6},{8,15},{9,8},{10,9... | collective-permute-start | bytes 786440 | tf_op jit(solution)/shard_map/ppermute | solution.py:365
  140.4 6.0 %output.2.refs_9_ = f32[512,1024]{1,0:T(8,128)S(1)} custom-call(s32[5,4]{1,0:T(8,128)S(1)} %stack.419.index_ref, bf16[256,512]{1,0:T(8,128)(2,1)S(1)} %attend.2.refs_0_, bf16[256,512]{1,0:T(8,128)(2,1)S(1)} %attend.3.refs_1_, bf16[256,512]{1,0:T(8,128)(2,1)S(1)} %collective-permute-done.12.refs_2_, bf16[256,512]{1,0:T(8,128)(2,1)S(1)} %collective-permute-done.15.refs_3_, ...), custom_call_target="tpu_custom_call" | custom-call | flops 2684354560 | bytes 12058624 | tf_op jit(solution)/shard_map/output/pallas_call | solution.py:197
  146.4 0.7 collective-permute-done.25.refs_4_
  147.1 5.8 %output.3 = bf16[512,1024]{1,0:T(8,128)(2,1)} custom-call(s32[3,4]{1,0:T(4,128)S(1)} %pad_add_fusion.index_ref, bf16[256,512]{1,0:T(8,128)(2,1)S(1)} %collective-permute-done.14.refs_0_, bf16[256,512]{1,0:T(8,128)(2,1)S(1)} %collective-permute-done.17.refs_1_, bf16[256,512]{1,0:T(8,128)(2,1)} %collective-permute-done.20.refs_2_, ...), custom_call_target="tpu_custom_call" | custom-call | flops 1610612736 | bytes 8912896 | tf_op jit(solution)/shard_map/output/pallas_call | solution.py:197
  (53 shorter events, 1.6 us)
Async XLA Ops:
  6.5 8.5 %collective-permute-start.2 = (bf16[256,512]{1,0:T(8,128)(2,1)}, bf16[256,512]{1,0:T(8,128)(2,1)S(1)}, u32[]{:S(2)}, u32[]{:S(2)}) collective-permute-start(bf16[256,512]{1,0:T(8,128)(2,1)} %refs_0_.4), channel_id=1, source_target_pairs={{0,32},{8,136},{16,48},{24,152},{32,0},{40,168},{48,16},{56,184},{... | collective-permute-start | bytes 786440 | tf_op jit(solution)/shard_map/ppermute | solution.py:303
  7.9 9.1 %collective-permute-start = (bf16[256,512]{1,0:T(8,128)(2,1)}, bf16[256,512]{1,0:T(8,128)(2,1)S(1)}, u32[]{:S(2)}, u32[]{:S(2)}) collective-permute-start(bf16[256,512]{1,0:T(8,128)(2,1)} %refs_0_.4), channel_id=1, source_target_pairs={{0,16},{8,72},{16,32},{24,88},{32,48},{40,104},{48,0},{56,120},{64... | collective-permute-start | bytes 786440 | tf_op jit(solution)/shard_map/ppermute | solution.py:301
  10.0 7.8 %collective-permute-start.1 = (bf16[256,512]{1,0:T(8,128)(2,1)}, bf16[256,512]{1,0:T(8,128)(2,1)S(1)}, u32[]{:S(2)}, u32[]{:S(2)}) collective-permute-start(bf16[256,512]{1,0:T(8,128)(2,1)} %refs_0_.4), channel_id=1, source_target_pairs={{0,48},{8,200},{16,0},{24,216},{32,16},{40,232},{48,32},{56,248},{... | collective-permute-start | bytes 786440 | tf_op jit(solution)/shard_map/ppermute | solution.py:302
  10.0 1.0 copy-start.1
  11.1 1.0 copy-start.2
  17.8 1.0 copy-start.3
  18.9 16.1 %collective-permute-start.3 = (bf16[1024,512]{1,0:T(8,128)(2,1)S(1)}, bf16[1024,512]{1,0:T(8,128)(2,1)S(1)}, u32[]{:S(2)}, u32[]{:S(2)}) collective-permute-start(bf16[1024,512]{1,0:T(8,128)(2,1)S(1)} %side_by_side.1.refs_2_), channel_id=1, source_target_pairs={{0,64},{8,24},{16,80},{24,40},{32,96},{40,56},{48,112},{56,8},{64,... | collective-permute-start | bytes 3145736 | tf_op jit(solution)/shard_map/ppermute | solution.py:307
  20.6 14.9 %collective-permute-start.4 = (bf16[1024,512]{1,0:T(8,128)(2,1)S(1)}, bf16[1024,512]{1,0:T(8,128)(2,1)}, u32[]{:S(2)}, u32[]{:S(2)}) collective-permute-start(bf16[1024,512]{1,0:T(8,128)(2,1)S(1)} %side_by_side.1.refs_2_), channel_id=1, source_target_pairs={{0,192},{8,56},{16,208},{24,8},{32,224},{40,24},{48,240},{56,40},{... | collective-permute-start | bytes 3145736 | tf_op jit(solution)/shard_map/ppermute | solution.py:308
  22.2 40.4 %all-to-all-start = ((bf16[8,2,256,128]{3,2,1,0:T(8,128)(2,1)}), bf16[8,2,256,128]{3,2,1,0:T(8,128)(2,1)S(1)}, u32[]{:S(2)}, u32[]{:S(2)}) async-start(bf16[8,2,256,128]{3,2,1,0:T(8,128)(2,1)} %split_heads.1), calls=%async_computation | async-start | bytes 2097152 | tf_op jit(solution)/shard_map/all_to_all | solution.py:305
  30.7 106.3 %all-gather.3.cloned.1.call-start = ((), (), s32[]{:S(2)}) async-start(), calls=%async_computation.1 | async-start | bytes 8650752 | tf_op jit(solution)/shard_map/all_gather | solution.py:346
  30.7 10.8 %collective-permute-start.5 = (bf16[1024,512]{1,0:T(8,128)(2,1)S(1)}, bf16[1024,512]{1,0:T(8,128)(2,1)}, u32[]{:S(2)}, u32[]{:S(2)}) collective-permute-start(bf16[1024,512]{1,0:T(8,128)(2,1)S(1)} %side_by_side.1.refs_2_), channel_id=1, source_target_pairs={{0,8},{8,0},{16,24},{24,16},{32,40},{40,32},{48,56},{56,48},{64,72... | collective-permute-start | bytes 3145736 | tf_op jit(solution)/shard_map/ppermute | solution.py:38
  35.0 18.9 %collective-permute-start.8 = (bf16[1024,512]{1,0:T(8,128)(2,1)S(1)}, bf16[1024,512]{1,0:T(8,128)(2,1)}, u32[]{:S(2)}, u32[]{:S(2)}) collective-permute-start(bf16[1024,512]{1,0:T(8,128)(2,1)S(1)} %collective-permute-done.3.refs_4_), channel_id=1, source_target_pairs={{0,8},{8,0},{16,24},{24,16},{32,40},{40,32},{48,56},{56,48},{64,72... | collective-permute-start | bytes 3145736 | tf_op jit(solution)/shard_map/ppermute | solution.py:38
  35.5 18.5 %collective-permute-start.9 = (bf16[1024,512]{1,0:T(8,128)(2,1)}, bf16[1024,512]{1,0:T(8,128)(2,1)}, u32[]{:S(2)}, u32[]{:S(2)}) collective-permute-start(bf16[1024,512]{1,0:T(8,128)(2,1)} %collective-permute-done.4.refs_5_), channel_id=1, source_target_pairs={{0,8},{8,0},{16,24},{24,16},{32,40},{40,32},{48,56},{56,48},{64,72... | collective-permute-start | bytes 3145736 | tf_op jit(solution)/shard_map/ppermute | solution.py:38
  35.5 36.7 %collective-permute-start.24 = (bf16[512,256]{1,0:T(8,128)(2,1)}, bf16[512,256]{1,0:T(8,128)(2,1)S(1)}, u32[]{:S(2)}, u32[]{:S(2)}) collective-permute-start(bf16[512,256]{1,0:T(8,128)(2,1)} %param.8), channel_id=1, source_target_pairs={{0,0},{1,48},{2,64},{3,112},{4,128},{5,176},{6,192},{7,240},{8,8},... | collective-permute-start | bytes 786440 | tf_op jit(solution)/shard_map/ppermute | solution.py:343
  46.0 1.0 copy-start
  47.0 15.6 %collective-permute-start.6 = (bf16[512,512]{1,0:T(8,128)(2,1)S(1)}, bf16[512,512]{1,0:T(8,128)(2,1)}, u32[]{:S(2)}, u32[]{:S(2)}) collective-permute-start(bf16[512,512]{1,0:T(8,128)(2,1)S(1)} %slice.8), channel_id=1, source_target_pairs={{0,64},{8,24},{16,80},{24,40},{32,96},{40,56},{48,112},{56,8},{64,... | collective-permute-start | bytes 1572872 | tf_op jit(solution)/shard_map/ppermute | solution.py:311
  51.2 11.4 %collective-permute-start.7 = (bf16[512,512]{1,0:T(8,128)(2,1)S(1)}, bf16[512,512]{1,0:T(8,128)(2,1)}, u32[]{:S(2)}, u32[]{:S(2)}) collective-permute-start(bf16[512,512]{1,0:T(8,128)(2,1)S(1)} %slice.9), channel_id=1, source_target_pairs={{0,192},{8,56},{16,208},{24,8},{32,224},{40,24},{48,240},{56,40},{... | collective-permute-start | bytes 1572872 | tf_op jit(solution)/shard_map/ppermute | solution.py:312
  72.2 0.7 copy-start.5
  73.4 2.2 %collective-permute-start.10 = (bf16[512,512]{1,0:T(8,128)(2,1)}, bf16[512,512]{1,0:T(8,128)(2,1)S(1)}, u32[]{:S(2)}, u32[]{:S(2)}) collective-permute-start(bf16[512,512]{1,0:T(8,128)(2,1)} %collective-permute-done.6.refs_4_), channel_id=1, source_target_pairs={{0,8},{8,0},{16,24},{24,16},{32,40},{40,32},{48,56},{56,48},{64,72... | collective-permute-start | bytes 1572872 | tf_op jit(solution)/shard_map/ppermute | solution.py:38
  73.8 2.5 %collective-permute-start.11 = (bf16[512,512]{1,0:T(8,128)(2,1)}, bf16[512,512]{1,0:T(8,128)(2,1)S(1)}, u32[]{:S(2)}, u32[]{:S(2)}) collective-permute-start(bf16[512,512]{1,0:T(8,128)(2,1)} %collective-permute-done.7.refs_5_), channel_id=1, source_target_pairs={{0,8},{8,0},{16,24},{24,16},{32,40},{40,32},{48,56},{56,48},{64,72... | collective-permute-start | bytes 1572872 | tf_op jit(solution)/shard_map/ppermute | solution.py:38
  75.3 4.7 %copy-start.4 = (s32[1,4,8]{2,1,0:T(4,128)S(1)}, s32[1,4,8]{2,1,0:T(4,128)}, u32[]{:S(2)}) copy-start(s32[1,4,8]{2,1,0:T(4,128)} %param.11) | copy-start | bytes 388
  83.0 10.0 %collective-permute-start.21 = (bf16[256,512]{1,0:T(8,128)(2,1)S(1)}, bf16[256,512]{1,0:T(8,128)(2,1)S(1)}, u32[]{:S(2)}, u32[]{:S(2)}) collective-permute-start(bf16[256,512]{1,0:T(8,128)(2,1)S(1)} %attend.3.refs_1_), channel_id=1, source_target_pairs={{0,7},{1,0},{2,1},{3,2},{4,3},{5,4},{6,5},{7,6},{8,15},{9,8},{10,9... | collective-permute-start | bytes 786440 | tf_op jit(solution)/shard_map/ppermute | solution.py:363
  89.4 10.5 %collective-permute-start.12 = (bf16[256,512]{1,0:T(8,128)(2,1)S(1)}, bf16[256,512]{1,0:T(8,128)(2,1)S(1)}, u32[]{:S(2)}, u32[]{:S(2)}) collective-permute-start(bf16[256,512]{1,0:T(8,128)(2,1)S(1)} %attend.2.refs_0_), channel_id=1, source_target_pairs={{0,1},{1,2},{2,3},{3,4},{4,5},{5,6},{6,7},{7,0},{8,9},{9,10},{10,1... | collective-permute-start | bytes 786440 | tf_op jit(solution)/shard_map/ppermute | solution.py:362
  89.6 15.8 %collective-permute-start.15 = (bf16[256,512]{1,0:T(8,128)(2,1)S(1)}, bf16[256,512]{1,0:T(8,128)(2,1)S(1)}, u32[]{:S(2)}, u32[]{:S(2)}) collective-permute-start(bf16[256,512]{1,0:T(8,128)(2,1)S(1)} %attend.3.refs_1_), channel_id=1, source_target_pairs={{0,1},{1,2},{2,3},{3,4},{4,5},{5,6},{6,7},{7,0},{8,9},{9,10},{10,1... | collective-permute-start | bytes 786440 | tf_op jit(solution)/shard_map/ppermute | solution.py:362
  90.6 14.9 %collective-permute-start.18 = (bf16[256,512]{1,0:T(8,128)(2,1)S(1)}, bf16[256,512]{1,0:T(8,128)(2,1)S(1)}, u32[]{:S(2)}, u32[]{:S(2)}) collective-permute-start(bf16[256,512]{1,0:T(8,128)(2,1)S(1)} %attend.2.refs_0_), channel_id=1, source_target_pairs={{0,7},{1,0},{2,1},{3,2},{4,3},{5,4},{6,5},{7,6},{8,15},{9,8},{10,9... | collective-permute-start | bytes 786440 | tf_op jit(solution)/shard_map/ppermute | solution.py:363
  92.9 15.8 %collective-permute-start.22 = (bf16[256,512]{1,0:T(8,128)(2,1)S(1)}, bf16[256,512]{1,0:T(8,128)(2,1)S(1)}, u32[]{:S(2)}, u32[]{:S(2)}) collective-permute-start(bf16[256,512]{1,0:T(8,128)(2,1)S(1)} %collective-permute-done.21.refs_5_), channel_id=1, source_target_pairs={{0,7},{1,0},{2,1},{3,2},{4,3},{5,4},{6,5},{7,6},{8,15},{9,8},{10,9... | collective-permute-start | bytes 786440 | tf_op jit(solution)/shard_map/ppermute | solution.py:363
  99.8 11.2 %collective-permute-start.13 = (bf16[256,512]{1,0:T(8,128)(2,1)S(1)}, bf16[256,512]{1,0:T(8,128)(2,1)S(1)}, u32[]{:S(2)}, u32[]{:S(2)}) collective-permute-start(bf16[256,512]{1,0:T(8,128)(2,1)S(1)} %collective-permute-done.12.refs_2_), channel_id=1, source_target_pairs={{0,1},{1,2},{2,3},{3,4},{4,5},{5,6},{6,7},{7,0},{8,9},{9,10},{10,1... | collective-permute-start | bytes 786440 | tf_op jit(solution)/shard_map/ppermute | solution.py:362
  105.5 11.2 %collective-permute-start.16 = (bf16[256,512]{1,0:T(8,128)(2,1)S(1)}, bf16[256,512]{1,0:T(8,128)(2,1)S(1)}, u32[]{:S(2)}, u32[]{:S(2)}) collective-permute-start(bf16[256,512]{1,0:T(8,128)(2,1)S(1)} %collective-permute-done.15.refs_3_), channel_id=1, source_target_pairs={{0,1},{1,2},{2,3},{3,4},{4,5},{5,6},{6,7},{7,0},{8,9},{9,10},{10,1... | collective-permute-start | bytes 786440 | tf_op jit(solution)/shard_map/ppermute | solution.py:362
  105.5 11.2 %collective-permute-start.19 = (bf16[256,512]{1,0:T(8,128)(2,1)S(1)}, bf16[256,512]{1,0:T(8,128)(2,1)S(1)}, u32[]{:S(2)}, u32[]{:S(2)}) collective-permute-start(bf16[256,512]{1,0:T(8,128)(2,1)S(1)} %collective-permute-done.18.refs_4_), channel_id=1, source_target_pairs={{0,7},{1,0},{2,1},{3,2},{4,3},{5,4},{6,5},{7,6},{8,15},{9,8},{10,9... | collective-permute-start | bytes 786440 | tf_op jit(solution)/shard_map/ppermute | solution.py:363
  108.7 11.2 %collective-permute-start.23 = (bf16[256,512]{1,0:T(8,128)(2,1)S(1)}, bf16[256,512]{1,0:T(8,128)(2,1)S(1)}, u32[]{:S(2)}, u32[]{:S(2)}) collective-permute-start(bf16[256,512]{1,0:T(8,128)(2,1)S(1)} %collective-permute-done.22.refs_9_), channel_id=1, source_target_pairs={{0,7},{1,0},{2,1},{3,2},{4,3},{5,4},{6,5},{7,6},{8,15},{9,8},{10,9... | collective-permute-start | bytes 786440 | tf_op jit(solution)/shard_map/ppermute | solution.py:363
  111.1 11.2 %collective-permute-start.14 = (bf16[256,512]{1,0:T(8,128)(2,1)S(1)}, bf16[256,512]{1,0:T(8,128)(2,1)S(1)}, u32[]{:S(2)}, u32[]{:S(2)}) collective-permute-start(bf16[256,512]{1,0:T(8,128)(2,1)S(1)} %collective-permute-done.13.refs_6_), channel_id=1, source_target_pairs={{0,1},{1,2},{2,3},{3,4},{4,5},{5,6},{6,7},{7,0},{8,9},{9,10},{10,1... | collective-permute-start | bytes 786440 | tf_op jit(solution)/shard_map/ppermute | solution.py:362
  116.7 29.7 %collective-permute-start.17 = (bf16[256,512]{1,0:T(8,128)(2,1)S(1)}, bf16[256,512]{1,0:T(8,128)(2,1)S(1)}, u32[]{:S(2)}, u32[]{:S(2)}) collective-permute-start(bf16[256,512]{1,0:T(8,128)(2,1)S(1)} %collective-permute-done.16.refs_7_), channel_id=1, source_target_pairs={{0,1},{1,2},{2,3},{3,4},{4,5},{5,6},{6,7},{7,0},{8,9},{9,10},{10,1... | collective-permute-start | bytes 786440 | tf_op jit(solution)/shard_map/ppermute | solution.py:362
  116.7 29.7 %collective-permute-start.20 = (bf16[256,512]{1,0:T(8,128)(2,1)S(1)}, bf16[256,512]{1,0:T(8,128)(2,1)}, u32[]{:S(2)}, u32[]{:S(2)}) collective-permute-start(bf16[256,512]{1,0:T(8,128)(2,1)S(1)} %collective-permute-done.19.refs_8_), channel_id=1, source_target_pairs={{0,7},{1,0},{2,1},{3,2},{4,3},{5,4},{6,5},{7,6},{8,15},{9,8},{10,9... | collective-permute-start | bytes 786440 | tf_op jit(solution)/shard_map/ppermute | solution.py:363
  137.0 10.1 %collective-permute-start.25 = (bf16[256,512]{1,0:T(8,128)(2,1)S(1)}, bf16[256,512]{1,0:T(8,128)(2,1)}, u32[]{:S(2)}, u32[]{:S(2)}) collective-permute-start(bf16[256,512]{1,0:T(8,128)(2,1)S(1)} %collective-permute-done.14.refs_0_), channel_id=1, source_target_pairs={{0,1},{1,2},{2,3},{3,4},{4,5},{5,6},{6,7},{7,0},{8,9},{9,10},{10,1... | collective-permute-start | bytes 786440 | tf_op jit(solution)/shard_map/ppermute | solution.py:365
  138.5 8.6 %collective-permute-start.26 = (bf16[256,512]{1,0:T(8,128)(2,1)S(1)}, bf16[256,512]{1,0:T(8,128)(2,1)}, u32[]{:S(2)}, u32[]{:S(2)}) collective-permute-start(bf16[256,512]{1,0:T(8,128)(2,1)S(1)} %collective-permute-done.23.refs_3_), channel_id=1, source_target_pairs={{0,7},{1,0},{2,1},{3,2},{4,3},{5,4},{6,5},{7,6},{8,15},{9,8},{10,9... | collective-permute-start | bytes 786440 | tf_op jit(solution)/shard_map/ppermute | solution.py:365
Sparse Core Ops, SparseCore 0:
  73.0 63.8 all-gather.2

commit v3 on v2

--- a/solution.py
+++ b/solution.py
@@ -287,22 +287,26 @@
 
 def wo_moves(fsdp_count, ctx_count):
     parts = fsdp_count // ctx_count
-    moves = []
+    within, across = [], []
     for f in range(fsdp_count):
         for c in range(ctx_count):
             core, x, y = f % 2, f // 2 % SIDE, f // 2 // SIDE
             x_to = x if c % 2 == 0 else x + (-1 if x % 2 == 0 else 1)
-            moves.append((f * ctx_count + c, fsdp_index(y + c // 2, x_to, core) * ctx_count + f // parts))
-    return moves
-
-
-def project_all(tokens, wq, by_head):
+            target = fsdp_index(y + c // 2, x_to, core) * ctx_count
+            within.append((f * ctx_count + c, target + c))
+            across.append((target + c, target + f // parts))
+    return within, across
+
+
+def project_all(tokens, wq, by_head, wo_near, wo_across, turns):
     own_line, near, far_away = wq_indices()
     minus = lax.ppermute(wq, "fsdp", ring_pairs(0, 1))
     plus = lax.ppermute(wq, "fsdp", ring_pairs(0, -1))
     far = lax.ppermute(wq, "fsdp", ring_pairs(0, 2))
-    line = side_by_side([wq, minus, plus, after(far, by_head)])
-    kv = lax.all_to_all(after(by_head, line), "ctx", 0, 0, tiled=True)
+    far, _, wo_near, turns = lax.optimization_barrier((far, by_head, wo_near, turns))
+    line = side_by_side([wq, minus, plus, far])
+    wo_here = lax.ppermute(wo_near, ("fsdp", "ctx"), wo_across)
+    kv = lax.all_to_all(after(by_head, wo_here), "ctx", 0, 0, tiled=True)
     half = line.shape[0] // 2
     line_minus = lax.ppermute(line, "fsdp", ring_pairs(1, 1))
     line_plus = lax.ppermute(line, "fsdp", ring_pairs(1, -1))
@@ -313,9 +317,9 @@
     second = project(
         tokens, [line_minus, line_plus, swap_cores(line_minus), swap_cores(line_plus)], near, waited
     )
-    far_top, far_low, second, kv = lax.optimization_barrier((far_top, far_low, second, kv))
+    far_top, far_low, second = lax.optimization_barrier((far_top, far_low, second))
     third = project(tokens, [far_top, far_low, swap_cores(far_top), swap_cores(far_low)], far_away, second)
-    return third, kv, second
+    return third, turns, kv, after(wo_here, first, line_minus, line_plus)
 
 
 def wq_indices():
@@ -340,12 +344,13 @@
     held = key_cache.shape[0]
 
     parts = fsdp_count // ctx_count
-    wo_here = lax.ppermute(wo, ("fsdp", "ctx"), wo_moves(fsdp_count, ctx_count))
+    within, across = wo_moves(fsdp_count, ctx_count)
+    wo_near = lax.ppermute(wo, ("fsdp", "ctx"), within)
     by_head = split_heads(key_cache, value_cache)
-    projected, kv, begun = project_all(tokens, wq, by_head)
-    weights = lax.all_gather(after(wo_here, begun), "fsdp", axis=0, tiled=False)
-
-    cos, sin = tables(rows, held * ctx_count - rows)
+    turns = tables(rows, held * ctx_count - rows)
+    projected, (cos, sin), kv, wo_here = project_all(tokens, wq, by_head, wo_near, across, turns)
+    weights = lax.all_gather(wo_here, "fsdp", axis=0, tiled=False)
+
     blocks = rows // BLOCK // 2
     contexts = [attend(projected, cos, sin, kv, key_blocks[0], n * blocks, blocks) for n in range(2)]
 
@@ -361,11 +366,9 @@
     for _ in range(3):
         down.append([lax.ppermute(c, "ctx", right) for c in down[-1]])
         up.append([lax.ppermute(c, "ctx", left) for c in up[-1]])
-    weights, last_down, last_up = lax.optimization_barrier((weights, down[3][0], up[3][1]))
-    far = [lax.ppermute(last_down, "ctx", right), lax.ppermute(last_up, "ctx", left)]
-
-    total = output([contexts, down[1], up[1], down[2], up[2]], weights, owner(0, -1, 1, -2, 2))
-    return output([down[3], up[3], far], weights, owner(-3, 3, 4), total, BF16)
+    far = [lax.ppermute(down[3][0], "ctx", right), lax.ppermute(up[3][1], "ctx", left)]
+    near = [contexts, down[1], up[1], down[2], up[2], down[3], up[3]]
+    return output(near + [far], weights, owner(0, -1, 1, -2, 2, -3, 3, 4), None, BF16)
 
 
 def solution(mesh):

time: 161 us -> 149 us (0.925)
  waiting for transfers between devices: 54.3 us -> 30.3 us
  starting transfers between devices: 46.3 us -> 57.2 us
  local copies, waits for them, and re-layouts: 5.84 us -> 11.1 us
  Pallas kernels: 35.6 us -> 32.2 us
    ppermute x6, waiting for transfers between devices: 18.9 us -> 0.1 us  [body(): down.append([lax.ppermute(c, 'ctx', right) for c in down[-1]])]
    all_gather x1, waiting for transfers between devices: 14.7 us -> 0.01 us  [body(): weights = lax.all_gather(wo_here, 'fsdp', axis=0, tiled=False)]
    ppermute x6, waiting for transfers between devices: 0.02 us -> 11.5 us  [body(): up.append([lax.ppermute(c, 'ctx', left) for c in up[-1]])]
    ppermute x3 -> x4, starting transfers between devices: 7.13 us -> 13.1 us  [the longest x1 7.81 us: project_all(): wo_here = lax.ppermute(wo_near, ('fsdp', 'ctx'), wo_across)]
    ppermute x6, starting transfers between devices: 15.2 us -> 20.9 us  [body(): up.append([lax.ppermute(c, 'ctx', left) for c in up[-1]])]
    unnamed x12 -> x26, local copies, waits for them, and re-layouts: 4.71 us -> 9.96 us
    all_to_all x1, waiting for transfers between devices: 0.01 us -> 4.93 us  [project_all(): kv = lax.all_to_all(after(by_head, wo_here), 'ctx', 0, 0, tiled=True)]
    ppermute x1, starting transfers between devices: 4.24 us -> 0.08 us  [project_all(): far_top = lax.ppermute(top, 'fsdp', ring_pairs(1, 1))]
  transfers between devices with their start and end apart: 29 -> 30, of which waited for: 15 -> 14; matrix products, arithmetic and copies ran while one was open for 2% -> 3% of each run, Pallas kernels for 19% -> 16%
where the time goes in v3:
time: 149 us; the launch traced here: 148 us
  starting transfers between devices  57.2 us (38%)
  Pallas kernels  32.2 us (22%)
  waiting for transfers between devices  30.3 us (20%)
  between operations  14.5 us (10%)
  local copies, waits for them, and re-layouts  11.1 us (7%)
  other arithmetic  2.66 us (2%)
    ppermute x6, starting transfers between devices, body(): up.append([lax.ppermute(c, 'ctx', left) for c in up[-1]])  20.9 us
    pallas_call x3, Pallas kernels, project(): pl.pallas_call(functools.partial(project_kernel, terms, before is not Non...  14.3 us
    ppermute x6, waiting for transfers between devices, body(): up.append([lax.ppermute(c, 'ctx', left) for c in up[-1]])  11.5 us
    all_to_all x1, starting transfers between devices, project_all(): kv = lax.all_to_all(after(by_head, wo_here), 'ctx', 0, 0, tiled=True)  10.9 us
    unnamed x26, local copies, waits for them, and re-layouts  9.96 us
    pallas_call x1, Pallas kernels, output(): pl.pallas_call(functools.partial(output_kernel, terms, before is not None...  8.82 us
    ppermute x1, starting transfers between devices, project_all(): wo_here = lax.ppermute(wo_near, ('fsdp', 'ctx'), wo_across)  7.81 us
    pallas_call x2, Pallas kernels, attend(): pl.pallas_call(functools.partial(attend_kernel, heads, entries, first, ow...  6.05 us
  transfers between devices with their start and end apart: 30, of which 14 were waited for; matrix products, arithmetic and copies ran while one was open for 3% of the time, Pallas kernels for 16%

profile of v3, /device:TPU:6, one launch (start us, length us, event | category | flops | bytes accessed | tf_op | source)
XLA Modules:
  0.0 147.9 jit_solution(16641501449649991539)
XLA Ops:
  6.5 2.2 %collective-permute-start = (bf16[256,512]{1,0:T(8,128)(2,1)}, bf16[256,512]{1,0:T(8,128)(2,1)S(1)}, u32[]{:S(2)}, u32[]{:S(2)}) collective-permute-start(bf16[256,512]{1,0:T(8,128)(2,1)} %refs_0_.4), channel_id=1, source_target_pairs={{0,16},{8,72},{16,32},{24,88},{32,48},{40,104},{48,0},{56,120},{64... | collective-permute-start | bytes 786440 | tf_op jit(solution)/shard_map/ppermute | solution.py:303
  8.8 1.5 collective-permute-start.2
  10.2 1.6 %collective-permute-start.3 = (bf16[512,256]{1,0:T(8,128)(2,1)}, bf16[512,256]{1,0:T(8,128)(2,1)S(1)}, u32[]{:S(2)}, u32[]{:S(2)}) collective-permute-start(bf16[512,256]{1,0:T(8,128)(2,1)} %param.8), channel_id=1, source_target_pairs={{0,0},{1,49},{2,66},{3,115},{4,132},{5,181},{6,198},{7,247},{8,8},... | collective-permute-start | bytes 786440 | tf_op jit(solution)/shard_map/ppermute | solution.py:348
  11.8 1.0 copy-done.8
  12.9 1.0 copy-done.9
  13.9 2.9 %split_heads.1 = bf16[8,2,256,128]{3,2,1,0:T(8,128)(2,1)} custom-call(bf16[256,1024]{1,0:T(8,128)(2,1)S(1)} %copy-done.8, bf16[256,1024]{1,0:T(8,128)(2,1)S(1)} %copy-done.9), custom_call_target="tpu_custom_call" | custom-call | bytes 2097152 | tf_op jit(solution)/shard_map/split_heads/pallas_call | solution.py:266
  16.8 1.0 fusion.2
  17.8 0.9 pad_maximum_fusion
  18.8 0.6 collective-permute-done.1.refs_2_
  19.4 0.9 copy-done.10
  20.6 0.9 collective-permute-start.4
  21.5 2.4 %collective-permute-start.5 = (bf16[1024,512]{1,0:T(8,128)(2,1)S(1)}, bf16[1024,512]{1,0:T(8,128)(2,1)}, u32[]{:S(2)}, u32[]{:S(2)}) collective-permute-start(bf16[1024,512]{1,0:T(8,128)(2,1)S(1)} %side_by_side.1.refs_2_), channel_id=1, source_target_pairs={{0,192},{8,56},{16,208},{24,8},{32,224},{40,24},{48,240},{56,40},{... | collective-permute-start | bytes 3145736 | tf_op jit(solution)/shard_map/ppermute | solution.py:312
  23.9 7.8 %collective-permute-start.13 = (bf16[512,256]{1,0:T(8,128)(2,1)}, bf16[512,256]{1,0:T(8,128)(2,1)}, u32[]{:S(2)}, u32[]{:S(2)}) collective-permute-start(bf16[512,256]{1,0:T(8,128)(2,1)} %copy-done.12), channel_id=1, source_target_pairs={{0,0},{49,48},{66,64},{115,112},{132,128},{181,176},{198,192},{247... | collective-permute-start | bytes 786440 | tf_op jit(solution)/shard_map/ppermute | solution.py:308
  31.8 4.2 %project.3.refs_8_ = f32[512,512]{1,0:T(8,128)S(1)} custom-call(s32[2,4]{1,0:T(2,128)S(1)} %pad_add_fusion.2.index_ref, bf16[512,8192]{1,0:T(8,128)(2,1)} %refs_3_.3, bf16[512,8192]{1,0:T(8,128)(2,1)} %refs_3_.3, bf16[1024,512]{1,0:T(8,128)(2,1)S(1)} %side_by_side.1.refs_2_, bf16[1024,512]{1,0:T(8,128)(2,1)S(1)} %collective-permute-done.6.refs_3_), custom_call_target="tpu_custom_call" | custom-call | flops 1073741824 | bytes 6291456 | tf_op jit(solution)/shard_map/project/pallas_call | solution.py:88
  36.0 1.0 copy-done
  36.9 5.0 %collective-permute-done.13 = bf16[512,256]{1,0:T(8,128)(2,1)} collective-permute-done((bf16[512,256]{1,0:T(8,128)(2,1)}, bf16[512,256]{1,0:T(8,128)(2,1)}, u32[]{:S(2)}, u32[]{:S(2)}) %collective-permute-start.13) | collective-permute-done | bytes 262176 | tf_op jit(solution)/shard_map/ppermute | solution.py:308
  42.6 10.9 %all-to-all-start = ((bf16[8,2,256,128]{3,2,1,0:T(8,128)(2,1)}), bf16[8,2,256,128]{3,2,1,0:T(8,128)(2,1)S(1)}, u32[]{:S(2)}, u32[]{:S(2)}) async-start(bf16[8,2,256,128]{3,2,1,0:T(8,128)(2,1)} %split_heads.1), calls=%async_computation | async-start | bytes 2097152 | tf_op jit(solution)/shard_map/all_to_all | solution.py:309
  53.6 1.1 slice.9
  54.7 3.2 %collective-permute-start.8 = (bf16[512,512]{1,0:T(8,128)(2,1)S(1)}, bf16[512,512]{1,0:T(8,128)(2,1)}, u32[]{:S(2)}, u32[]{:S(2)}) collective-permute-start(bf16[512,512]{1,0:T(8,128)(2,1)S(1)} %slice.9), channel_id=1, source_target_pairs={{0,192},{8,56},{16,208},{24,8},{32,224},{40,24},{48,240},{56,40},{... | collective-permute-start | bytes 1572872 | tf_op jit(solution)/shard_map/ppermute | solution.py:316
  58.2 1.2 copy-done.3
  59.4 6.4 %project.4.refs_8_ = f32[512,512]{1,0:T(8,128)S(1)} custom-call(s32[4,4]{1,0:T(4,128)S(1)} %pad_add_fusion.1.index_ref, bf16[512,8192]{1,0:T(8,128)(2,1)} %refs_3_.3, bf16[512,8192]{1,0:T(8,128)(2,1)} %refs_3_.3, bf16[512,8192]{1,0:T(8,128)(2,1)} %refs_3_.3, bf16[512,8192]{1,0:T(8,128)(2,1)} %refs_3_.3, bf16[1024,512]{1,0:T(8,128)(2,1)S(1)} %copy-done.3, ...), custom_call_target="tpu_custom_call" | custom-call | flops 2147483648 | bytes 10485760 | tf_op jit(solution)/shard_map/project/pallas_call | solution.py:88
  65.8 2.2 %collective-permute-done.7.refs_4_ = bf16[512,512]{1,0:T(8,128)(2,1)} collective-permute-done((bf16[512,512]{1,0:T(8,128)(2,1)S(1)}, bf16[512,512]{1,0:T(8,128)(2,1)}, u32[]{:S(2)}, u32[]{:S(2)}) %collective-permute-start.7) | collective-permute-done | bytes 524320 | tf_op jit(solution)/shard_map/ppermute | solution.py:315
  68.8 1.4 collective-permute-done.11.refs_6_
  70.3 0.8 copy-done.4
  71.1 0.8 copy-done.6
  71.9 1.0 copy-done.5
  72.9 1.0 copy-done.7
  74.0 3.7 %project.5.q_ref = f32[512,512]{1,0:T(8,128)S(1)} custom-call(s32[4,2]{1,0:T(4,128)S(1)} %pad_add_fusion.index_ref, bf16[512,8192]{1,0:T(8,128)(2,1)} %refs_3_.3, bf16[512,8192]{1,0:T(8,128)(2,1)} %refs_3_.3, bf16[512,8192]{1,0:T(8,128)(2,1)} %refs_3_.3, bf16[512,8192]{1,0:T(8,128)(2,1)} %refs_3_.3, bf16[512,512]{1,0:T(8,128)(2,1)} %collective-permute-done.7.refs_4_, ...), custom_call_target="tpu_custom_call" | custom-call | flops 1073741824 | bytes 6291456 | tf_op jit(solution)/shard_map/project/pallas_call | solution.py:88
  77.7 4.9 %all-to-all-done.kv_ref = bf16[8,2,256,128]{3,2,1,0:T(8,128)(2,1)S(1)} async-done(((bf16[8,2,256,128]{3,2,1,0:T(8,128)(2,1)}), bf16[8,2,256,128]{3,2,1,0:T(8,128)(2,1)S(1)}, u32[]{:S(2)}, u32[]{:S(2)}) %all-to-all-start) | async-done | bytes 1048608 | tf_op jit(solution)/shard_map/all_to_all | solution.py:309
  82.6 1.0 copy-done.1
  83.6 3.0 %attend.2.refs_0_ = bf16[256,512]{1,0:T(8,128)(2,1)S(1)} custom-call(s32[4,8]{1,0:T(4,128)S(1)} %bitcast.102, f32[512,512]{1,0:T(8,128)S(1)} %project.5.q_ref, f32[512,128]{1,0:T(8,128)S(1)} %get-tuple-element.24.cos_ref, f32[512,128]{1,0:T(8,128)S(1)} %copy-done.1, bf16[8,2,256,128]{3,2,1,0:T(8,128)(2,1)S(1)} %all-to-all-done.kv_ref), custom_call_target="tpu_custom_call" | custom-call | flops 536870912 | bytes 1835008 | tf_op jit(solution)/shard_map/attend/pallas_call | solution.py:143
  87.2 3.0 %attend.3.refs_1_ = bf16[256,512]{1,0:T(8,128)(2,1)S(1)} custom-call(s32[4,8]{1,0:T(4,128)S(1)} %bitcast.103, f32[512,512]{1,0:T(8,128)S(1)} %project.5.q_ref, f32[512,128]{1,0:T(8,128)S(1)} %get-tuple-element.24.cos_ref, f32[512,128]{1,0:T(8,128)S(1)} %copy-done.1, bf16[8,2,256,128]{3,2,1,0:T(8,128)(2,1)S(1)} %all-to-all-done.kv_ref), custom_call_target="tpu_custom_call" | custom-call | flops 536870912 | bytes 1835008 | tf_op jit(solution)/shard_map/attend/pallas_call | solution.py:143
  90.2 2.9 %collective-permute-start.17 = (bf16[256,512]{1,0:T(8,128)(2,1)S(1)}, bf16[256,512]{1,0:T(8,128)(2,1)S(1)}, u32[]{:S(2)}, u32[]{:S(2)}) collective-permute-start(bf16[256,512]{1,0:T(8,128)(2,1)S(1)} %attend.3.refs_1_), channel_id=1, source_target_pairs={{0,7},{1,0},{2,1},{3,2},{4,3},{5,4},{6,5},{7,6},{8,15},{9,8},{10,9... | collective-permute-start | bytes 786440 | tf_op jit(solution)/shard_map/ppermute | solution.py:368
  93.1 3.2 %collective-permute-start.16 = (bf16[256,512]{1,0:T(8,128)(2,1)S(1)}, bf16[256,512]{1,0:T(8,128)(2,1)S(1)}, u32[]{:S(2)}, u32[]{:S(2)}) collective-permute-start(bf16[256,512]{1,0:T(8,128)(2,1)S(1)} %attend.2.refs_0_), channel_id=1, source_target_pairs={{0,7},{1,0},{2,1},{3,2},{4,3},{5,4},{6,5},{7,6},{8,15},{9,8},{10,9... | collective-permute-start | bytes 786440 | tf_op jit(solution)/shard_map/ppermute | solution.py:368
  96.3 3.5 %collective-permute-done.17.refs_5_ = bf16[256,512]{1,0:T(8,128)(2,1)S(1)} collective-permute-done((bf16[256,512]{1,0:T(8,128)(2,1)S(1)}, bf16[256,512]{1,0:T(8,128)(2,1)S(1)}, u32[]{:S(2)}, u32[]{:S(2)}) %collective-permute-start.17) | collective-permute-done | bytes 262176 | tf_op jit(solution)/shard_map/ppermute | solution.py:368
  99.8 3.7 %collective-permute-start.21 = (bf16[256,512]{1,0:T(8,128)(2,1)S(1)}, bf16[256,512]{1,0:T(8,128)(2,1)S(1)}, u32[]{:S(2)}, u32[]{:S(2)}) collective-permute-start(bf16[256,512]{1,0:T(8,128)(2,1)S(1)} %collective-permute-done.17.refs_5_), channel_id=1, source_target_pairs={{0,7},{1,0},{2,1},{3,2},{4,3},{5,4},{6,5},{7,6},{8,15},{9,8},{10,9... | collective-permute-start | bytes 786440 | tf_op jit(solution)/shard_map/ppermute | solution.py:368
  103.5 1.9 %collective-permute-done.16.refs_4_ = bf16[256,512]{1,0:T(8,128)(2,1)S(1)} collective-permute-done((bf16[256,512]{1,0:T(8,128)(2,1)S(1)}, bf16[256,512]{1,0:T(8,128)(2,1)S(1)}, u32[]{:S(2)}, u32[]{:S(2)}) %collective-permute-start.16) | collective-permute-done | bytes 262176 | tf_op jit(solution)/shard_map/ppermute | solution.py:368
  105.4 3.7 %collective-permute-start.20 = (bf16[256,512]{1,0:T(8,128)(2,1)S(1)}, bf16[256,512]{1,0:T(8,128)(2,1)S(1)}, u32[]{:S(2)}, u32[]{:S(2)}) collective-permute-start(bf16[256,512]{1,0:T(8,128)(2,1)S(1)} %collective-permute-done.16.refs_4_), channel_id=1, source_target_pairs={{0,7},{1,0},{2,1},{3,2},{4,3},{5,4},{6,5},{7,6},{8,15},{9,8},{10,9... | collective-permute-start | bytes 786440 | tf_op jit(solution)/shard_map/ppermute | solution.py:368
  109.1 1.9 %collective-permute-done.21.refs_9_ = bf16[256,512]{1,0:T(8,128)(2,1)S(1)} collective-permute-done((bf16[256,512]{1,0:T(8,128)(2,1)S(1)}, bf16[256,512]{1,0:T(8,128)(2,1)S(1)}, u32[]{:S(2)}, u32[]{:S(2)}) %collective-permute-start.21) | collective-permute-done | bytes 262176 | tf_op jit(solution)/shard_map/ppermute | solution.py:368
  111.0 3.7 %collective-permute-start.25 = (bf16[256,512]{1,0:T(8,128)(2,1)S(1)}, bf16[256,512]{1,0:T(8,128)(2,1)S(1)}, u32[]{:S(2)}, u32[]{:S(2)}) collective-permute-start(bf16[256,512]{1,0:T(8,128)(2,1)S(1)} %collective-permute-done.21.refs_9_), channel_id=1, source_target_pairs={{0,7},{1,0},{2,1},{3,2},{4,3},{5,4},{6,5},{7,6},{8,15},{9,8},{10,9... | collective-permute-start | bytes 786440 | tf_op jit(solution)/shard_map/ppermute | solution.py:368
  115.1 1.6 %collective-permute-done.20.refs_8_ = bf16[256,512]{1,0:T(8,128)(2,1)S(1)} collective-permute-done((bf16[256,512]{1,0:T(8,128)(2,1)S(1)}, bf16[256,512]{1,0:T(8,128)(2,1)S(1)}, u32[]{:S(2)}, u32[]{:S(2)}) %collective-permute-start.20) | collective-permute-done | bytes 262176 | tf_op jit(solution)/shard_map/ppermute | solution.py:368
  116.7 3.7 %collective-permute-start.24 = (bf16[256,512]{1,0:T(8,128)(2,1)S(1)}, bf16[256,512]{1,0:T(8,128)(2,1)}, u32[]{:S(2)}, u32[]{:S(2)}) collective-permute-start(bf16[256,512]{1,0:T(8,128)(2,1)S(1)} %collective-permute-done.20.refs_8_), channel_id=1, source_target_pairs={{0,7},{1,0},{2,1},{3,2},{4,3},{5,4},{6,5},{7,6},{8,15},{9,8},{10,9... | collective-permute-start | bytes 786440 | tf_op jit(solution)/shard_map/ppermute | solution.py:368
  120.4 1.9 %collective-permute-done.25.refs_13_ = bf16[256,512]{1,0:T(8,128)(2,1)S(1)} collective-permute-done((bf16[256,512]{1,0:T(8,128)(2,1)S(1)}, bf16[256,512]{1,0:T(8,128)(2,1)S(1)}, u32[]{:S(2)}, u32[]{:S(2)}) %collective-permute-start.25) | collective-permute-done | bytes 262176 | tf_op jit(solution)/shard_map/ppermute | solution.py:368
  122.3 3.7 %collective-permute-start.27 = (bf16[256,512]{1,0:T(8,128)(2,1)S(1)}, bf16[256,512]{1,0:T(8,128)(2,1)}, u32[]{:S(2)}, u32[]{:S(2)}) collective-permute-start(bf16[256,512]{1,0:T(8,128)(2,1)S(1)} %collective-permute-done.25.refs_13_), channel_id=1, source_target_pairs={{0,7},{1,0},{2,1},{3,2},{4,3},{5,4},{6,5},{7,6},{8,15},{9,8},{10,9... | collective-permute-start | bytes 786440 | tf_op jit(solution)/shard_map/ppermute | solution.py:369
  127.1 0.8 collective-permute-done.24.refs_12_
  127.9 2.2 %collective-permute-done.26.refs_14_ = bf16[256,512]{1,0:T(8,128)(2,1)} collective-permute-done((bf16[256,512]{1,0:T(8,128)(2,1)S(1)}, bf16[256,512]{1,0:T(8,128)(2,1)}, u32[]{:S(2)}, u32[]{:S(2)}) %collective-permute-start.26) | collective-permute-done | bytes 262176 | tf_op jit(solution)/shard_map/ppermute | solution.py:369
  130.1 2.1 %collective-permute-done.27.refs_15_ = bf16[256,512]{1,0:T(8,128)(2,1)} collective-permute-done((bf16[256,512]{1,0:T(8,128)(2,1)S(1)}, bf16[256,512]{1,0:T(8,128)(2,1)}, u32[]{:S(2)}, u32[]{:S(2)}) %collective-permute-start.27) | collective-permute-done | bytes 262176 | tf_op jit(solution)/shard_map/ppermute | solution.py:369
  132.2 8.8 %output.1 = bf16[512,1024]{1,0:T(8,128)(2,1)} custom-call(s32[8,4]{1,0:T(8,128)S(1)} %stack.360.index_ref, bf16[256,512]{1,0:T(8,128)(2,1)S(1)} %attend.2.refs_0_, bf16[256,512]{1,0:T(8,128)(2,1)S(1)} %attend.3.refs_1_, bf16[256,512]{1,0:T(8,128)(2,1)S(1)} %collective-permute-done.14.refs_2_, bf16[256,512]{1,0:T(8,128)(2,1)S(1)} %collective-permute-done.15.refs_3_, ...), custom_call_target="tpu_custom_call" | custom-call | flops 4294967296 | bytes 16777216 | tf_op jit(solution)/shard_map/output/pallas_call | solution.py:197
  (66 shorter events, 3.3 us)
Async XLA Ops:
  6.5 125.7 %all-gather.3.cloned.1.call-start = ((), (), s32[]{:S(2)}) async-start(), calls=%async_computation.1 | async-start | bytes 8650752 | tf_op jit(solution)/shard_map/all_gather | solution.py:352
  6.5 12.2 %collective-permute-start = (bf16[256,512]{1,0:T(8,128)(2,1)}, bf16[256,512]{1,0:T(8,128)(2,1)S(1)}, u32[]{:S(2)}, u32[]{:S(2)}) collective-permute-start(bf16[256,512]{1,0:T(8,128)(2,1)} %refs_0_.4), channel_id=1, source_target_pairs={{0,16},{8,72},{16,32},{24,88},{32,48},{40,104},{48,0},{56,120},{64... | collective-permute-start | bytes 786440 | tf_op jit(solution)/shard_map/ppermute | solution.py:303
  8.8 10.6 %collective-permute-start.1 = (bf16[256,512]{1,0:T(8,128)(2,1)}, bf16[256,512]{1,0:T(8,128)(2,1)S(1)}, u32[]{:S(2)}, u32[]{:S(2)}) collective-permute-start(bf16[256,512]{1,0:T(8,128)(2,1)} %refs_0_.4), channel_id=1, source_target_pairs={{0,48},{8,200},{16,0},{24,216},{32,16},{40,232},{48,32},{56,248},{... | collective-permute-start | bytes 786440 | tf_op jit(solution)/shard_map/ppermute | solution.py:304
  8.8 10.0 %collective-permute-start.2 = (bf16[256,512]{1,0:T(8,128)(2,1)}, bf16[256,512]{1,0:T(8,128)(2,1)S(1)}, u32[]{:S(2)}, u32[]{:S(2)}) collective-permute-start(bf16[256,512]{1,0:T(8,128)(2,1)} %refs_0_.4), channel_id=1, source_target_pairs={{0,32},{8,136},{16,48},{24,152},{32,0},{40,168},{48,16},{56,184},{... | collective-permute-start | bytes 786440 | tf_op jit(solution)/shard_map/ppermute | solution.py:305
  10.2 8.5 %collective-permute-start.3 = (bf16[512,256]{1,0:T(8,128)(2,1)}, bf16[512,256]{1,0:T(8,128)(2,1)S(1)}, u32[]{:S(2)}, u32[]{:S(2)}) collective-permute-start(bf16[512,256]{1,0:T(8,128)(2,1)} %param.8), channel_id=1, source_target_pairs={{0,0},{1,49},{2,66},{3,115},{4,132},{5,181},{6,198},{7,247},{8,8},... | collective-permute-start | bytes 786440 | tf_op jit(solution)/shard_map/ppermute | solution.py:348
  11.8 1.0 copy-start.8
  12.9 1.0 copy-start.9
  18.8 1.7 %copy-start.12 = (bf16[512,256]{1,0:T(8,128)(2,1)}, bf16[512,256]{1,0:T(8,128)(2,1)S(1)}, u32[]{:S(2)}) copy-start(bf16[512,256]{1,0:T(8,128)(2,1)S(1)} %collective-permute-done.3) | copy-start | bytes 786436
  19.4 1.0 copy-start.10
  20.4 11.3 %collective-permute-start.6 = (bf16[1024,512]{1,0:T(8,128)(2,1)S(1)}, bf16[1024,512]{1,0:T(8,128)(2,1)S(1)}, u32[]{:S(2)}, u32[]{:S(2)}) collective-permute-start(bf16[1024,512]{1,0:T(8,128)(2,1)S(1)} %side_by_side.1.refs_2_), channel_id=1, source_target_pairs={{0,8},{8,0},{16,24},{24,16},{32,40},{40,32},{48,56},{56,48},{64,72... | collective-permute-start | bytes 3145736 | tf_op jit(solution)/shard_map/ppermute | solution.py:38
  20.6 21.4 %collective-permute-start.4 = (bf16[1024,512]{1,0:T(8,128)(2,1)S(1)}, bf16[1024,512]{1,0:T(8,128)(2,1)S(1)}, u32[]{:S(2)}, u32[]{:S(2)}) collective-permute-start(bf16[1024,512]{1,0:T(8,128)(2,1)S(1)} %side_by_side.1.refs_2_), channel_id=1, source_target_pairs={{0,64},{8,24},{16,80},{24,40},{32,96},{40,56},{48,112},{56,8},{64,... | collective-permute-start | bytes 3145736 | tf_op jit(solution)/shard_map/ppermute | solution.py:311
  21.5 20.5 %collective-permute-start.5 = (bf16[1024,512]{1,0:T(8,128)(2,1)S(1)}, bf16[1024,512]{1,0:T(8,128)(2,1)}, u32[]{:S(2)}, u32[]{:S(2)}) collective-permute-start(bf16[1024,512]{1,0:T(8,128)(2,1)S(1)} %side_by_side.1.refs_2_), channel_id=1, source_target_pairs={{0,192},{8,56},{16,208},{24,8},{32,224},{40,24},{48,240},{56,40},{... | collective-permute-start | bytes 3145736 | tf_op jit(solution)/shard_map/ppermute | solution.py:312
  23.9 18.1 %collective-permute-start.13 = (bf16[512,256]{1,0:T(8,128)(2,1)}, bf16[512,256]{1,0:T(8,128)(2,1)}, u32[]{:S(2)}, u32[]{:S(2)}) collective-permute-start(bf16[512,256]{1,0:T(8,128)(2,1)} %copy-done.12), channel_id=1, source_target_pairs={{0,0},{49,48},{66,64},{115,112},{132,128},{181,176},{198,192},{247... | collective-permute-start | bytes 786440 | tf_op jit(solution)/shard_map/ppermute | solution.py:308
  36.0 1.0 copy-start
  42.0 16.2 %copy-start.2 = (bf16[1024,512]{1,0:T(8,128)(2,1)}, bf16[1024,512]{1,0:T(8,128)(2,1)S(1)}, u32[]{:S(2)}) copy-start(bf16[1024,512]{1,0:T(8,128)(2,1)S(1)} %collective-permute-done.4.refs_4_) | copy-start | bytes 3145732
  42.0 16.2 %collective-permute-start.9 = (bf16[1024,512]{1,0:T(8,128)(2,1)S(1)}, bf16[1024,512]{1,0:T(8,128)(2,1)S(1)}, u32[]{:S(2)}, u32[]{:S(2)}) collective-permute-start(bf16[1024,512]{1,0:T(8,128)(2,1)S(1)} %collective-permute-done.4.refs_4_), channel_id=1, source_target_pairs={{0,8},{8,0},{16,24},{24,16},{32,40},{40,32},{48,56},{56,48},{64,72... | collective-permute-start | bytes 3145736 | tf_op jit(solution)/shard_map/ppermute | solution.py:38
  42.1 16.1 %collective-permute-start.10 = (bf16[1024,512]{1,0:T(8,128)(2,1)}, bf16[1024,512]{1,0:T(8,128)(2,1)}, u32[]{:S(2)}, u32[]{:S(2)}) collective-permute-start(bf16[1024,512]{1,0:T(8,128)(2,1)} %collective-permute-done.5.refs_5_), channel_id=1, source_target_pairs={{0,8},{8,0},{16,24},{24,16},{32,40},{40,32},{48,56},{56,48},{64,72... | collective-permute-start | bytes 3145736 | tf_op jit(solution)/shard_map/ppermute | solution.py:38
  42.6 40.0 %all-to-all-start = ((bf16[8,2,256,128]{3,2,1,0:T(8,128)(2,1)}), bf16[8,2,256,128]{3,2,1,0:T(8,128)(2,1)S(1)}, u32[]{:S(2)}, u32[]{:S(2)}) async-start(bf16[8,2,256,128]{3,2,1,0:T(8,128)(2,1)} %split_heads.1), calls=%async_computation | async-start | bytes 2097152 | tf_op jit(solution)/shard_map/all_to_all | solution.py:309
  54.7 13.4 %collective-permute-start.7 = (bf16[512,512]{1,0:T(8,128)(2,1)S(1)}, bf16[512,512]{1,0:T(8,128)(2,1)}, u32[]{:S(2)}, u32[]{:S(2)}) collective-permute-start(bf16[512,512]{1,0:T(8,128)(2,1)S(1)} %slice.8), channel_id=1, source_target_pairs={{0,64},{8,24},{16,80},{24,40},{32,96},{40,56},{48,112},{56,8},{64,... | collective-permute-start | bytes 1572872 | tf_op jit(solution)/shard_map/ppermute | solution.py:315
  54.7 13.4 %collective-permute-start.8 = (bf16[512,512]{1,0:T(8,128)(2,1)S(1)}, bf16[512,512]{1,0:T(8,128)(2,1)}, u32[]{:S(2)}, u32[]{:S(2)}) collective-permute-start(bf16[512,512]{1,0:T(8,128)(2,1)S(1)} %slice.9), channel_id=1, source_target_pairs={{0,192},{8,56},{16,208},{24,8},{32,224},{40,24},{48,240},{56,40},{... | collective-permute-start | bytes 1572872 | tf_op jit(solution)/shard_map/ppermute | solution.py:316
  58.2 1.2 copy-start.3
  68.2 2.1 %collective-permute-start.11 = (bf16[512,512]{1,0:T(8,128)(2,1)}, bf16[512,512]{1,0:T(8,128)(2,1)S(1)}, u32[]{:S(2)}, u32[]{:S(2)}) collective-permute-start(bf16[512,512]{1,0:T(8,128)(2,1)} %collective-permute-done.7.refs_4_), channel_id=1, source_target_pairs={{0,8},{8,0},{16,24},{24,16},{32,40},{40,32},{48,56},{56,48},{64,72... | collective-permute-start | bytes 1572872 | tf_op jit(solution)/shard_map/ppermute | solution.py:38
  68.2 2.9 %collective-permute-start.12 = (bf16[512,512]{1,0:T(8,128)(2,1)}, bf16[512,512]{1,0:T(8,128)(2,1)S(1)}, u32[]{:S(2)}, u32[]{:S(2)}) collective-permute-start(bf16[512,512]{1,0:T(8,128)(2,1)} %collective-permute-done.8.refs_5_), channel_id=1, source_target_pairs={{0,8},{8,0},{16,24},{24,16},{32,40},{40,32},{48,56},{56,48},{64,72... | collective-permute-start | bytes 1572872 | tf_op jit(solution)/shard_map/ppermute | solution.py:38
  68.8 13.8 %copy-start.11 = (s32[1,4,8]{2,1,0:T(4,128)S(1)}, s32[1,4,8]{2,1,0:T(4,128)}, u32[]{:S(2)}) copy-start(s32[1,4,8]{2,1,0:T(4,128)} %param.11) | copy-start | bytes 388
  70.3 0.8 copy-start.4
  71.1 0.8 copy-start.6
  71.9 1.0 copy-start.5
  72.9 1.0 copy-start.7
  82.6 1.0 copy-start.1
  86.6 9.7 %collective-permute-start.14 = (bf16[256,512]{1,0:T(8,128)(2,1)S(1)}, bf16[256,512]{1,0:T(8,128)(2,1)S(1)}, u32[]{:S(2)}, u32[]{:S(2)}) collective-permute-start(bf16[256,512]{1,0:T(8,128)(2,1)S(1)} %attend.2.refs_0_), channel_id=1, source_target_pairs={{0,1},{1,2},{2,3},{3,4},{4,5},{5,6},{6,7},{7,0},{8,9},{9,10},{10,1... | collective-permute-start | bytes 786440 | tf_op jit(solution)/shard_map/ppermute | solution.py:367
  90.2 9.6 %collective-permute-start.17 = (bf16[256,512]{1,0:T(8,128)(2,1)S(1)}, bf16[256,512]{1,0:T(8,128)(2,1)S(1)}, u32[]{:S(2)}, u32[]{:S(2)}) collective-permute-start(bf16[256,512]{1,0:T(8,128)(2,1)S(1)} %attend.3.refs_1_), channel_id=1, source_target_pairs={{0,7},{1,0},{2,1},{3,2},{4,3},{5,4},{6,5},{7,6},{8,15},{9,8},{10,9... | collective-permute-start | bytes 786440 | tf_op jit(solution)/shard_map/ppermute | solution.py:368
  93.1 10.5 %collective-permute-start.15 = (bf16[256,512]{1,0:T(8,128)(2,1)S(1)}, bf16[256,512]{1,0:T(8,128)(2,1)S(1)}, u32[]{:S(2)}, u32[]{:S(2)}) collective-permute-start(bf16[256,512]{1,0:T(8,128)(2,1)S(1)} %attend.3.refs_1_), channel_id=1, source_target_pairs={{0,1},{1,2},{2,3},{3,4},{4,5},{5,6},{6,7},{7,0},{8,9},{9,10},{10,1... | collective-permute-start | bytes 786440 | tf_op jit(solution)/shard_map/ppermute | solution.py:367
  93.1 12.3 %collective-permute-start.16 = (bf16[256,512]{1,0:T(8,128)(2,1)S(1)}, bf16[256,512]{1,0:T(8,128)(2,1)S(1)}, u32[]{:S(2)}, u32[]{:S(2)}) collective-permute-start(bf16[256,512]{1,0:T(8,128)(2,1)S(1)} %attend.2.refs_0_), channel_id=1, source_target_pairs={{0,7},{1,0},{2,1},{3,2},{4,3},{5,4},{6,5},{7,6},{8,15},{9,8},{10,9... | collective-permute-start | bytes 786440 | tf_op jit(solution)/shard_map/ppermute | solution.py:368
  96.3 12.8 %collective-permute-start.18 = (bf16[256,512]{1,0:T(8,128)(2,1)S(1)}, bf16[256,512]{1,0:T(8,128)(2,1)S(1)}, u32[]{:S(2)}, u32[]{:S(2)}) collective-permute-start(bf16[256,512]{1,0:T(8,128)(2,1)S(1)} %collective-permute-done.14.refs_2_), channel_id=1, source_target_pairs={{0,1},{1,2},{2,3},{3,4},{4,5},{5,6},{6,7},{7,0},{8,9},{9,10},{10,1... | collective-permute-start | bytes 786440 | tf_op jit(solution)/shard_map/ppermute | solution.py:367
  99.8 11.2 %collective-permute-start.21 = (bf16[256,512]{1,0:T(8,128)(2,1)S(1)}, bf16[256,512]{1,0:T(8,128)(2,1)S(1)}, u32[]{:S(2)}, u32[]{:S(2)}) collective-permute-start(bf16[256,512]{1,0:T(8,128)(2,1)S(1)} %collective-permute-done.17.refs_5_), channel_id=1, source_target_pairs={{0,7},{1,0},{2,1},{3,2},{4,3},{5,4},{6,5},{7,6},{8,15},{9,8},{10,9... | collective-permute-start | bytes 786440 | tf_op jit(solution)/shard_map/ppermute | solution.py:368
  103.5 11.3 %collective-permute-start.19 = (bf16[256,512]{1,0:T(8,128)(2,1)S(1)}, bf16[256,512]{1,0:T(8,128)(2,1)S(1)}, u32[]{:S(2)}, u32[]{:S(2)}) collective-permute-start(bf16[256,512]{1,0:T(8,128)(2,1)S(1)} %collective-permute-done.15.refs_3_), channel_id=1, source_target_pairs={{0,1},{1,2},{2,3},{3,4},{4,5},{5,6},{6,7},{7,0},{8,9},{9,10},{10,1... | collective-permute-start | bytes 786440 | tf_op jit(solution)/shard_map/ppermute | solution.py:367
  105.4 11.2 %collective-permute-start.20 = (bf16[256,512]{1,0:T(8,128)(2,1)S(1)}, bf16[256,512]{1,0:T(8,128)(2,1)S(1)}, u32[]{:S(2)}, u32[]{:S(2)}) collective-permute-start(bf16[256,512]{1,0:T(8,128)(2,1)S(1)} %collective-permute-done.16.refs_4_), channel_id=1, source_target_pairs={{0,7},{1,0},{2,1},{3,2},{4,3},{5,4},{6,5},{7,6},{8,15},{9,8},{10,9... | collective-permute-start | bytes 786440 | tf_op jit(solution)/shard_map/ppermute | solution.py:368
  109.1 11.2 %collective-permute-start.22 = (bf16[256,512]{1,0:T(8,128)(2,1)S(1)}, bf16[256,512]{1,0:T(8,128)(2,1)S(1)}, u32[]{:S(2)}, u32[]{:S(2)}) collective-permute-start(bf16[256,512]{1,0:T(8,128)(2,1)S(1)} %collective-permute-done.18.refs_6_), channel_id=1, source_target_pairs={{0,1},{1,2},{2,3},{3,4},{4,5},{5,6},{6,7},{7,0},{8,9},{9,10},{10,1... | collective-permute-start | bytes 786440 | tf_op jit(solution)/shard_map/ppermute | solution.py:367
  111.0 11.2 %collective-permute-start.25 = (bf16[256,512]{1,0:T(8,128)(2,1)S(1)}, bf16[256,512]{1,0:T(8,128)(2,1)S(1)}, u32[]{:S(2)}, u32[]{:S(2)}) collective-permute-start(bf16[256,512]{1,0:T(8,128)(2,1)S(1)} %collective-permute-done.21.refs_9_), channel_id=1, source_target_pairs={{0,7},{1,0},{2,1},{3,2},{4,3},{5,4},{6,5},{7,6},{8,15},{9,8},{10,9... | collective-permute-start | bytes 786440 | tf_op jit(solution)/shard_map/ppermute | solution.py:368
  114.8 12.3 %collective-permute-start.23 = (bf16[256,512]{1,0:T(8,128)(2,1)S(1)}, bf16[256,512]{1,0:T(8,128)(2,1)S(1)}, u32[]{:S(2)}, u32[]{:S(2)}) collective-permute-start(bf16[256,512]{1,0:T(8,128)(2,1)S(1)} %collective-permute-done.19.refs_7_), channel_id=1, source_target_pairs={{0,1},{1,2},{2,3},{3,4},{4,5},{5,6},{6,7},{7,0},{8,9},{9,10},{10,1... | collective-permute-start | bytes 786440 | tf_op jit(solution)/shard_map/ppermute | solution.py:367
  116.7 11.2 %collective-permute-start.24 = (bf16[256,512]{1,0:T(8,128)(2,1)S(1)}, bf16[256,512]{1,0:T(8,128)(2,1)}, u32[]{:S(2)}, u32[]{:S(2)}) collective-permute-start(bf16[256,512]{1,0:T(8,128)(2,1)S(1)} %collective-permute-done.20.refs_8_), channel_id=1, source_target_pairs={{0,7},{1,0},{2,1},{3,2},{4,3},{5,4},{6,5},{7,6},{8,15},{9,8},{10,9... | collective-permute-start | bytes 786440 | tf_op jit(solution)/shard_map/ppermute | solution.py:368
  120.4 9.8 %collective-permute-start.26 = (bf16[256,512]{1,0:T(8,128)(2,1)S(1)}, bf16[256,512]{1,0:T(8,128)(2,1)}, u32[]{:S(2)}, u32[]{:S(2)}) collective-permute-start(bf16[256,512]{1,0:T(8,128)(2,1)S(1)} %collective-permute-done.22.refs_10_), channel_id=1, source_target_pairs={{0,1},{1,2},{2,3},{3,4},{4,5},{5,6},{6,7},{7,0},{8,9},{9,10},{10,1... | collective-permute-start | bytes 786440 | tf_op jit(solution)/shard_map/ppermute | solution.py:369
  122.3 10.0 %collective-permute-start.27 = (bf16[256,512]{1,0:T(8,128)(2,1)S(1)}, bf16[256,512]{1,0:T(8,128)(2,1)}, u32[]{:S(2)}, u32[]{:S(2)}) collective-permute-start(bf16[256,512]{1,0:T(8,128)(2,1)S(1)} %collective-permute-done.25.refs_13_), channel_id=1, source_target_pairs={{0,7},{1,0},{2,1},{3,2},{4,3},{5,4},{6,5},{7,6},{8,15},{9,8},{10,9... | collective-permute-start | bytes 786440 | tf_op jit(solution)/shard_map/ppermute | solution.py:369
Sparse Core Ops, SparseCore 0:
  42.1 62.4 all-gather.2

commit v4 on v3

--- a/solution.py
+++ b/solution.py
@@ -73,7 +73,7 @@
         out[...] = total[...]
 
 
-def project(tokens, pieces, index, before=None):
+def project(tokens, pieces, index, before=None, vmem=VMEM_LIMIT):
     rows = tokens.shape[0]
     terms = len(pieces)
     depth, cols = tokens.shape[1] // (2 * SIDE * SIDE), pieces[0].shape[1]
@@ -95,7 +95,7 @@
             scratch_shapes=[pltpu.VMEM((rows, cols), F32)],
         ),
         out_shape=jax.ShapeDtypeStruct((rows, cols), F32),
-        compiler_params=pltpu.CompilerParams(vmem_limit_bytes=VMEM_LIMIT),
+        compiler_params=pltpu.CompilerParams(vmem_limit_bytes=vmem),
         cost_estimate=pl.CostEstimate(
             flops=2 * rows * cols * depth * steps * terms,
             bytes_accessed=2 * (rows + cols) * depth * steps * terms + 8 * rows * cols,
@@ -318,7 +318,7 @@
         tokens, [line_minus, line_plus, swap_cores(line_minus), swap_cores(line_plus)], near, waited
     )
     far_top, far_low, second = lax.optimization_barrier((far_top, far_low, second))
-    third = project(tokens, [far_top, far_low, swap_cores(far_top), swap_cores(far_low)], far_away, second)
+    third = project(tokens, [far_top, far_low, swap_cores(far_top), swap_cores(far_low)], far_away, second, 60 * 2**20)
     return third, turns, kv, after(wo_here, first, line_minus, line_plus)
 
 
@@ -366,9 +366,10 @@
     for _ in range(3):
         down.append([lax.ppermute(c, "ctx", right) for c in down[-1]])
         up.append([lax.ppermute(c, "ctx", left) for c in up[-1]])
-    far = [lax.ppermute(down[3][0], "ctx", right), lax.ppermute(up[3][1], "ctx", left)]
-    near = [contexts, down[1], up[1], down[2], up[2], down[3], up[3]]
-    return output(near + [far], weights, owner(0, -1, 1, -2, 2, -3, 3, 4), None, BF16)
+    weights, last_down, last_up = lax.optimization_barrier((weights, down[3][0], up[3][1]))
+    far = [lax.ppermute(last_down, "ctx", right), lax.ppermute(last_up, "ctx", left)]
+    total = output([contexts, down[1], up[1], down[2], up[2]], weights, owner(0, -1, 1, -2, 2))
+    return output([down[3], up[3], far], weights, owner(-3, 3, 4), total, BF16)
 
 
 def solution(mesh):

time: 149 us -> 146 us (0.980)
  Pallas kernels: 32.2 us -> 37.4 us
  waiting for transfers between devices: 30.3 us -> 25.7 us
  local copies, waits for them, and re-layouts: 11.1 us -> 8.46 us
    ppermute x2, waiting for transfers between devices: 4.34 us -> 0.23 us  [the longest x1 0.23 us: body(): lax.ppermute(last_up, 'ctx', left)]
    pallas_call x1 -> x2, Pallas kernels: 8.82 us -> 11.8 us  [output(): pl.pallas_call(functools.partial(output_kernel, terms, before is not None...]
    unnamed x26 -> x20, local copies, waits for them, and re-layouts: 9.96 us -> 7.32 us
    pallas_call x3, Pallas kernels: 14.3 us -> 16.6 us  [project(): pl.pallas_call(functools.partial(project_kernel, terms, before is not Non...]
    ppermute x6, waiting for transfers between devices: 11.5 us -> 10 us  [body(): up.append([lax.ppermute(c, 'ctx', left) for c in up[-1]])]
  transfers between devices with their start and end apart: 30 -> 30, of which waited for: 14 -> 13; matrix products, arithmetic and copies ran while one was open for 3% -> 3% of each run, Pallas kernels for 16% -> 22%
where the time goes in v4:
time: 146 us; the launch traced here: 145 us
  starting transfers between devices  57 us (39%)
  Pallas kernels  37.4 us (26%)
  waiting for transfers between devices  25.7 us (18%)
  between operations  14.3 us (10%)
  local copies, waits for them, and re-layouts  8.46 us (6%)
  other arithmetic  2.63 us (2%)
    ppermute x6, starting transfers between devices, body(): up.append([lax.ppermute(c, 'ctx', left) for c in up[-1]])  20.7 us
    pallas_call x3, Pallas kernels, project(): pl.pallas_call(functools.partial(project_kernel, terms, before is not Non...  16.6 us
    pallas_call x2, Pallas kernels, output(): pl.pallas_call(functools.partial(output_kernel, terms, before is not None...  11.8 us
    all_to_all x1, starting transfers between devices, project_all(): kv = lax.all_to_all(after(by_head, wo_here), 'ctx', 0, 0, tiled=True)  10.9 us
    ppermute x6, waiting for transfers between devices, body(): up.append([lax.ppermute(c, 'ctx', left) for c in up[-1]])  10 us
    ppermute x1, starting transfers between devices, project_all(): wo_here = lax.ppermute(wo_near, ('fsdp', 'ctx'), wo_across)  7.7 us
    unnamed x20, local copies, waits for them, and re-layouts  7.32 us
    pallas_call x2, Pallas kernels, attend(): pl.pallas_call(functools.partial(attend_kernel, heads, entries, first, ow...  6.03 us
  transfers between devices with their start and end apart: 30, of which 13 were waited for; matrix products, arithmetic and copies ran while one was open for 3% of the time, Pallas kernels for 22%

profile of v4, /device:TPU:6, one launch (start us, length us, event | category | flops | bytes accessed | tf_op | source)
XLA Modules:
  0.0 145.4 jit_solution(1700594517763123364)
XLA Ops:
  6.5 2.2 %collective-permute-start = (bf16[256,512]{1,0:T(8,128)(2,1)}, bf16[256,512]{1,0:T(8,128)(2,1)S(1)}, u32[]{:S(2)}, u32[]{:S(2)}) collective-permute-start(bf16[256,512]{1,0:T(8,128)(2,1)} %refs_0_.4), channel_id=1, source_target_pairs={{0,16},{8,72},{16,32},{24,88},{32,48},{40,104},{48,0},{56,120},{64... | collective-permute-start | bytes 786440 | tf_op jit(solution)/shard_map/ppermute | solution.py:303
  8.8 1.5 %collective-permute-start.2 = (bf16[256,512]{1,0:T(8,128)(2,1)}, bf16[256,512]{1,0:T(8,128)(2,1)S(1)}, u32[]{:S(2)}, u32[]{:S(2)}) collective-permute-start(bf16[256,512]{1,0:T(8,128)(2,1)} %refs_0_.4), channel_id=1, source_target_pairs={{0,32},{8,136},{16,48},{24,152},{32,0},{40,168},{48,16},{56,184},{... | collective-permute-start | bytes 786440 | tf_op jit(solution)/shard_map/ppermute | solution.py:305
  10.2 1.6 %collective-permute-start.3 = (bf16[512,256]{1,0:T(8,128)(2,1)}, bf16[512,256]{1,0:T(8,128)(2,1)S(1)}, u32[]{:S(2)}, u32[]{:S(2)}) collective-permute-start(bf16[512,256]{1,0:T(8,128)(2,1)} %param.8), channel_id=1, source_target_pairs={{0,0},{1,49},{2,66},{3,115},{4,132},{5,181},{6,198},{7,247},{8,8},... | collective-permute-start | bytes 786440 | tf_op jit(solution)/shard_map/ppermute | solution.py:348
  11.8 1.0 copy-done.3
  12.9 1.0 copy-done.4
  13.9 2.9 %split_heads.1 = bf16[8,2,256,128]{3,2,1,0:T(8,128)(2,1)} custom-call(bf16[256,1024]{1,0:T(8,128)(2,1)S(1)} %copy-done.3, bf16[256,1024]{1,0:T(8,128)(2,1)S(1)} %copy-done.4), custom_call_target="tpu_custom_call" | custom-call | bytes 2097152 | tf_op jit(solution)/shard_map/split_heads/pallas_call | solution.py:266
  16.8 1.0 fusion.2
  18.1 1.3 collective-permute-done.1.refs_2_
  19.4 0.9 copy-done.5
  20.7 3.2 %collective-permute-start.5 = (bf16[1024,512]{1,0:T(8,128)(2,1)S(1)}, bf16[1024,512]{1,0:T(8,128)(2,1)}, u32[]{:S(2)}, u32[]{:S(2)}) collective-permute-start(bf16[1024,512]{1,0:T(8,128)(2,1)S(1)} %side_by_side.1.refs_2_), channel_id=1, source_target_pairs={{0,192},{8,56},{16,208},{24,8},{32,224},{40,24},{48,240},{56,40},{... | collective-permute-start | bytes 3145736 | tf_op jit(solution)/shard_map/ppermute | solution.py:312
  23.8 7.7 %collective-permute-start.13 = (bf16[512,256]{1,0:T(8,128)(2,1)S(1)}, bf16[512,256]{1,0:T(8,128)(2,1)S(1)}, u32[]{:S(2)}, u32[]{:S(2)}) collective-permute-start(bf16[512,256]{1,0:T(8,128)(2,1)S(1)} %collective-permute-done.3), channel_id=1, source_target_pairs={{0,0},{49,48},{66,64},{115,112},{132,128},{181,176},{198,192},{247... | collective-permute-start | bytes 786440 | tf_op jit(solution)/shard_map/ppermute | solution.py:308
  31.7 4.4 %project.3.refs_8_ = f32[512,512]{1,0:T(8,128)S(1)} custom-call(s32[2,4]{1,0:T(2,128)S(1)} %pad_add_fusion.3.index_ref, bf16[512,8192]{1,0:T(8,128)(2,1)} %refs_3_.3, bf16[512,8192]{1,0:T(8,128)(2,1)} %refs_3_.3, bf16[1024,512]{1,0:T(8,128)(2,1)S(1)} %side_by_side.1.refs_2_, bf16[1024,512]{1,0:T(8,128)(2,1)} %collective-permute-done.6.refs_3_), custom_call_target="tpu_custom_call" | custom-call | flops 1073741824 | bytes 6291456 | tf_op jit(solution)/shard_map/project/pallas_call | solution.py:88
  36.1 1.0 copy-done.1
  37.1 4.5 %collective-permute-done.13 = bf16[512,256]{1,0:T(8,128)(2,1)S(1)} collective-permute-done((bf16[512,256]{1,0:T(8,128)(2,1)S(1)}, bf16[512,256]{1,0:T(8,128)(2,1)S(1)}, u32[]{:S(2)}, u32[]{:S(2)}) %collective-permute-start.13) | collective-permute-done | bytes 262176 | tf_op jit(solution)/shard_map/ppermute | solution.py:308
  41.5 0.7 copy-done.9
  42.4 0.5 collective-permute-start.10
  42.8 10.9 %all-to-all-start = ((bf16[8,2,256,128]{3,2,1,0:T(8,128)(2,1)}), bf16[8,2,256,128]{3,2,1,0:T(8,128)(2,1)S(1)}, u32[]{:S(2)}, u32[]{:S(2)}) async-start(bf16[8,2,256,128]{3,2,1,0:T(8,128)(2,1)} %split_heads.1), calls=%async_computation | async-start | bytes 2097152 | tf_op jit(solution)/shard_map/all_to_all | solution.py:309
  53.8 1.1 slice.9
  55.0 3.2 %collective-permute-start.8 = (bf16[512,512]{1,0:T(8,128)(2,1)S(1)}, bf16[512,512]{1,0:T(8,128)(2,1)}, u32[]{:S(2)}, u32[]{:S(2)}) collective-permute-start(bf16[512,512]{1,0:T(8,128)(2,1)S(1)} %slice.9), channel_id=1, source_target_pairs={{0,192},{8,56},{16,208},{24,8},{32,224},{40,24},{48,240},{56,40},{... | collective-permute-start | bytes 1572872 | tf_op jit(solution)/shard_map/ppermute | solution.py:316
  58.4 6.7 %project.4.refs_8_ = f32[512,512]{1,0:T(8,128)S(1)} custom-call(s32[4,4]{1,0:T(4,128)S(1)} %pad_add_fusion.2.index_ref, bf16[512,8192]{1,0:T(8,128)(2,1)} %refs_3_.3, bf16[512,8192]{1,0:T(8,128)(2,1)} %refs_3_.3, bf16[512,8192]{1,0:T(8,128)(2,1)} %refs_3_.3, bf16[512,8192]{1,0:T(8,128)(2,1)} %refs_3_.3, ...), custom_call_target="tpu_custom_call" | custom-call | flops 2147483648 | bytes 10485760 | tf_op jit(solution)/shard_map/project/pallas_call | solution.py:88
  65.1 1.0 copy-done.2
  66.1 2.1 %collective-permute-done.7.refs_4_ = bf16[512,512]{1,0:T(8,128)(2,1)S(1)} collective-permute-done((bf16[512,512]{1,0:T(8,128)(2,1)S(1)}, bf16[512,512]{1,0:T(8,128)(2,1)S(1)}, u32[]{:S(2)}, u32[]{:S(2)}) %collective-permute-start.7) | collective-permute-done | bytes 524320 | tf_op jit(solution)/shard_map/ppermute | solution.py:315
  68.2 0.3 collective-permute-done.8.refs_5_
  68.5 0.5 collective-permute-start.12
  69.2 0.6 pad_add_fusion.1.index_ref
  69.8 1.4 collective-permute-done.11.refs_6_
  71.1 0.4 collective-permute-done.12.refs_7_
  71.5 0.4 copy-done.8
  71.9 5.5 %project.5.q_ref = f32[512,512]{1,0:T(8,128)} custom-call(s32[4,2]{1,0:T(4,128)} %pad_add_fusion.1.index_ref, bf16[512,8192]{1,0:T(8,128)(2,1)} %refs_3_.3, bf16[512,8192]{1,0:T(8,128)(2,1)} %refs_3_.3, bf16[512,8192]{1,0:T(8,128)(2,1)} %refs_3_.3, bf16[512,8192]{1,0:T(8,128)(2,1)} %refs_3_.3, bf16[512,512]{1,0:T(8,128)(2,1)} %copy-done.7, ...), custom_call_target="tpu_custom_call" | custom-call | flops 1073741824 | bytes 6291456 | tf_op jit(solution)/shard_map/project/pallas_call | solution.py:88
  77.4 5.4 %all-to-all-done.kv_ref = bf16[8,2,256,128]{3,2,1,0:T(8,128)(2,1)S(1)} async-done(((bf16[8,2,256,128]{3,2,1,0:T(8,128)(2,1)}), bf16[8,2,256,128]{3,2,1,0:T(8,128)(2,1)S(1)}, u32[]{:S(2)}, u32[]{:S(2)}) %all-to-all-start) | async-done | bytes 1048608 | tf_op jit(solution)/shard_map/all_to_all | solution.py:309
  82.8 1.2 copy-done
  84.1 3.0 %attend.2.refs_0_ = bf16[256,512]{1,0:T(8,128)(2,1)S(1)} custom-call(s32[4,8]{1,0:T(4,128)S(1)} %bitcast.102, f32[512,512]{1,0:T(8,128)S(1)} %copy-done, f32[512,128]{1,0:T(8,128)S(1)} %get-tuple-element.27.cos_ref, f32[512,128]{1,0:T(8,128)S(1)} %get-tuple-element.28.sin_ref, bf16[8,2,256,128]{3,2,1,0:T(8,128)(2,1)S(1)} %all-to-all-done.kv_ref), custom_call_target="tpu_custom_call" | custom-call | flops 536870912 | bytes 1835008 | tf_op jit(solution)/shard_map/attend/pallas_call | solution.py:143
  87.1 0.7 collective-permute-start.14
  87.8 3.0 %attend.3.refs_1_ = bf16[256,512]{1,0:T(8,128)(2,1)S(1)} custom-call(s32[4,8]{1,0:T(4,128)S(1)} %bitcast.103, f32[512,512]{1,0:T(8,128)S(1)} %copy-done, f32[512,128]{1,0:T(8,128)S(1)} %get-tuple-element.27.cos_ref, f32[512,128]{1,0:T(8,128)S(1)} %get-tuple-element.28.sin_ref, bf16[8,2,256,128]{3,2,1,0:T(8,128)(2,1)S(1)} %all-to-all-done.kv_ref), custom_call_target="tpu_custom_call" | custom-call | flops 536870912 | bytes 1835008 | tf_op jit(solution)/shard_map/attend/pallas_call | solution.py:143
  90.8 2.7 %collective-permute-start.23 = (bf16[256,512]{1,0:T(8,128)(2,1)S(1)}, bf16[256,512]{1,0:T(8,128)(2,1)S(1)}, u32[]{:S(2)}, u32[]{:S(2)}) collective-permute-start(bf16[256,512]{1,0:T(8,128)(2,1)S(1)} %attend.3.refs_1_), channel_id=1, source_target_pairs={{0,7},{1,0},{2,1},{3,2},{4,3},{5,4},{6,5},{7,6},{8,15},{9,8},{10,9... | collective-permute-start | bytes 786440 | tf_op jit(solution)/shard_map/ppermute | solution.py:368
  93.5 3.2 %collective-permute-start.20 = (bf16[256,512]{1,0:T(8,128)(2,1)S(1)}, bf16[256,512]{1,0:T(8,128)(2,1)S(1)}, u32[]{:S(2)}, u32[]{:S(2)}) collective-permute-start(bf16[256,512]{1,0:T(8,128)(2,1)S(1)} %attend.2.refs_0_), channel_id=1, source_target_pairs={{0,7},{1,0},{2,1},{3,2},{4,3},{5,4},{6,5},{7,6},{8,15},{9,8},{10,9... | collective-permute-start | bytes 786440 | tf_op jit(solution)/shard_map/ppermute | solution.py:368
  96.8 3.5 %collective-permute-done.23.refs_5_ = bf16[256,512]{1,0:T(8,128)(2,1)S(1)} collective-permute-done((bf16[256,512]{1,0:T(8,128)(2,1)S(1)}, bf16[256,512]{1,0:T(8,128)(2,1)S(1)}, u32[]{:S(2)}, u32[]{:S(2)}) %collective-permute-start.23) | collective-permute-done | bytes 262176 | tf_op jit(solution)/shard_map/ppermute | solution.py:368
  100.2 3.7 %collective-permute-start.24 = (bf16[256,512]{1,0:T(8,128)(2,1)S(1)}, bf16[256,512]{1,0:T(8,128)(2,1)S(1)}, u32[]{:S(2)}, u32[]{:S(2)}) collective-permute-start(bf16[256,512]{1,0:T(8,128)(2,1)S(1)} %collective-permute-done.23.refs_5_), channel_id=1, source_target_pairs={{0,7},{1,0},{2,1},{3,2},{4,3},{5,4},{6,5},{7,6},{8,15},{9,8},{10,9... | collective-permute-start | bytes 786440 | tf_op jit(solution)/shard_map/ppermute | solution.py:368
  104.1 1.7 %collective-permute-done.20.refs_4_ = bf16[256,512]{1,0:T(8,128)(2,1)S(1)} collective-permute-done((bf16[256,512]{1,0:T(8,128)(2,1)S(1)}, bf16[256,512]{1,0:T(8,128)(2,1)S(1)}, u32[]{:S(2)}, u32[]{:S(2)}) %collective-permute-start.20) | collective-permute-done | bytes 262176 | tf_op jit(solution)/shard_map/ppermute | solution.py:368
  105.8 3.7 %collective-permute-start.21 = (bf16[256,512]{1,0:T(8,128)(2,1)S(1)}, bf16[256,512]{1,0:T(8,128)(2,1)S(1)}, u32[]{:S(2)}, u32[]{:S(2)}) collective-permute-start(bf16[256,512]{1,0:T(8,128)(2,1)S(1)} %collective-permute-done.20.refs_4_), channel_id=1, source_target_pairs={{0,7},{1,0},{2,1},{3,2},{4,3},{5,4},{6,5},{7,6},{8,15},{9,8},{10,9... | collective-permute-start | bytes 786440 | tf_op jit(solution)/shard_map/ppermute | solution.py:368
  109.6 1.9 %collective-permute-done.24.refs_9_ = bf16[256,512]{1,0:T(8,128)(2,1)S(1)} collective-permute-done((bf16[256,512]{1,0:T(8,128)(2,1)S(1)}, bf16[256,512]{1,0:T(8,128)(2,1)S(1)}, u32[]{:S(2)}, u32[]{:S(2)}) %collective-permute-start.24) | collective-permute-done | bytes 262176 | tf_op jit(solution)/shard_map/ppermute | solution.py:368
  111.5 3.7 %collective-permute-start.25 = (bf16[256,512]{1,0:T(8,128)(2,1)S(1)}, bf16[256,512]{1,0:T(8,128)(2,1)S(1)}, u32[]{:S(2)}, u32[]{:S(2)}) collective-permute-start(bf16[256,512]{1,0:T(8,128)(2,1)S(1)} %collective-permute-done.24.refs_9_), channel_id=1, source_target_pairs={{0,7},{1,0},{2,1},{3,2},{4,3},{5,4},{6,5},{7,6},{8,15},{9,8},{10,9... | collective-permute-start | bytes 786440 | tf_op jit(solution)/shard_map/ppermute | solution.py:368
  116.0 1.0 collective-permute-done.21.refs_8_
  117.1 3.7 %collective-permute-start.22 = (bf16[256,512]{1,0:T(8,128)(2,1)S(1)}, bf16[256,512]{1,0:T(8,128)(2,1)}, u32[]{:S(2)}, u32[]{:S(2)}) collective-permute-start(bf16[256,512]{1,0:T(8,128)(2,1)S(1)} %collective-permute-done.21.refs_8_), channel_id=1, source_target_pairs={{0,7},{1,0},{2,1},{3,2},{4,3},{5,4},{6,5},{7,6},{8,15},{9,8},{10,9... | collective-permute-start | bytes 786440 | tf_op jit(solution)/shard_map/ppermute | solution.py:368
  120.8 1.9 %collective-permute-done.25.refs_3_ = bf16[256,512]{1,0:T(8,128)(2,1)S(1)} collective-permute-done((bf16[256,512]{1,0:T(8,128)(2,1)S(1)}, bf16[256,512]{1,0:T(8,128)(2,1)S(1)}, u32[]{:S(2)}, u32[]{:S(2)}) %collective-permute-start.25) | collective-permute-done | bytes 262176 | tf_op jit(solution)/shard_map/ppermute | solution.py:368
  122.9 3.5 %collective-permute-start.27 = (bf16[256,512]{1,0:T(8,128)(2,1)S(1)}, bf16[256,512]{1,0:T(8,128)(2,1)}, u32[]{:S(2)}, u32[]{:S(2)}) collective-permute-start(bf16[256,512]{1,0:T(8,128)(2,1)S(1)} %collective-permute-done.25.refs_3_), channel_id=1, source_target_pairs={{0,7},{1,0},{2,1},{3,2},{4,3},{5,4},{6,5},{7,6},{8,15},{9,8},{10,9... | collective-permute-start | bytes 786440 | tf_op jit(solution)/shard_map/ppermute | solution.py:370
  126.5 6.0 %output.2.refs_9_ = f32[512,1024]{1,0:T(8,128)S(1)} custom-call(s32[5,4]{1,0:T(8,128)S(1)} %stack.419.index_ref, bf16[256,512]{1,0:T(8,128)(2,1)S(1)} %attend.2.refs_0_, bf16[256,512]{1,0:T(8,128)(2,1)S(1)} %attend.3.refs_1_, bf16[256,512]{1,0:T(8,128)(2,1)S(1)} %collective-permute-done.14.refs_2_, bf16[256,512]{1,0:T(8,128)(2,1)S(1)} %collective-permute-done.17.refs_3_, ...), custom_call_target="tpu_custom_call" | custom-call | flops 2684354560 | bytes 12058624 | tf_op jit(solution)/shard_map/output/pallas_call | solution.py:197
  132.8 5.8 %output.3 = bf16[512,1024]{1,0:T(8,128)(2,1)} custom-call(s32[3,4]{1,0:T(4,128)S(1)} %pad_add_fusion.index_ref, bf16[256,512]{1,0:T(8,128)(2,1)S(1)} %collective-permute-done.16.refs_0_, bf16[256,512]{1,0:T(8,128)(2,1)S(1)} %collective-permute-done.19.refs_1_, bf16[256,512]{1,0:T(8,128)(2,1)} %collective-permute-done.22.refs_2_, ...), custom_call_target="tpu_custom_call" | custom-call | flops 1610612736 | bytes 8912896 | tf_op jit(solution)/shard_map/output/pallas_call | solution.py:197
  (63 shorter events, 2.3 us)
Async XLA Ops:
  6.5 116.2 %all-gather.3.cloned.1.call-start = ((), (), s32[]{:S(2)}) async-start(), calls=%async_computation.1 | async-start | bytes 8650752 | tf_op jit(solution)/shard_map/all_gather | solution.py:352
  6.5 11.5 %collective-permute-start = (bf16[256,512]{1,0:T(8,128)(2,1)}, bf16[256,512]{1,0:T(8,128)(2,1)S(1)}, u32[]{:S(2)}, u32[]{:S(2)}) collective-permute-start(bf16[256,512]{1,0:T(8,128)(2,1)} %refs_0_.4), channel_id=1, source_target_pairs={{0,16},{8,72},{16,32},{24,88},{32,48},{40,104},{48,0},{56,120},{64... | collective-permute-start | bytes 786440 | tf_op jit(solution)/shard_map/ppermute | solution.py:303
  8.8 10.6 %collective-permute-start.1 = (bf16[256,512]{1,0:T(8,128)(2,1)}, bf16[256,512]{1,0:T(8,128)(2,1)S(1)}, u32[]{:S(2)}, u32[]{:S(2)}) collective-permute-start(bf16[256,512]{1,0:T(8,128)(2,1)} %refs_0_.4), channel_id=1, source_target_pairs={{0,48},{8,200},{16,0},{24,216},{32,16},{40,232},{48,32},{56,248},{... | collective-permute-start | bytes 786440 | tf_op jit(solution)/shard_map/ppermute | solution.py:304
  8.8 9.3 %collective-permute-start.2 = (bf16[256,512]{1,0:T(8,128)(2,1)}, bf16[256,512]{1,0:T(8,128)(2,1)S(1)}, u32[]{:S(2)}, u32[]{:S(2)}) collective-permute-start(bf16[256,512]{1,0:T(8,128)(2,1)} %refs_0_.4), channel_id=1, source_target_pairs={{0,32},{8,136},{16,48},{24,152},{32,0},{40,168},{48,16},{56,184},{... | collective-permute-start | bytes 786440 | tf_op jit(solution)/shard_map/ppermute | solution.py:305
  10.2 7.8 %collective-permute-start.3 = (bf16[512,256]{1,0:T(8,128)(2,1)}, bf16[512,256]{1,0:T(8,128)(2,1)S(1)}, u32[]{:S(2)}, u32[]{:S(2)}) collective-permute-start(bf16[512,256]{1,0:T(8,128)(2,1)} %param.8), channel_id=1, source_target_pairs={{0,0},{1,49},{2,66},{3,115},{4,132},{5,181},{6,198},{7,247},{8,8},... | collective-permute-start | bytes 786440 | tf_op jit(solution)/shard_map/ppermute | solution.py:348
  11.8 1.0 copy-start.3
  12.9 1.0 copy-start.4
  19.4 1.0 copy-start.5
  20.4 11.2 %collective-permute-start.6 = (bf16[1024,512]{1,0:T(8,128)(2,1)S(1)}, bf16[1024,512]{1,0:T(8,128)(2,1)}, u32[]{:S(2)}, u32[]{:S(2)}) collective-permute-start(bf16[1024,512]{1,0:T(8,128)(2,1)S(1)} %side_by_side.1.refs_2_), channel_id=1, source_target_pairs={{0,8},{8,0},{16,24},{24,16},{32,40},{40,32},{48,56},{56,48},{64,72... | collective-permute-start | bytes 3145736 | tf_op jit(solution)/shard_map/ppermute | solution.py:38
  20.5 21.0 %collective-permute-start.4 = (bf16[1024,512]{1,0:T(8,128)(2,1)S(1)}, bf16[1024,512]{1,0:T(8,128)(2,1)S(1)}, u32[]{:S(2)}, u32[]{:S(2)}) collective-permute-start(bf16[1024,512]{1,0:T(8,128)(2,1)S(1)} %side_by_side.1.refs_2_), channel_id=1, source_target_pairs={{0,64},{8,24},{16,80},{24,40},{32,96},{40,56},{48,112},{56,8},{64,... | collective-permute-start | bytes 3145736 | tf_op jit(solution)/shard_map/ppermute | solution.py:311
  20.7 20.9 %collective-permute-start.5 = (bf16[1024,512]{1,0:T(8,128)(2,1)S(1)}, bf16[1024,512]{1,0:T(8,128)(2,1)}, u32[]{:S(2)}, u32[]{:S(2)}) collective-permute-start(bf16[1024,512]{1,0:T(8,128)(2,1)S(1)} %side_by_side.1.refs_2_), channel_id=1, source_target_pairs={{0,192},{8,56},{16,208},{24,8},{32,224},{40,24},{48,240},{56,40},{... | collective-permute-start | bytes 3145736 | tf_op jit(solution)/shard_map/ppermute | solution.py:312
  23.8 17.7 %collective-permute-start.13 = (bf16[512,256]{1,0:T(8,128)(2,1)S(1)}, bf16[512,256]{1,0:T(8,128)(2,1)S(1)}, u32[]{:S(2)}, u32[]{:S(2)}) collective-permute-start(bf16[512,256]{1,0:T(8,128)(2,1)S(1)} %collective-permute-done.3), channel_id=1, source_target_pairs={{0,0},{49,48},{66,64},{115,112},{132,128},{181,176},{198,192},{247... | collective-permute-start | bytes 786440 | tf_op jit(solution)/shard_map/ppermute | solution.py:308
  36.1 1.0 copy-start.1
  41.5 0.7 copy-start.9
  42.2 16.1 %collective-permute-start.9 = (bf16[1024,512]{1,0:T(8,128)(2,1)S(1)}, bf16[1024,512]{1,0:T(8,128)(2,1)}, u32[]{:S(2)}, u32[]{:S(2)}) collective-permute-start(bf16[1024,512]{1,0:T(8,128)(2,1)S(1)} %collective-permute-done.4.refs_4_), channel_id=1, source_target_pairs={{0,8},{8,0},{16,24},{24,16},{32,40},{40,32},{48,56},{56,48},{64,72... | collective-permute-start | bytes 3145736 | tf_op jit(solution)/shard_map/ppermute | solution.py:38
  42.4 16.1 %collective-permute-start.10 = (bf16[1024,512]{1,0:T(8,128)(2,1)}, bf16[1024,512]{1,0:T(8,128)(2,1)}, u32[]{:S(2)}, u32[]{:S(2)}) collective-permute-start(bf16[1024,512]{1,0:T(8,128)(2,1)} %collective-permute-done.5.refs_5_), channel_id=1, source_target_pairs={{0,8},{8,0},{16,24},{24,16},{32,40},{40,32},{48,56},{56,48},{64,72... | collective-permute-start | bytes 3145736 | tf_op jit(solution)/shard_map/ppermute | solution.py:38
  42.8 40.0 %all-to-all-start = ((bf16[8,2,256,128]{3,2,1,0:T(8,128)(2,1)}), bf16[8,2,256,128]{3,2,1,0:T(8,128)(2,1)S(1)}, u32[]{:S(2)}, u32[]{:S(2)}) async-start(bf16[8,2,256,128]{3,2,1,0:T(8,128)(2,1)} %split_heads.1), calls=%async_computation | async-start | bytes 2097152 | tf_op jit(solution)/shard_map/all_to_all | solution.py:309
  54.9 13.3 %collective-permute-start.7 = (bf16[512,512]{1,0:T(8,128)(2,1)S(1)}, bf16[512,512]{1,0:T(8,128)(2,1)S(1)}, u32[]{:S(2)}, u32[]{:S(2)}) collective-permute-start(bf16[512,512]{1,0:T(8,128)(2,1)S(1)} %slice.8), channel_id=1, source_target_pairs={{0,64},{8,24},{16,80},{24,40},{32,96},{40,56},{48,112},{56,8},{64,... | collective-permute-start | bytes 1572872 | tf_op jit(solution)/shard_map/ppermute | solution.py:315
  55.0 13.5 %collective-permute-start.8 = (bf16[512,512]{1,0:T(8,128)(2,1)S(1)}, bf16[512,512]{1,0:T(8,128)(2,1)}, u32[]{:S(2)}, u32[]{:S(2)}) collective-permute-start(bf16[512,512]{1,0:T(8,128)(2,1)S(1)} %slice.9), channel_id=1, source_target_pairs={{0,192},{8,56},{16,208},{24,8},{32,224},{40,24},{48,240},{56,40},{... | collective-permute-start | bytes 1572872 | tf_op jit(solution)/shard_map/ppermute | solution.py:316
  65.1 1.0 copy-start.2
  68.2 3.3 %copy-start.7 = (bf16[512,512]{1,0:T(8,128)(2,1)}, bf16[512,512]{1,0:T(8,128)(2,1)S(1)}, u32[]{:S(2)}) copy-start(bf16[512,512]{1,0:T(8,128)(2,1)S(1)} %collective-permute-done.7.refs_4_) | copy-start | bytes 1572868
  68.5 2.6 %collective-permute-start.11 = (bf16[512,512]{1,0:T(8,128)(2,1)S(1)}, bf16[512,512]{1,0:T(8,128)(2,1)S(1)}, u32[]{:S(2)}, u32[]{:S(2)}) collective-permute-start(bf16[512,512]{1,0:T(8,128)(2,1)S(1)} %collective-permute-done.7.refs_4_), channel_id=1, source_target_pairs={{0,8},{8,0},{16,24},{24,16},{32,40},{40,32},{48,56},{56,48},{64,72... | collective-permute-start | bytes 1572872 | tf_op jit(solution)/shard_map/ppermute | solution.py:38
  68.5 3.0 %collective-permute-start.12 = (bf16[512,512]{1,0:T(8,128)(2,1)}, bf16[512,512]{1,0:T(8,128)(2,1)}, u32[]{:S(2)}, u32[]{:S(2)}) collective-permute-start(bf16[512,512]{1,0:T(8,128)(2,1)} %collective-permute-done.8.refs_5_), channel_id=1, source_target_pairs={{0,8},{8,0},{16,24},{24,16},{32,40},{40,32},{48,56},{56,48},{64,72... | collective-permute-start | bytes 1572872 | tf_op jit(solution)/shard_map/ppermute | solution.py:38
  69.8 13.1 %copy-start.6 = (s32[1,4,8]{2,1,0:T(4,128)S(1)}, s32[1,4,8]{2,1,0:T(4,128)}, u32[]{:S(2)}) copy-start(s32[1,4,8]{2,1,0:T(4,128)} %param.11) | copy-start | bytes 388
  71.1 0.8 copy-start.8
  82.8 1.2 copy-start
  87.1 9.7 %collective-permute-start.14 = (bf16[256,512]{1,0:T(8,128)(2,1)S(1)}, bf16[256,512]{1,0:T(8,128)(2,1)S(1)}, u32[]{:S(2)}, u32[]{:S(2)}) collective-permute-start(bf16[256,512]{1,0:T(8,128)(2,1)S(1)} %attend.2.refs_0_), channel_id=1, source_target_pairs={{0,1},{1,2},{2,3},{3,4},{4,5},{5,6},{6,7},{7,0},{8,9},{9,10},{10,1... | collective-permute-start | bytes 786440 | tf_op jit(solution)/shard_map/ppermute | solution.py:367
  90.8 9.4 %collective-permute-start.23 = (bf16[256,512]{1,0:T(8,128)(2,1)S(1)}, bf16[256,512]{1,0:T(8,128)(2,1)S(1)}, u32[]{:S(2)}, u32[]{:S(2)}) collective-permute-start(bf16[256,512]{1,0:T(8,128)(2,1)S(1)} %attend.3.refs_1_), channel_id=1, source_target_pairs={{0,7},{1,0},{2,1},{3,2},{4,3},{5,4},{6,5},{7,6},{8,15},{9,8},{10,9... | collective-permute-start | bytes 786440 | tf_op jit(solution)/shard_map/ppermute | solution.py:368
  93.5 10.6 %collective-permute-start.17 = (bf16[256,512]{1,0:T(8,128)(2,1)S(1)}, bf16[256,512]{1,0:T(8,128)(2,1)S(1)}, u32[]{:S(2)}, u32[]{:S(2)}) collective-permute-start(bf16[256,512]{1,0:T(8,128)(2,1)S(1)} %attend.3.refs_1_), channel_id=1, source_target_pairs={{0,1},{1,2},{2,3},{3,4},{4,5},{5,6},{6,7},{7,0},{8,9},{9,10},{10,1... | collective-permute-start | bytes 786440 | tf_op jit(solution)/shard_map/ppermute | solution.py:367
  93.5 12.3 %collective-permute-start.20 = (bf16[256,512]{1,0:T(8,128)(2,1)S(1)}, bf16[256,512]{1,0:T(8,128)(2,1)S(1)}, u32[]{:S(2)}, u32[]{:S(2)}) collective-permute-start(bf16[256,512]{1,0:T(8,128)(2,1)S(1)} %attend.2.refs_0_), channel_id=1, source_target_pairs={{0,7},{1,0},{2,1},{3,2},{4,3},{5,4},{6,5},{7,6},{8,15},{9,8},{10,9... | collective-permute-start | bytes 786440 | tf_op jit(solution)/shard_map/ppermute | solution.py:368
  96.7 12.8 %collective-permute-start.15 = (bf16[256,512]{1,0:T(8,128)(2,1)S(1)}, bf16[256,512]{1,0:T(8,128)(2,1)S(1)}, u32[]{:S(2)}, u32[]{:S(2)}) collective-permute-start(bf16[256,512]{1,0:T(8,128)(2,1)S(1)} %collective-permute-done.14.refs_2_), channel_id=1, source_target_pairs={{0,1},{1,2},{2,3},{3,4},{4,5},{5,6},{6,7},{7,0},{8,9},{9,10},{10,1... | collective-permute-start | bytes 786440 | tf_op jit(solution)/shard_map/ppermute | solution.py:367
  100.2 11.2 %collective-permute-start.24 = (bf16[256,512]{1,0:T(8,128)(2,1)S(1)}, bf16[256,512]{1,0:T(8,128)(2,1)S(1)}, u32[]{:S(2)}, u32[]{:S(2)}) collective-permute-start(bf16[256,512]{1,0:T(8,128)(2,1)S(1)} %collective-permute-done.23.refs_5_), channel_id=1, source_target_pairs={{0,7},{1,0},{2,1},{3,2},{4,3},{5,4},{6,5},{7,6},{8,15},{9,8},{10,9... | collective-permute-start | bytes 786440 | tf_op jit(solution)/shard_map/ppermute | solution.py:368
  104.1 11.9 %collective-permute-start.18 = (bf16[256,512]{1,0:T(8,128)(2,1)S(1)}, bf16[256,512]{1,0:T(8,128)(2,1)S(1)}, u32[]{:S(2)}, u32[]{:S(2)}) collective-permute-start(bf16[256,512]{1,0:T(8,128)(2,1)S(1)} %collective-permute-done.17.refs_3_), channel_id=1, source_target_pairs={{0,1},{1,2},{2,3},{3,4},{4,5},{5,6},{6,7},{7,0},{8,9},{9,10},{10,1... | collective-permute-start | bytes 786440 | tf_op jit(solution)/shard_map/ppermute | solution.py:367
  105.8 11.2 %collective-permute-start.21 = (bf16[256,512]{1,0:T(8,128)(2,1)S(1)}, bf16[256,512]{1,0:T(8,128)(2,1)S(1)}, u32[]{:S(2)}, u32[]{:S(2)}) collective-permute-start(bf16[256,512]{1,0:T(8,128)(2,1)S(1)} %collective-permute-done.20.refs_4_), channel_id=1, source_target_pairs={{0,7},{1,0},{2,1},{3,2},{4,3},{5,4},{6,5},{7,6},{8,15},{9,8},{10,9... | collective-permute-start | bytes 786440 | tf_op jit(solution)/shard_map/ppermute | solution.py:368
  109.6 11.2 %collective-permute-start.16 = (bf16[256,512]{1,0:T(8,128)(2,1)S(1)}, bf16[256,512]{1,0:T(8,128)(2,1)S(1)}, u32[]{:S(2)}, u32[]{:S(2)}) collective-permute-start(bf16[256,512]{1,0:T(8,128)(2,1)S(1)} %collective-permute-done.15.refs_6_), channel_id=1, source_target_pairs={{0,1},{1,2},{2,3},{3,4},{4,5},{5,6},{6,7},{7,0},{8,9},{9,10},{10,1... | collective-permute-start | bytes 786440 | tf_op jit(solution)/shard_map/ppermute | solution.py:367
  111.5 11.2 %collective-permute-start.25 = (bf16[256,512]{1,0:T(8,128)(2,1)S(1)}, bf16[256,512]{1,0:T(8,128)(2,1)S(1)}, u32[]{:S(2)}, u32[]{:S(2)}) collective-permute-start(bf16[256,512]{1,0:T(8,128)(2,1)S(1)} %collective-permute-done.24.refs_9_), channel_id=1, source_target_pairs={{0,7},{1,0},{2,1},{3,2},{4,3},{5,4},{6,5},{7,6},{8,15},{9,8},{10,9... | collective-permute-start | bytes 786440 | tf_op jit(solution)/shard_map/ppermute | solution.py:368
  115.9 16.6 %collective-permute-start.19 = (bf16[256,512]{1,0:T(8,128)(2,1)S(1)}, bf16[256,512]{1,0:T(8,128)(2,1)S(1)}, u32[]{:S(2)}, u32[]{:S(2)}) collective-permute-start(bf16[256,512]{1,0:T(8,128)(2,1)S(1)} %collective-permute-done.18.refs_7_), channel_id=1, source_target_pairs={{0,1},{1,2},{2,3},{3,4},{4,5},{5,6},{6,7},{7,0},{8,9},{9,10},{10,1... | collective-permute-start | bytes 786440 | tf_op jit(solution)/shard_map/ppermute | solution.py:367
  117.1 15.4 %collective-permute-start.22 = (bf16[256,512]{1,0:T(8,128)(2,1)S(1)}, bf16[256,512]{1,0:T(8,128)(2,1)}, u32[]{:S(2)}, u32[]{:S(2)}) collective-permute-start(bf16[256,512]{1,0:T(8,128)(2,1)S(1)} %collective-permute-done.21.refs_8_), channel_id=1, source_target_pairs={{0,7},{1,0},{2,1},{3,2},{4,3},{5,4},{6,5},{7,6},{8,15},{9,8},{10,9... | collective-permute-start | bytes 786440 | tf_op jit(solution)/shard_map/ppermute | solution.py:368
  122.7 9.8 %collective-permute-start.26 = (bf16[256,512]{1,0:T(8,128)(2,1)S(1)}, bf16[256,512]{1,0:T(8,128)(2,1)}, u32[]{:S(2)}, u32[]{:S(2)}) collective-permute-start(bf16[256,512]{1,0:T(8,128)(2,1)S(1)} %collective-permute-done.16.refs_0_), channel_id=1, source_target_pairs={{0,1},{1,2},{2,3},{3,4},{4,5},{5,6},{6,7},{7,0},{8,9},{9,10},{10,1... | collective-permute-start | bytes 786440 | tf_op jit(solution)/shard_map/ppermute | solution.py:370
  122.9 9.9 %collective-permute-start.27 = (bf16[256,512]{1,0:T(8,128)(2,1)S(1)}, bf16[256,512]{1,0:T(8,128)(2,1)}, u32[]{:S(2)}, u32[]{:S(2)}) collective-permute-start(bf16[256,512]{1,0:T(8,128)(2,1)S(1)} %collective-permute-done.25.refs_3_), channel_id=1, source_target_pairs={{0,7},{1,0},{2,1},{3,2},{4,3},{5,4},{6,5},{7,6},{8,15},{9,8},{10,9... | collective-permute-start | bytes 786440 | tf_op jit(solution)/shard_map/ppermute | solution.py:370
Sparse Core Ops, SparseCore 0:
  42.4 62.1 all-gather.2

commit v5 on v4

--- a/solution.py
+++ b/solution.py
@@ -368,8 +368,8 @@
         up.append([lax.ppermute(c, "ctx", left) for c in up[-1]])
     weights, last_down, last_up = lax.optimization_barrier((weights, down[3][0], up[3][1]))
     far = [lax.ppermute(last_down, "ctx", right), lax.ppermute(last_up, "ctx", left)]
-    total = output([contexts, down[1], up[1], down[2], up[2]], weights, owner(0, -1, 1, -2, 2))
-    return output([down[3], up[3], far], weights, owner(-3, 3, 4), total, BF16)
+    total = output([contexts, down[1], up[1], down[2], up[2], down[3]], weights, owner(0, -1, 1, -2, 2, -3))
+    return output([up[3], far], weights, owner(3, 4), total, BF16)
 
 
 def solution(mesh):

time: 146 us -> 148 us (1.014)
  waiting for transfers between devices: 25.7 us -> 35.7 us
  starting transfers between devices: 57 us -> 49.4 us
    ppermute x6, waiting for transfers between devices: 0.09 us -> 19.4 us  [body(): down.append([lax.ppermute(c, 'ctx', right) for c in down[-1]])]
    ppermute x6, starting transfers between devices: 20.7 us -> 8.39 us  [body(): up.append([lax.ppermute(c, 'ctx', left) for c in up[-1]])]
    ppermute x6, waiting for transfers between devices: 10 us -> 0.82 us  [body(): up.append([lax.ppermute(c, 'ctx', left) for c in up[-1]])]
    ppermute x6, starting transfers between devices: 0.8 us -> 6.02 us  [body(): down.append([lax.ppermute(c, 'ctx', right) for c in down[-1]])]
  transfers between devices with their start and end apart: 30 -> 30, of which waited for: 13 -> 14; matrix products, arithmetic and copies ran while one was open for 3% -> 2% of each run, Pallas kernels for 22% -> 22%
where the time goes in v5:
time: 148 us; the launch traced here: 147 us
  starting transfers between devices  49.4 us (33%)
  Pallas kernels  37.3 us (25%)
  waiting for transfers between devices  35.7 us (24%)
  between operations  14 us (9%)
  local copies, waits for them, and re-layouts  8.45 us (6%)
  other arithmetic  2.51 us (2%)
    ppermute x6, waiting for transfers between devices, body(): down.append([lax.ppermute(c, 'ctx', right) for c in down[-1]])  19.4 us
    pallas_call x3, Pallas kernels, project(): pl.pallas_call(functools.partial(project_kernel, terms, before is not Non...  16.6 us
    pallas_call x2, Pallas kernels, output(): pl.pallas_call(functools.partial(output_kernel, terms, before is not None...  11.6 us
    all_to_all x1, starting transfers between devices, project_all(): kv = lax.all_to_all(after(by_head, wo_here), 'ctx', 0, 0, tiled=True)  10.9 us
    ppermute x6, starting transfers between devices, body(): up.append([lax.ppermute(c, 'ctx', left) for c in up[-1]])  8.39 us
    ppermute x1, starting transfers between devices, project_all(): wo_here = lax.ppermute(wo_near, ('fsdp', 'ctx'), wo_across)  7.7 us
    unnamed x20, local copies, waits for them, and re-layouts  7.31 us
    pallas_call x2, Pallas kernels, attend(): pl.pallas_call(functools.partial(attend_kernel, heads, entries, first, ow...  6.03 us
  transfers between devices with their start and end apart: 30, of which 14 were waited for; matrix products, arithmetic and copies ran while one was open for 2% of the time, Pallas kernels for 22%

profile of v5, /device:TPU:6, one launch (start us, length us, event | category | flops | bytes accessed | tf_op | source)
XLA Modules:
  0.0 147.3 jit_solution(13008431178898066266)
XLA Ops:
  6.5 2.2 %collective-permute-start = (bf16[256,512]{1,0:T(8,128)(2,1)}, bf16[256,512]{1,0:T(8,128)(2,1)S(1)}, u32[]{:S(2)}, u32[]{:S(2)}) collective-permute-start(bf16[256,512]{1,0:T(8,128)(2,1)} %refs_0_.4), channel_id=1, source_target_pairs={{0,16},{8,72},{16,32},{24,88},{32,48},{40,104},{48,0},{56,120},{64... | collective-permute-start | bytes 786440 | tf_op jit(solution)/shard_map/ppermute | solution.py:303
  8.8 1.5 collective-permute-start.2
  10.2 1.6 %collective-permute-start.3 = (bf16[512,256]{1,0:T(8,128)(2,1)}, bf16[512,256]{1,0:T(8,128)(2,1)S(1)}, u32[]{:S(2)}, u32[]{:S(2)}) collective-permute-start(bf16[512,256]{1,0:T(8,128)(2,1)} %param.8), channel_id=1, source_target_pairs={{0,0},{1,49},{2,66},{3,115},{4,132},{5,181},{6,198},{7,247},{8,8},... | collective-permute-start | bytes 786440 | tf_op jit(solution)/shard_map/ppermute | solution.py:348
  11.8 1.0 copy-done.3
  12.9 1.0 copy-done.4
  13.9 2.9 %split_heads.1 = bf16[8,2,256,128]{3,2,1,0:T(8,128)(2,1)} custom-call(bf16[256,1024]{1,0:T(8,128)(2,1)S(1)} %copy-done.3, bf16[256,1024]{1,0:T(8,128)(2,1)S(1)} %copy-done.4), custom_call_target="tpu_custom_call" | custom-call | bytes 2097152 | tf_op jit(solution)/shard_map/split_heads/pallas_call | solution.py:266
  16.8 1.0 fusion.2
  18.0 1.3 collective-permute-done.1.refs_2_
  19.4 0.9 copy-done.5
  20.6 3.2 %collective-permute-start.5 = (bf16[1024,512]{1,0:T(8,128)(2,1)S(1)}, bf16[1024,512]{1,0:T(8,128)(2,1)}, u32[]{:S(2)}, u32[]{:S(2)}) collective-permute-start(bf16[1024,512]{1,0:T(8,128)(2,1)S(1)} %side_by_side.1.refs_2_), channel_id=1, source_target_pairs={{0,192},{8,56},{16,208},{24,8},{32,224},{40,24},{48,240},{56,40},{... | collective-permute-start | bytes 3145736 | tf_op jit(solution)/shard_map/ppermute | solution.py:312
  23.8 7.7 %collective-permute-start.13 = (bf16[512,256]{1,0:T(8,128)(2,1)S(1)}, bf16[512,256]{1,0:T(8,128)(2,1)S(1)}, u32[]{:S(2)}, u32[]{:S(2)}) collective-permute-start(bf16[512,256]{1,0:T(8,128)(2,1)S(1)} %collective-permute-done.3), channel_id=1, source_target_pairs={{0,0},{49,48},{66,64},{115,112},{132,128},{181,176},{198,192},{247... | collective-permute-start | bytes 786440 | tf_op jit(solution)/shard_map/ppermute | solution.py:308
  31.7 4.4 %project.3.refs_8_ = f32[512,512]{1,0:T(8,128)S(1)} custom-call(s32[2,4]{1,0:T(2,128)S(1)} %pad_add_fusion.3.index_ref, bf16[512,8192]{1,0:T(8,128)(2,1)} %refs_3_.3, bf16[512,8192]{1,0:T(8,128)(2,1)} %refs_3_.3, bf16[1024,512]{1,0:T(8,128)(2,1)S(1)} %side_by_side.1.refs_2_, bf16[1024,512]{1,0:T(8,128)(2,1)} %collective-permute-done.6.refs_3_), custom_call_target="tpu_custom_call" | custom-call | flops 1073741824 | bytes 6291456 | tf_op jit(solution)/shard_map/project/pallas_call | solution.py:88
  36.1 1.0 copy-done.1
  37.1 4.5 %collective-permute-done.13 = bf16[512,256]{1,0:T(8,128)(2,1)S(1)} collective-permute-done((bf16[512,256]{1,0:T(8,128)(2,1)S(1)}, bf16[512,256]{1,0:T(8,128)(2,1)S(1)}, u32[]{:S(2)}, u32[]{:S(2)}) %collective-permute-start.13) | collective-permute-done | bytes 262176 | tf_op jit(solution)/shard_map/ppermute | solution.py:308
  41.5 0.7 copy-done.9
  42.8 10.9 %all-to-all-start = ((bf16[8,2,256,128]{3,2,1,0:T(8,128)(2,1)}), bf16[8,2,256,128]{3,2,1,0:T(8,128)(2,1)S(1)}, u32[]{:S(2)}, u32[]{:S(2)}) async-start(bf16[8,2,256,128]{3,2,1,0:T(8,128)(2,1)} %split_heads.1), calls=%async_computation | async-start | bytes 2097152 | tf_op jit(solution)/shard_map/all_to_all | solution.py:309
  53.8 1.1 slice.9
  55.0 3.2 %collective-permute-start.8 = (bf16[512,512]{1,0:T(8,128)(2,1)S(1)}, bf16[512,512]{1,0:T(8,128)(2,1)}, u32[]{:S(2)}, u32[]{:S(2)}) collective-permute-start(bf16[512,512]{1,0:T(8,128)(2,1)S(1)} %slice.9), channel_id=1, source_target_pairs={{0,192},{8,56},{16,208},{24,8},{32,224},{40,24},{48,240},{56,40},{... | collective-permute-start | bytes 1572872 | tf_op jit(solution)/shard_map/ppermute | solution.py:316
  58.4 6.7 %project.4.refs_8_ = f32[512,512]{1,0:T(8,128)S(1)} custom-call(s32[4,4]{1,0:T(4,128)S(1)} %pad_add_fusion.1.index_ref, bf16[512,8192]{1,0:T(8,128)(2,1)} %refs_3_.3, bf16[512,8192]{1,0:T(8,128)(2,1)} %refs_3_.3, bf16[512,8192]{1,0:T(8,128)(2,1)} %refs_3_.3, bf16[512,8192]{1,0:T(8,128)(2,1)} %refs_3_.3, ...), custom_call_target="tpu_custom_call" | custom-call | flops 2147483648 | bytes 10485760 | tf_op jit(solution)/shard_map/project/pallas_call | solution.py:88
  65.1 1.0 copy-done.2
  66.1 2.1 %collective-permute-done.7.refs_4_ = bf16[512,512]{1,0:T(8,128)(2,1)S(1)} collective-permute-done((bf16[512,512]{1,0:T(8,128)(2,1)S(1)}, bf16[512,512]{1,0:T(8,128)(2,1)S(1)}, u32[]{:S(2)}, u32[]{:S(2)}) %collective-permute-start.7) | collective-permute-done | bytes 524320 | tf_op jit(solution)/shard_map/ppermute | solution.py:315
  69.7 1.4 collective-permute-done.11.refs_6_
  71.9 5.5 %project.5.q_ref = f32[512,512]{1,0:T(8,128)} custom-call(s32[4,2]{1,0:T(4,128)} %pad_add_fusion.index_ref, bf16[512,8192]{1,0:T(8,128)(2,1)} %refs_3_.3, bf16[512,8192]{1,0:T(8,128)(2,1)} %refs_3_.3, bf16[512,8192]{1,0:T(8,128)(2,1)} %refs_3_.3, bf16[512,8192]{1,0:T(8,128)(2,1)} %refs_3_.3, bf16[512,512]{1,0:T(8,128)(2,1)} %copy-done.7, ...), custom_call_target="tpu_custom_call" | custom-call | flops 1073741824 | bytes 6291456 | tf_op jit(solution)/shard_map/project/pallas_call | solution.py:88
  77.4 5.4 %all-to-all-done.kv_ref = bf16[8,2,256,128]{3,2,1,0:T(8,128)(2,1)S(1)} async-done(((bf16[8,2,256,128]{3,2,1,0:T(8,128)(2,1)}), bf16[8,2,256,128]{3,2,1,0:T(8,128)(2,1)S(1)}, u32[]{:S(2)}, u32[]{:S(2)}) %all-to-all-start) | async-done | bytes 1048608 | tf_op jit(solution)/shard_map/all_to_all | solution.py:309
  82.8 1.2 copy-done
  84.1 3.0 %attend.3.refs_1_ = bf16[256,512]{1,0:T(8,128)(2,1)S(1)} custom-call(s32[4,8]{1,0:T(4,128)S(1)} %bitcast.102, f32[512,512]{1,0:T(8,128)S(1)} %copy-done, f32[512,128]{1,0:T(8,128)S(1)} %get-tuple-element.27.cos_ref, f32[512,128]{1,0:T(8,128)S(1)} %get-tuple-element.28.sin_ref, bf16[8,2,256,128]{3,2,1,0:T(8,128)(2,1)S(1)} %all-to-all-done.kv_ref), custom_call_target="tpu_custom_call" | custom-call | flops 536870912 | bytes 1835008 | tf_op jit(solution)/shard_map/attend/pallas_call | solution.py:143
  87.2 3.0 %attend.2.refs_0_ = bf16[256,512]{1,0:T(8,128)(2,1)S(1)} custom-call(s32[4,8]{1,0:T(4,128)S(1)} %bitcast.103, f32[512,512]{1,0:T(8,128)S(1)} %copy-done, f32[512,128]{1,0:T(8,128)S(1)} %get-tuple-element.27.cos_ref, f32[512,128]{1,0:T(8,128)S(1)} %get-tuple-element.28.sin_ref, bf16[8,2,256,128]{3,2,1,0:T(8,128)(2,1)S(1)} %all-to-all-done.kv_ref), custom_call_target="tpu_custom_call" | custom-call | flops 536870912 | bytes 1835008 | tf_op jit(solution)/shard_map/attend/pallas_call | solution.py:143
  90.2 2.1 %collective-permute-start.20 = (bf16[256,512]{1,0:T(8,128)(2,1)S(1)}, bf16[256,512]{1,0:T(8,128)(2,1)S(1)}, u32[]{:S(2)}, u32[]{:S(2)}) collective-permute-start(bf16[256,512]{1,0:T(8,128)(2,1)S(1)} %attend.2.refs_0_), channel_id=1, source_target_pairs={{0,1},{1,2},{2,3},{3,4},{4,5},{5,6},{6,7},{7,0},{8,9},{9,10},{10,1... | collective-permute-start | bytes 786440 | tf_op jit(solution)/shard_map/ppermute | solution.py:367
  92.3 0.6 collective-permute-start.25
  92.9 2.6 %collective-permute-start.14 = (bf16[256,512]{1,0:T(8,128)(2,1)S(1)}, bf16[256,512]{1,0:T(8,128)(2,1)S(1)}, u32[]{:S(2)}, u32[]{:S(2)}) collective-permute-start(bf16[256,512]{1,0:T(8,128)(2,1)S(1)} %attend.2.refs_0_), channel_id=1, source_target_pairs={{0,7},{1,0},{2,1},{3,2},{4,3},{5,4},{6,5},{7,6},{8,15},{9,8},{10,9... | collective-permute-start | bytes 786440 | tf_op jit(solution)/shard_map/ppermute | solution.py:368
  95.5 0.8 collective-permute-done.17.refs_5_
  96.3 0.6 collective-permute-start.18
  97.0 3.7 %collective-permute-done.20.refs_2_ = bf16[256,512]{1,0:T(8,128)(2,1)S(1)} collective-permute-done((bf16[256,512]{1,0:T(8,128)(2,1)S(1)}, bf16[256,512]{1,0:T(8,128)(2,1)S(1)}, u32[]{:S(2)}, u32[]{:S(2)}) %collective-permute-start.20) | collective-permute-done | bytes 262176 | tf_op jit(solution)/shard_map/ppermute | solution.py:367
  100.7 0.8 collective-permute-start.21
  101.5 4.8 %collective-permute-done.25.refs_3_ = bf16[256,512]{1,0:T(8,128)(2,1)S(1)} collective-permute-done((bf16[256,512]{1,0:T(8,128)(2,1)S(1)}, bf16[256,512]{1,0:T(8,128)(2,1)S(1)}, u32[]{:S(2)}, u32[]{:S(2)}) %collective-permute-start.25) | collective-permute-done | bytes 262176 | tf_op jit(solution)/shard_map/ppermute | solution.py:367
  106.3 0.8 collective-permute-start.26
  107.3 2.4 %collective-permute-start.15 = (bf16[256,512]{1,0:T(8,128)(2,1)S(1)}, bf16[256,512]{1,0:T(8,128)(2,1)S(1)}, u32[]{:S(2)}, u32[]{:S(2)}) collective-permute-start(bf16[256,512]{1,0:T(8,128)(2,1)S(1)} %collective-permute-done.14.refs_4_), channel_id=1, source_target_pairs={{0,7},{1,0},{2,1},{3,2},{4,3},{5,4},{6,5},{7,6},{8,15},{9,8},{10,9... | collective-permute-start | bytes 786440 | tf_op jit(solution)/shard_map/ppermute | solution.py:368
  109.8 2.1 %collective-permute-done.21.refs_6_ = bf16[256,512]{1,0:T(8,128)(2,1)S(1)} collective-permute-done((bf16[256,512]{1,0:T(8,128)(2,1)S(1)}, bf16[256,512]{1,0:T(8,128)(2,1)S(1)}, u32[]{:S(2)}, u32[]{:S(2)}) %collective-permute-start.21) | collective-permute-done | bytes 262176 | tf_op jit(solution)/shard_map/ppermute | solution.py:367
  111.9 0.8 collective-permute-start.22
  112.7 4.8 %collective-permute-done.26.refs_7_ = bf16[256,512]{1,0:T(8,128)(2,1)S(1)} collective-permute-done((bf16[256,512]{1,0:T(8,128)(2,1)S(1)}, bf16[256,512]{1,0:T(8,128)(2,1)S(1)}, u32[]{:S(2)}, u32[]{:S(2)}) %collective-permute-start.26) | collective-permute-done | bytes 262176 | tf_op jit(solution)/shard_map/ppermute | solution.py:367
  117.5 0.8 collective-permute-start.27
  118.9 2.5 %collective-permute-start.16 = (bf16[256,512]{1,0:T(8,128)(2,1)S(1)}, bf16[256,512]{1,0:T(8,128)(2,1)}, u32[]{:S(2)}, u32[]{:S(2)}) collective-permute-start(bf16[256,512]{1,0:T(8,128)(2,1)S(1)} %collective-permute-done.15.refs_8_), channel_id=1, source_target_pairs={{0,7},{1,0},{2,1},{3,2},{4,3},{5,4},{6,5},{7,6},{8,15},{9,8},{10,9... | collective-permute-start | bytes 786440 | tf_op jit(solution)/shard_map/ppermute | solution.py:368
  121.4 1.7 %collective-permute-done.22.refs_10_ = bf16[256,512]{1,0:T(8,128)(2,1)S(1)} collective-permute-done((bf16[256,512]{1,0:T(8,128)(2,1)S(1)}, bf16[256,512]{1,0:T(8,128)(2,1)S(1)}, u32[]{:S(2)}, u32[]{:S(2)}) %collective-permute-start.22) | collective-permute-done | bytes 262176 | tf_op jit(solution)/shard_map/ppermute | solution.py:367
  123.1 0.8 collective-permute-start.23
  124.0 2.4 %collective-permute-start.24 = (bf16[256,512]{1,0:T(8,128)(2,1)S(1)}, bf16[256,512]{1,0:T(8,128)(2,1)S(1)}, u32[]{:S(2)}, u32[]{:S(2)}) collective-permute-start(bf16[256,512]{1,0:T(8,128)(2,1)S(1)} %collective-permute-done.19.refs_1_), channel_id=1, source_target_pairs={{0,7},{1,0},{2,1},{3,2},{4,3},{5,4},{6,5},{7,6},{8,15},{9,8},{10,9... | collective-permute-start | bytes 786440 | tf_op jit(solution)/shard_map/ppermute | solution.py:370
  126.4 2.4 %collective-permute-done.27.refs_11_ = bf16[256,512]{1,0:T(8,128)(2,1)S(1)} collective-permute-done((bf16[256,512]{1,0:T(8,128)(2,1)S(1)}, bf16[256,512]{1,0:T(8,128)(2,1)S(1)}, u32[]{:S(2)}, u32[]{:S(2)}) %collective-permute-start.27) | collective-permute-done | bytes 262176 | tf_op jit(solution)/shard_map/ppermute | solution.py:367
  128.7 6.6 %output.2.refs_6_ = f32[512,1024]{1,0:T(8,128)S(1)} custom-call(s32[6,4]{1,0:T(8,128)S(1)} %stack.419.index_ref, bf16[256,512]{1,0:T(8,128)(2,1)S(1)} %attend.2.refs_0_, bf16[256,512]{1,0:T(8,128)(2,1)S(1)} %attend.3.refs_1_, bf16[256,512]{1,0:T(8,128)(2,1)S(1)} %collective-permute-done.20.refs_2_, bf16[256,512]{1,0:T(8,128)(2,1)S(1)} %collective-permute-done.25.refs_3_, ...), custom_call_target="tpu_custom_call" | custom-call | flops 3221225472 | bytes 13631488 | tf_op jit(solution)/shard_map/output/pallas_call | solution.py:197
  135.4 5.1 %output.3 = bf16[512,1024]{1,0:T(8,128)(2,1)} custom-call(s32[2,4]{1,0:T(2,128)S(1)} %pad_add_fusion.2.index_ref, bf16[256,512]{1,0:T(8,128)(2,1)} %collective-permute-done.16.refs_0_, bf16[256,512]{1,0:T(8,128)(2,1)S(1)} %collective-permute-done.19.refs_1_, bf16[256,512]{1,0:T(8,128)(2,1)S(1)} %collective-permute-done.23.refs_2_, ...), custom_call_target="tpu_custom_call" | custom-call | flops 1073741824 | bytes 7340032 | tf_op jit(solution)/shard_map/output/pallas_call | solution.py:197
  (62 shorter events, 4.5 us)
Async XLA Ops:
  6.5 116.6 %all-gather.3.cloned.1.call-start = ((), (), s32[]{:S(2)}) async-start(), calls=%async_computation.1 | async-start | bytes 8650752 | tf_op jit(solution)/shard_map/all_gather | solution.py:352
  6.5 11.5 %collective-permute-start = (bf16[256,512]{1,0:T(8,128)(2,1)}, bf16[256,512]{1,0:T(8,128)(2,1)S(1)}, u32[]{:S(2)}, u32[]{:S(2)}) collective-permute-start(bf16[256,512]{1,0:T(8,128)(2,1)} %refs_0_.4), channel_id=1, source_target_pairs={{0,16},{8,72},{16,32},{24,88},{32,48},{40,104},{48,0},{56,120},{64... | collective-permute-start | bytes 786440 | tf_op jit(solution)/shard_map/ppermute | solution.py:303
  8.8 10.6 %collective-permute-start.1 = (bf16[256,512]{1,0:T(8,128)(2,1)}, bf16[256,512]{1,0:T(8,128)(2,1)S(1)}, u32[]{:S(2)}, u32[]{:S(2)}) collective-permute-start(bf16[256,512]{1,0:T(8,128)(2,1)} %refs_0_.4), channel_id=1, source_target_pairs={{0,48},{8,200},{16,0},{24,216},{32,16},{40,232},{48,32},{56,248},{... | collective-permute-start | bytes 786440 | tf_op jit(solution)/shard_map/ppermute | solution.py:304
  8.8 9.3 %collective-permute-start.2 = (bf16[256,512]{1,0:T(8,128)(2,1)}, bf16[256,512]{1,0:T(8,128)(2,1)S(1)}, u32[]{:S(2)}, u32[]{:S(2)}) collective-permute-start(bf16[256,512]{1,0:T(8,128)(2,1)} %refs_0_.4), channel_id=1, source_target_pairs={{0,32},{8,136},{16,48},{24,152},{32,0},{40,168},{48,16},{56,184},{... | collective-permute-start | bytes 786440 | tf_op jit(solution)/shard_map/ppermute | solution.py:305
  10.2 7.8 %collective-permute-start.3 = (bf16[512,256]{1,0:T(8,128)(2,1)}, bf16[512,256]{1,0:T(8,128)(2,1)S(1)}, u32[]{:S(2)}, u32[]{:S(2)}) collective-permute-start(bf16[512,256]{1,0:T(8,128)(2,1)} %param.8), channel_id=1, source_target_pairs={{0,0},{1,49},{2,66},{3,115},{4,132},{5,181},{6,198},{7,247},{8,8},... | collective-permute-start | bytes 786440 | tf_op jit(solution)/shard_map/ppermute | solution.py:348
  11.8 1.0 copy-start.3
  12.9 1.0 copy-start.4
  19.4 1.0 copy-start.5
  20.4 11.2 %collective-permute-start.6 = (bf16[1024,512]{1,0:T(8,128)(2,1)S(1)}, bf16[1024,512]{1,0:T(8,128)(2,1)}, u32[]{:S(2)}, u32[]{:S(2)}) collective-permute-start(bf16[1024,512]{1,0:T(8,128)(2,1)S(1)} %side_by_side.1.refs_2_), channel_id=1, source_target_pairs={{0,8},{8,0},{16,24},{24,16},{32,40},{40,32},{48,56},{56,48},{64,72... | collective-permute-start | bytes 3145736 | tf_op jit(solution)/shard_map/ppermute | solution.py:38
  20.5 21.0 %collective-permute-start.4 = (bf16[1024,512]{1,0:T(8,128)(2,1)S(1)}, bf16[1024,512]{1,0:T(8,128)(2,1)S(1)}, u32[]{:S(2)}, u32[]{:S(2)}) collective-permute-start(bf16[1024,512]{1,0:T(8,128)(2,1)S(1)} %side_by_side.1.refs_2_), channel_id=1, source_target_pairs={{0,64},{8,24},{16,80},{24,40},{32,96},{40,56},{48,112},{56,8},{64,... | collective-permute-start | bytes 3145736 | tf_op jit(solution)/shard_map/ppermute | solution.py:311
  20.6 20.9 %collective-permute-start.5 = (bf16[1024,512]{1,0:T(8,128)(2,1)S(1)}, bf16[1024,512]{1,0:T(8,128)(2,1)}, u32[]{:S(2)}, u32[]{:S(2)}) collective-permute-start(bf16[1024,512]{1,0:T(8,128)(2,1)S(1)} %side_by_side.1.refs_2_), channel_id=1, source_target_pairs={{0,192},{8,56},{16,208},{24,8},{32,224},{40,24},{48,240},{56,40},{... | collective-permute-start | bytes 3145736 | tf_op jit(solution)/shard_map/ppermute | solution.py:312
  23.8 17.7 %collective-permute-start.13 = (bf16[512,256]{1,0:T(8,128)(2,1)S(1)}, bf16[512,256]{1,0:T(8,128)(2,1)S(1)}, u32[]{:S(2)}, u32[]{:S(2)}) collective-permute-start(bf16[512,256]{1,0:T(8,128)(2,1)S(1)} %collective-permute-done.3), channel_id=1, source_target_pairs={{0,0},{49,48},{66,64},{115,112},{132,128},{181,176},{198,192},{247... | collective-permute-start | bytes 786440 | tf_op jit(solution)/shard_map/ppermute | solution.py:308
  36.1 1.0 copy-start.1
  41.5 0.7 copy-start.9
  42.2 16.1 %collective-permute-start.9 = (bf16[1024,512]{1,0:T(8,128)(2,1)S(1)}, bf16[1024,512]{1,0:T(8,128)(2,1)}, u32[]{:S(2)}, u32[]{:S(2)}) collective-permute-start(bf16[1024,512]{1,0:T(8,128)(2,1)S(1)} %collective-permute-done.4.refs_4_), channel_id=1, source_target_pairs={{0,8},{8,0},{16,24},{24,16},{32,40},{40,32},{48,56},{56,48},{64,72... | collective-permute-start | bytes 3145736 | tf_op jit(solution)/shard_map/ppermute | solution.py:38
  42.3 16.1 %collective-permute-start.10 = (bf16[1024,512]{1,0:T(8,128)(2,1)}, bf16[1024,512]{1,0:T(8,128)(2,1)}, u32[]{:S(2)}, u32[]{:S(2)}) collective-permute-start(bf16[1024,512]{1,0:T(8,128)(2,1)} %collective-permute-done.5.refs_5_), channel_id=1, source_target_pairs={{0,8},{8,0},{16,24},{24,16},{32,40},{40,32},{48,56},{56,48},{64,72... | collective-permute-start | bytes 3145736 | tf_op jit(solution)/shard_map/ppermute | solution.py:38
  42.8 40.0 %all-to-all-start = ((bf16[8,2,256,128]{3,2,1,0:T(8,128)(2,1)}), bf16[8,2,256,128]{3,2,1,0:T(8,128)(2,1)S(1)}, u32[]{:S(2)}, u32[]{:S(2)}) async-start(bf16[8,2,256,128]{3,2,1,0:T(8,128)(2,1)} %split_heads.1), calls=%async_computation | async-start | bytes 2097152 | tf_op jit(solution)/shard_map/all_to_all | solution.py:309
  54.9 13.3 %collective-permute-start.7 = (bf16[512,512]{1,0:T(8,128)(2,1)S(1)}, bf16[512,512]{1,0:T(8,128)(2,1)S(1)}, u32[]{:S(2)}, u32[]{:S(2)}) collective-permute-start(bf16[512,512]{1,0:T(8,128)(2,1)S(1)} %slice.8), channel_id=1, source_target_pairs={{0,64},{8,24},{16,80},{24,40},{32,96},{40,56},{48,112},{56,8},{64,... | collective-permute-start | bytes 1572872 | tf_op jit(solution)/shard_map/ppermute | solution.py:315
  55.0 13.5 %collective-permute-start.8 = (bf16[512,512]{1,0:T(8,128)(2,1)S(1)}, bf16[512,512]{1,0:T(8,128)(2,1)}, u32[]{:S(2)}, u32[]{:S(2)}) collective-permute-start(bf16[512,512]{1,0:T(8,128)(2,1)S(1)} %slice.9), channel_id=1, source_target_pairs={{0,192},{8,56},{16,208},{24,8},{32,224},{40,24},{48,240},{56,40},{... | collective-permute-start | bytes 1572872 | tf_op jit(solution)/shard_map/ppermute | solution.py:316
  65.1 1.0 copy-start.2
  68.2 3.3 %copy-start.7 = (bf16[512,512]{1,0:T(8,128)(2,1)}, bf16[512,512]{1,0:T(8,128)(2,1)S(1)}, u32[]{:S(2)}) copy-start(bf16[512,512]{1,0:T(8,128)(2,1)S(1)} %collective-permute-done.7.refs_4_) | copy-start | bytes 1572868
  68.5 2.6 %collective-permute-start.11 = (bf16[512,512]{1,0:T(8,128)(2,1)S(1)}, bf16[512,512]{1,0:T(8,128)(2,1)S(1)}, u32[]{:S(2)}, u32[]{:S(2)}) collective-permute-start(bf16[512,512]{1,0:T(8,128)(2,1)S(1)} %collective-permute-done.7.refs_4_), channel_id=1, source_target_pairs={{0,8},{8,0},{16,24},{24,16},{32,40},{40,32},{48,56},{56,48},{64,72... | collective-permute-start | bytes 1572872 | tf_op jit(solution)/shard_map/ppermute | solution.py:38
  68.5 3.0 %collective-permute-start.12 = (bf16[512,512]{1,0:T(8,128)(2,1)}, bf16[512,512]{1,0:T(8,128)(2,1)}, u32[]{:S(2)}, u32[]{:S(2)}) collective-permute-start(bf16[512,512]{1,0:T(8,128)(2,1)} %collective-permute-done.8.refs_5_), channel_id=1, source_target_pairs={{0,8},{8,0},{16,24},{24,16},{32,40},{40,32},{48,56},{56,48},{64,72... | collective-permute-start | bytes 1572872 | tf_op jit(solution)/shard_map/ppermute | solution.py:38
  69.7 13.1 %copy-start.6 = (s32[1,4,8]{2,1,0:T(4,128)S(1)}, s32[1,4,8]{2,1,0:T(4,128)}, u32[]{:S(2)}) copy-start(s32[1,4,8]{2,1,0:T(4,128)} %param.11) | copy-start | bytes 388
  71.1 0.8 copy-start.8
  82.8 1.2 copy-start
  87.1 9.2 %collective-permute-start.17 = (bf16[256,512]{1,0:T(8,128)(2,1)S(1)}, bf16[256,512]{1,0:T(8,128)(2,1)S(1)}, u32[]{:S(2)}, u32[]{:S(2)}) collective-permute-start(bf16[256,512]{1,0:T(8,128)(2,1)S(1)} %attend.3.refs_1_), channel_id=1, source_target_pairs={{0,7},{1,0},{2,1},{3,2},{4,3},{5,4},{6,5},{7,6},{8,15},{9,8},{10,9... | collective-permute-start | bytes 786440 | tf_op jit(solution)/shard_map/ppermute | solution.py:368
  90.2 10.4 %collective-permute-start.20 = (bf16[256,512]{1,0:T(8,128)(2,1)S(1)}, bf16[256,512]{1,0:T(8,128)(2,1)S(1)}, u32[]{:S(2)}, u32[]{:S(2)}) collective-permute-start(bf16[256,512]{1,0:T(8,128)(2,1)S(1)} %attend.2.refs_0_), channel_id=1, source_target_pairs={{0,1},{1,2},{2,3},{3,4},{4,5},{5,6},{6,7},{7,0},{8,9},{9,10},{10,1... | collective-permute-start | bytes 786440 | tf_op jit(solution)/shard_map/ppermute | solution.py:367
  92.3 14.0 %collective-permute-start.25 = (bf16[256,512]{1,0:T(8,128)(2,1)S(1)}, bf16[256,512]{1,0:T(8,128)(2,1)S(1)}, u32[]{:S(2)}, u32[]{:S(2)}) collective-permute-start(bf16[256,512]{1,0:T(8,128)(2,1)S(1)} %attend.3.refs_1_), channel_id=1, source_target_pairs={{0,1},{1,2},{2,3},{3,4},{4,5},{5,6},{6,7},{7,0},{8,9},{9,10},{10,1... | collective-permute-start | bytes 786440 | tf_op jit(solution)/shard_map/ppermute | solution.py:367
  92.9 14.4 %collective-permute-start.14 = (bf16[256,512]{1,0:T(8,128)(2,1)S(1)}, bf16[256,512]{1,0:T(8,128)(2,1)S(1)}, u32[]{:S(2)}, u32[]{:S(2)}) collective-permute-start(bf16[256,512]{1,0:T(8,128)(2,1)S(1)} %attend.2.refs_0_), channel_id=1, source_target_pairs={{0,7},{1,0},{2,1},{3,2},{4,3},{5,4},{6,5},{7,6},{8,15},{9,8},{10,9... | collective-permute-start | bytes 786440 | tf_op jit(solution)/shard_map/ppermute | solution.py:368
  96.3 13.4 %collective-permute-start.18 = (bf16[256,512]{1,0:T(8,128)(2,1)S(1)}, bf16[256,512]{1,0:T(8,128)(2,1)S(1)}, u32[]{:S(2)}, u32[]{:S(2)}) collective-permute-start(bf16[256,512]{1,0:T(8,128)(2,1)S(1)} %collective-permute-done.17.refs_5_), channel_id=1, source_target_pairs={{0,7},{1,0},{2,1},{3,2},{4,3},{5,4},{6,5},{7,6},{8,15},{9,8},{10,9... | collective-permute-start | bytes 786440 | tf_op jit(solution)/shard_map/ppermute | solution.py:368
  100.7 11.2 %collective-permute-start.21 = (bf16[256,512]{1,0:T(8,128)(2,1)S(1)}, bf16[256,512]{1,0:T(8,128)(2,1)S(1)}, u32[]{:S(2)}, u32[]{:S(2)}) collective-permute-start(bf16[256,512]{1,0:T(8,128)(2,1)S(1)} %collective-permute-done.20.refs_2_), channel_id=1, source_target_pairs={{0,1},{1,2},{2,3},{3,4},{4,5},{5,6},{6,7},{7,0},{8,9},{9,10},{10,1... | collective-permute-start | bytes 786440 | tf_op jit(solution)/shard_map/ppermute | solution.py:367
  106.3 11.2 %collective-permute-start.26 = (bf16[256,512]{1,0:T(8,128)(2,1)S(1)}, bf16[256,512]{1,0:T(8,128)(2,1)S(1)}, u32[]{:S(2)}, u32[]{:S(2)}) collective-permute-start(bf16[256,512]{1,0:T(8,128)(2,1)S(1)} %collective-permute-done.25.refs_3_), channel_id=1, source_target_pairs={{0,1},{1,2},{2,3},{3,4},{4,5},{5,6},{6,7},{7,0},{8,9},{9,10},{10,1... | collective-permute-start | bytes 786440 | tf_op jit(solution)/shard_map/ppermute | solution.py:367
  107.3 11.7 %collective-permute-start.15 = (bf16[256,512]{1,0:T(8,128)(2,1)S(1)}, bf16[256,512]{1,0:T(8,128)(2,1)S(1)}, u32[]{:S(2)}, u32[]{:S(2)}) collective-permute-start(bf16[256,512]{1,0:T(8,128)(2,1)S(1)} %collective-permute-done.14.refs_4_), channel_id=1, source_target_pairs={{0,7},{1,0},{2,1},{3,2},{4,3},{5,4},{6,5},{7,6},{8,15},{9,8},{10,9... | collective-permute-start | bytes 786440 | tf_op jit(solution)/shard_map/ppermute | solution.py:368
  109.7 11.7 %collective-permute-start.19 = (bf16[256,512]{1,0:T(8,128)(2,1)S(1)}, bf16[256,512]{1,0:T(8,128)(2,1)S(1)}, u32[]{:S(2)}, u32[]{:S(2)}) collective-permute-start(bf16[256,512]{1,0:T(8,128)(2,1)S(1)} %collective-permute-done.18.refs_9_), channel_id=1, source_target_pairs={{0,7},{1,0},{2,1},{3,2},{4,3},{5,4},{6,5},{7,6},{8,15},{9,8},{10,9... | collective-permute-start | bytes 786440 | tf_op jit(solution)/shard_map/ppermute | solution.py:368
  111.9 11.2 %collective-permute-start.22 = (bf16[256,512]{1,0:T(8,128)(2,1)S(1)}, bf16[256,512]{1,0:T(8,128)(2,1)S(1)}, u32[]{:S(2)}, u32[]{:S(2)}) collective-permute-start(bf16[256,512]{1,0:T(8,128)(2,1)S(1)} %collective-permute-done.21.refs_6_), channel_id=1, source_target_pairs={{0,1},{1,2},{2,3},{3,4},{4,5},{5,6},{6,7},{7,0},{8,9},{9,10},{10,1... | collective-permute-start | bytes 786440 | tf_op jit(solution)/shard_map/ppermute | solution.py:367
  117.5 11.2 %collective-permute-start.27 = (bf16[256,512]{1,0:T(8,128)(2,1)S(1)}, bf16[256,512]{1,0:T(8,128)(2,1)S(1)}, u32[]{:S(2)}, u32[]{:S(2)}) collective-permute-start(bf16[256,512]{1,0:T(8,128)(2,1)S(1)} %collective-permute-done.26.refs_7_), channel_id=1, source_target_pairs={{0,1},{1,2},{2,3},{3,4},{4,5},{5,6},{6,7},{7,0},{8,9},{9,10},{10,1... | collective-permute-start | bytes 786440 | tf_op jit(solution)/shard_map/ppermute | solution.py:367
  118.9 16.4 %collective-permute-start.16 = (bf16[256,512]{1,0:T(8,128)(2,1)S(1)}, bf16[256,512]{1,0:T(8,128)(2,1)}, u32[]{:S(2)}, u32[]{:S(2)}) collective-permute-start(bf16[256,512]{1,0:T(8,128)(2,1)S(1)} %collective-permute-done.15.refs_8_), channel_id=1, source_target_pairs={{0,7},{1,0},{2,1},{3,2},{4,3},{5,4},{6,5},{7,6},{8,15},{9,8},{10,9... | collective-permute-start | bytes 786440 | tf_op jit(solution)/shard_map/ppermute | solution.py:368
  123.1 12.2 %collective-permute-start.23 = (bf16[256,512]{1,0:T(8,128)(2,1)S(1)}, bf16[256,512]{1,0:T(8,128)(2,1)S(1)}, u32[]{:S(2)}, u32[]{:S(2)}) collective-permute-start(bf16[256,512]{1,0:T(8,128)(2,1)S(1)} %collective-permute-done.22.refs_10_), channel_id=1, source_target_pairs={{0,1},{1,2},{2,3},{3,4},{4,5},{5,6},{6,7},{7,0},{8,9},{9,10},{10,1... | collective-permute-start | bytes 786440 | tf_op jit(solution)/shard_map/ppermute | solution.py:370
  124.0 11.4 %collective-permute-start.24 = (bf16[256,512]{1,0:T(8,128)(2,1)S(1)}, bf16[256,512]{1,0:T(8,128)(2,1)S(1)}, u32[]{:S(2)}, u32[]{:S(2)}) collective-permute-start(bf16[256,512]{1,0:T(8,128)(2,1)S(1)} %collective-permute-done.19.refs_1_), channel_id=1, source_target_pairs={{0,7},{1,0},{2,1},{3,2},{4,3},{5,4},{6,5},{7,6},{8,15},{9,8},{10,9... | collective-permute-start | bytes 786440 | tf_op jit(solution)/shard_map/ppermute | solution.py:370
Sparse Core Ops, SparseCore 0:
  42.4 62.1 all-gather.2
